TPU v7x, 32 devices: a whole 2x2x4 slice. The times are simulated.
32 devices in a mesh: group: 2 (over x), dp: 2 (over core), expert: 8 (over z, y).
Axes of the slice: x: 2, y: 2, z: 4, core: 2. Of those that a mesh axis runs over, the one named last changes fastest.
Arguments:
- layer_input: bfloat16 [2, 128, 4096], P(None, ('group', 'dp', 'expert')), parts along dimension 1, may hold values from -6 to 6
- prompt_ssm: float32 [8, 16, 4096], P(('group', 'dp'), None, 'expert'), parts along dimension 0, may hold values from -4 to 4
- prompt_conv: float32 [8, 3, 4096], P(('group', 'dp'), None, 'expert'), parts along dimension 0, may hold values from -6 to 6
- sample_prompt: int32 [128], P(('group', 'dp')), parts along dimension 0, may hold values from 0 to 3, as said below
- mamba_gain: float32 [4096], replicated, may hold values from 0.25 to 1.75
- in_proj: bfloat16 [2, 4096, 4096], P(None, None, 'expert'), may hold values from -0.09375 to 0.09375
- conv_weight: float32 [4, 4096], P(None, 'expert'), may hold values from -3 to 3
- conv_bias: float32 [4096], P('expert'), may hold values from -3 to 3
- x_proj: bfloat16 [288, 4096], P(None, 'expert'), may hold values from -0.09375 to 0.09375
- dt_proj: bfloat16 [256, 4096], P(None, 'expert'), may hold values from -0.375 to 0.375
- dt_bias: float32 [4096], P('expert'), may hold values from -4 to -1
- a_log: float32 [16, 4096], P(None, 'expert'), may hold values from -3 to 2
- d_skip: float32 [4096], P('expert'), may hold values from 0.5 to 1.5
- out_proj: bfloat16 [4096, 4096], P('expert'), may hold values from -0.09375 to 0.09375
- moe_gain: float32 [4096], replicated, may hold values from 0.1 to 1.9
- route_ids: int32 [2, 128, 2], P(None, ('group', 'dp', 'expert')), parts along dimension 1, may hold values from 0 to 15, as said below
- route_weights: float32 [2, 128, 2], P(None, ('group', 'dp', 'expert')), parts along dimension 1, may hold values from 0.2 to 0.9
- w_gate: bfloat16 [2, 7168, 4096], P('dp', 'expert'), may hold values from -0.09375 to 0.09375
- w_up: bfloat16 [2, 7168, 4096], P('dp', 'expert'), may hold values from -0.09375 to 0.09375
- w_down: bfloat16 [2, 7168, 4096], P('dp', 'expert'), may hold values from -0.0625 to 0.0625
Outputs:
- layer_output: bfloat16 [2, 128, 4096], P(None, ('group', 'dp', 'expert')), parts along dimension 1
- ssm_state: float32 [128, 16, 4096], P(('group', 'dp'), None, 'expert'), parts along dimension 0
- conv_state: float32 [128, 3, 4096], P(('group', 'dp'), None, 'expert'), parts along dimension 0
There are 2 independent parts, one for each index of `group`. A program takes and returns all parts, laid end to end along the dimension named above; an argument that names none is the same for every part. Nothing has to cross between parts.
Inputs may be any that keep to these rules, and one draw needn't show every extreme that they name: `sample_prompt`: each prompt is the prompt of exactly 16 rows. `route_ids`: each row names 2 different experts; in each step and each aligned block of 4 rows (the rows of one device) at most 2 rows name a given expert below 2, and in every step some expert below 2 is named by exactly 2 rows in every block.
All inputs are finite; a program needn't handle non-finite values.
Results may differ from a plain program's by a relative error of at most 0.014.
Values may be sent and summed in bfloat16 or wider, within the bound.
No kernel may reach another device: no remote copies, remote signals or barrier semaphores. Data moves between devices by JAX's collectives and lax.ppermute only.
A program may use at most 128 MiB of HBM per device.

v0:
```python
import jax
import jax.numpy as jnp
from jax import lax
from jax.sharding import PartitionSpec as P

CAP = 2


def normalize(values, gain):
    return values * lax.rsqrt(jnp.mean(values * values, axis=-1, keepdims=True) + 1e-05) * gain


def expert_hidden(rows_in, gate_rows, up_rows):
    dims = (((1,), (1,)), ((), ()))
    gate_val = lax.dot_general(rows_in, gate_rows, dims, preferred_element_type=jnp.float32)
    up_val = lax.dot_general(rows_in, up_rows, dims, preferred_element_type=jnp.float32)
    return (jax.nn.silu(gate_val) * up_val).astype(jnp.bfloat16)


def route_tables(identity_rows, weight_rows, experts, capacity):
    which = jnp.arange(experts)
    named = identity_rows[:, :, None] == which[None, None, :]
    chosen = jnp.any(named, axis=1)
    shares = jnp.sum(jnp.where(named, weight_rows[:, :, None], 0.0), axis=1)
    slot_of = jnp.cumsum(chosen.astype(jnp.int32), axis=0) - 1
    placing = chosen[None] & (slot_of[None] == jnp.arange(capacity)[:, None, None])
    placing = jnp.transpose(placing, (2, 0, 1)).astype(jnp.float32)
    return (placing, shares)


def fill_buffer(placing, routed):
    return jnp.einsum(
        "ksr,rd->ksd", placing.astype(jnp.bfloat16), routed, preferred_element_type=jnp.float32
    ).astype(jnp.bfloat16)


def combine_back(placing, shares, returned):
    weighted = placing * jnp.transpose(shares)[:, None, :]
    return jnp.einsum(
        "ksr,ksd->rd", weighted, returned.astype(jnp.float32), precision=lax.Precision.HIGHEST
    )


def on_device(
    layer_input,
    prompt_ssm,
    prompt_conv,
    sample_prompt,
    mamba_gain,
    in_proj,
    conv_weight,
    conv_bias,
    x_proj,
    dt_proj,
    dt_bias,
    a_log,
    d_skip,
    out_proj,
    moe_gain,
    route_ids,
    route_weights,
    w_gate,
    w_up,
    w_down,
):
    all_ssm, all_conv = (
        lax.all_gather(prompt_ssm, "dp", axis=0, tiled=True),
        lax.all_gather(prompt_conv, "dp", axis=0, tiled=True),
    )
    ssm_state = jnp.take(all_ssm, sample_prompt, axis=0)
    conv_state = jnp.take(all_conv, sample_prompt, axis=0)
    decay_rate = -jnp.exp(a_log)
    experts = lax.axis_size("dp")
    width = layer_input.shape[2]
    steps = layer_input.shape[0]
    rank_width = dt_proj.shape[0]
    states = a_log.shape[0]
    dt_float = dt_proj.astype(jnp.float32)
    outputs = []
    for step_index in range(steps):
        inputs = layer_input[step_index].astype(jnp.float32)
        if step_index > 0:
            inputs = outputs[-1].astype(jnp.float32) + inputs
        normed = normalize(inputs, mamba_gain).astype(jnp.bfloat16)
        both = jnp.einsum(
            "rd,kdc->rkc",
            lax.all_gather(normed, "expert", axis=0, tiled=True),
            in_proj,
            preferred_element_type=jnp.float32,
        )
        x_part = both[:, 0, :]
        z_part = both[:, 1, :]
        window = jnp.concatenate([conv_state, x_part[:, None, :]], axis=1)
        conv_act = jax.nn.silu(jnp.sum(window * conv_weight[None], axis=1) + conv_bias).astype(
            jnp.bfloat16
        )
        conv_next = window[:, 1:, :]
        mixer_partial_value = lax.dot_general(
            conv_act, x_proj, (((1,), (1,)), ((), ())), preferred_element_type=jnp.float32
        )
        projected = lax.psum(mixer_partial_value, "expert")
        step_size = jax.nn.softplus(
            jnp.dot(projected[:, :rank_width], dt_float, precision=lax.Precision.HIGHEST) + dt_bias
        )
        input_map = projected[:, rank_width : rank_width + states]
        output_map = projected[:, rank_width + states :]
        act_float = conv_act.astype(jnp.float32)
        ssm_next = (
            jnp.exp(step_size[:, None, :] * decay_rate[None]) * ssm_state
            + step_size[:, None, :] * input_map[:, :, None] * act_float[:, None, :]
        )
        gated = (
            (jnp.sum(ssm_next * output_map[:, :, None], axis=1) + d_skip * act_float)
            * jax.nn.silu(z_part)
        ).astype(jnp.bfloat16)
        mixed = lax.psum_scatter(
            jnp.dot(gated, out_proj, preferred_element_type=jnp.float32).astype(jnp.bfloat16),
            "expert",
            scatter_dimension=0,
            tiled=True,
        ).astype(jnp.float32)
        residual = inputs + mixed
        ssm_state = ssm_next
        conv_state = conv_next
        routed = normalize(residual, moe_gain).astype(jnp.bfloat16)
        placing, shares = route_tables(
            route_ids[step_index], route_weights[step_index], experts, CAP
        )
        buffer = fill_buffer(placing, routed)
        slots = buffer.shape[1]
        owner = lax.axis_index("dp")
        picked = lax.dynamic_index_in_dim(
            lax.all_gather(buffer[None], ("dp", "expert"), axis=0, tiled=True),
            owner,
            1,
            keepdims=False,
        )
        hidden = expert_hidden(picked.reshape(-1, width), w_gate[0], w_up[0])
        sources = hidden.shape[0] // slots
        mine = (jnp.arange(experts) == owner)[None, :, None, None]
        spread_out = jnp.where(
            mine, hidden.reshape(sources, 1, slots, -1), jnp.zeros((), jnp.bfloat16)
        ).reshape(sources * experts * slots, -1)
        partial_value = lax.psum_scatter(
            jnp.dot(spread_out, w_down[0], preferred_element_type=jnp.float32),
            ("dp", "expert"),
            scatter_dimension=0,
            tiled=True,
        )
        returned = partial_value.astype(jnp.bfloat16).reshape(experts, slots, width)
        outputs.append((residual + combine_back(placing, shares, returned)).astype(jnp.bfloat16))
    return (jnp.stack(outputs), ssm_state, conv_state)


def solution(mesh):
    in_specs = (
        P(None, ("group", "dp", "expert"), None),
        P(("group", "dp"), None, "expert"),
        P(("group", "dp"), None, "expert"),
        P(("group", "dp")),
        P(),
        P(None, None, "expert"),
        P(None, "expert"),
        P("expert"),
        P(None, "expert"),
        P(None, "expert"),
        P("expert"),
        P(None, "expert"),
        P("expert"),
        P("expert", None),
        P(),
        P(None, ("group", "dp", "expert"), None),
        P(None, ("group", "dp", "expert"), None),
        P("dp", "expert", None),
        P("dp", "expert", None),
        P("dp", "expert", None),
    )
    out_specs = (
        P(None, ("group", "dp", "expert"), None),
        P(("group", "dp"), None, "expert"),
        P(("group", "dp"), None, "expert"),
    )
    return jax.shard_map(
        on_device, mesh=mesh, in_specs=in_specs, out_specs=out_specs, check_vma=False
    )
```

profile of v0, /device:TPU:0, one launch (start us, length us, event | category | flops | bytes accessed | tf_op | source)
XLA Modules:
  0.0 573.2 jit_solution(7925349174261862744)
XLA Ops:
  10.2 1.9 all_gather.18
  12.9 2.1 all_gather.20
  15.9 32.4 %all-gather.2 = bf16[8,4,4096]{2,1,0:T(4,128)(2,1)S(1)} all-gather(bf16[1,4,4096]{2,1,0:T(4,128)(2,1)S(1)} %fusion.42), channel_id=1, replica_groups=mesh['group'=2,'dp'=2,'expert'=8] {'expert'}, dimensions={0}, use_global_device_ids=true | all-gather | bytes 294912 | tf_op jit(solution)/shard_map/all_gather | solution.py:87
  48.4 4.9 fusion.79
  56.1 37.5 %psum.14 = f32[32,288]{1,0:T(8,128)S(1)} all-reduce(f32[32,288]{1,0:T(8,128)S(1)} %fusion.80), channel_id=1, replica_groups=mesh['group'=2,'dp'=2,'expert'=8] {'expert'}, use_global_device_ids=true, to_apply=%region_2.3 | all-reduce | flops 9216 | bytes 73728 | tf_op jit(solution)/shard_map/psum | solution.py:101
  95.9 3.9 convolution_convert_fusion.1
  119.1 1.8 fusion.34
  121.0 46.9 %all-reduce.9.cloned.1.call-done = bf16[32,4096]{1,0:T(8,128)(2,1)} async-done(((bf16[32,4096]{1,0:T(8,128)(2,1)}), bf16[32,4096]{1,0:T(8,128)(2,1)}) %all-reduce.9.cloned.1.call-update) | async-done | bytes 262160
  169.9 31.9 %all-gather = bf16[32,2,4096]{2,1,0:T(2,128)(2,1)S(1)} all-gather(bf16[2,2,4096]{2,1,0:T(2,128)(2,1)S(1)} %convolution_convert_fusion.3), channel_id=2, replica_groups=mesh['group'=2,'dp'=2,'expert'=8] {'dp','expert'}, dimensions={0}, use_global_device_ids=true | all-gather | bytes 557056 | tf_op jit(solution)/shard_map/all_gather | solution.py:133
  204.5 5.6 fusion.10
  210.1 2.3 fusion.26
  212.7 4.5 fusion.2
  217.3 74.8 %all-reduce.12 = bf16[64,4096]{1,0:T(8,128)(2,1)S(1)} all-reduce(f32[64,4096]{1,0:T(8,128)S(1)} %fusion.2), channel_id=5, replica_groups=mesh['group'=2,'dp'=2,'expert'=8] {'dp','expert'}, use_global_device_ids=true, to_apply=%region_9.10.clone | all-reduce | flops 262144 | bytes 1572864
  293.6 30.8 %all-gather.3 = bf16[8,4,4096]{2,1,0:T(4,128)(2,1)S(1)} all-gather(bf16[1,4,4096]{2,1,0:T(4,128)(2,1)S(1)} %fusion.39), channel_id=1, replica_groups=mesh['group'=2,'dp'=2,'expert'=8] {'expert'}, dimensions={0}, use_global_device_ids=true | all-gather | bytes 294912 | tf_op jit(solution)/shard_map/all_gather | solution.py:87
  324.5 4.9 fusion.81
  330.1 36.1 %psum.15 = f32[32,288]{1,0:T(8,128)S(1)} all-reduce(f32[32,288]{1,0:T(8,128)S(1)} %fusion.82), channel_id=1, replica_groups=mesh['group'=2,'dp'=2,'expert'=8] {'expert'}, use_global_device_ids=true, to_apply=%region_12.13 | all-reduce | flops 9216 | bytes 73728 | tf_op jit(solution)/shard_map/psum | solution.py:101
  366.7 1.8 multiply_reduce_fusion
  368.4 3.7 convolution_convert_fusion
  373.2 67.1 %all-reduce.11.cloned.1.call-done = bf16[32,4096]{1,0:T(8,128)(2,1)} async-done(((bf16[32,4096]{1,0:T(8,128)(2,1)}), bf16[32,4096]{1,0:T(8,128)(2,1)}) %all-reduce.11.cloned.1.call-update) | async-done | bytes 262160
  442.3 31.9 %all-gather.1 = bf16[32,2,4096]{2,1,0:T(2,128)(2,1)S(1)} all-gather(bf16[2,2,4096]{2,1,0:T(2,128)(2,1)S(1)} %convolution_convert_fusion.2), channel_id=3, replica_groups=mesh['group'=2,'dp'=2,'expert'=8] {'dp','expert'}, dimensions={0}, use_global_device_ids=true | all-gather | bytes 557056 | tf_op jit(solution)/shard_map/all_gather | solution.py:133
  474.6 5.3 fusion.8
  479.9 5.4 fusion.23
  485.5 4.5 fusion
  490.0 74.4 %all-reduce.13 = bf16[64,4096]{1,0:T(8,128)(2,1)S(1)} all-reduce(f32[64,4096]{1,0:T(8,128)S(1)} %fusion), channel_id=7, replica_groups=mesh['group'=2,'dp'=2,'expert'=8] {'dp','expert'}, use_global_device_ids=true, to_apply=%region_19.20.clone | all-reduce | flops 262144 | bytes 1572864
  (155 shorter events, 40.7 us)
Async XLA Ops:
  7.2 48.8 %copy-start = (bf16[288,512]{1,0:T(8,128)(2,1)S(1)}, bf16[288,512]{1,0:T(8,128)(2,1)}, u32[]{:S(2)}) copy-start(bf16[288,512]{1,0:T(8,128)(2,1)} %param.28) | copy-start | bytes 884740
  7.2 160.7 %all-reduce.9.cloned.1.call-start = ((), (), s32[]{:S(2)}) async-start(), calls=%async_computation | async-start | bytes 524288
  7.9 86.8 %copy-start.24 = (pred[32]{0:T(512)(128)(4,1)}, pred[32]{0:T(512)(128)(4,1)S(1)}, u32[]{:S(2)}) copy-start(pred[32]{0:T(512)(128)(4,1)S(1)} %compare_and_fusion.4) | copy-start | bytes 100
  48.4 45.9 %copy-start.7 = (bf16[256,512]{1,0:T(8,128)(2,1)S(1)}, bf16[256,512]{1,0:T(8,128)(2,1)}, u32[]{:S(2)}) copy-start(bf16[256,512]{1,0:T(8,128)(2,1)} %param.29) | copy-start | bytes 786436
  48.4 45.9 %copy-start.18 = (f32[512]{0:T(512)S(1)}, f32[512]{0:T(512)}, u32[]{:S(2)}) copy-start(f32[512]{0:T(512)} %param.30) | copy-start | bytes 6148
  95.9 114.2 %slice-start = ((s8[7340032]{0:T(1024)(128)(4,1)}), s8[3145728]{0:T(1024)(128)(4,1)S(1)}, s32[]{:S(2)}) async-start(s8[7340032]{0:T(1024)(128)(4,1)} %bitcast.122), calls=%async_computation.2 | async-start | bytes 6291456
  99.9 340.4 %all-reduce.11.cloned.1.call-start = ((), (), s32[]{:S(2)}) async-start(), calls=%async_computation.1 | async-start | bytes 524288
  212.7 79.5 %copy-start.13 = (bf16[2,4,4096]{2,1,0:T(4,128)(2,1)S(1)}, bf16[2,4,4096]{2,1,0:T(4,128)(2,1)}, u32[]{:S(2)}) copy-start(bf16[2,4,4096]{2,1,0:T(4,128)(2,1)} %param.20) | copy-start | bytes 196612
  212.7 79.5 %copy-start.31 = (s32[2,4]{1,0:T(2,128)S(1)}, s32[2,4]{1,0:T(2,128)}, u32[]{:S(2)}) copy-start(s32[2,4]{1,0:T(2,128)} %copy.47) | copy-start | bytes 100
  212.7 79.5 %copy-start.32 = (f32[4,2]{0,1:T(2,128)S(1)}, f32[4,2]{0,1:T(2,128)}, u32[]{:S(2)}) copy-start(f32[4,2]{0,1:T(2,128)} %select_reduce_fusion.1) | copy-start | bytes 100
  212.7 79.5 %copy-start.35 = (pred[4,2]{0,1:T(4,128)(4,1)S(1)}, pred[4,2]{0,1:T(4,128)(4,1)}, u32[]{:S(2)}) copy-start(pred[4,2]{0,1:T(4,128)(4,1)} %fusion.58) | copy-start | bytes 28
  212.7 80.7 %copy-start.15 = (f32[4096]{0:T(1024)S(1)}, f32[4096]{0:T(1024)}, u32[]{:S(2)}) copy-start(f32[4096]{0:T(1024)} %param.24) | copy-start | bytes 49156
  324.4 41.9 %copy-start.8 = (bf16[256,512]{1,0:T(8,128)(2,1)S(1)}, bf16[256,512]{1,0:T(8,128)(2,1)}, u32[]{:S(2)}) copy-start(bf16[256,512]{1,0:T(8,128)(2,1)} %param.29) | copy-start | bytes 786436
  324.4 41.9 %copy-start.19 = (f32[512]{0:T(512)S(1)}, f32[512]{0:T(512)}, u32[]{:S(2)}) copy-start(f32[512]{0:T(512)} %param.30) | copy-start | bytes 6148
  324.5 42.2 %copy-start.2 = (f32[32,16,512]{2,1,0:T(8,128)S(1)}, f32[32,16,512]{2,1,0:T(8,128)}, u32[]{:S(2)}) copy-start(f32[32,16,512]{2,1,0:T(8,128)} %copy-done.1) | copy-start | bytes 3145732
  324.5 42.2 %copy-start.10 = (f32[32,512]{1,0:T(8,128)S(1)}, f32[32,512]{1,0:T(8,128)}, u32[]{:S(2)}) copy-start(f32[32,512]{1,0:T(8,128)} %copy-done.9) | copy-start | bytes 196612
  324.5 42.2 %copy-start.12 = (f32[32,512]{1,0:T(8,128)S(1)}, f32[32,512]{1,0:T(8,128)}, u32[]{:S(2)}) copy-start(f32[32,512]{1,0:T(8,128)} %copy-done.11) | copy-start | bytes 196612
  324.5 42.2 %copy-start.25 = (pred[32]{0:T(512)(128)(4,1)S(1)}, pred[32]{0:T(512)(128)(4,1)}, u32[]{:S(2)}) copy-start(pred[32]{0:T(512)(128)(4,1)} %copy-done.24) | copy-start | bytes 100
  324.5 43.9 %copy-start.20 = (f32[512]{0:T(512)S(1)}, f32[512]{0:T(512)}, u32[]{:S(2)}) copy-start(f32[512]{0:T(512)} %param.32) | copy-start | bytes 6148
  329.4 42.7 %copy-start.21 = (s32[4,2]{1,0:T(4,128)S(1)}, s32[4,2]{1,0:T(4,128)}, u32[]{:S(2)}) copy-start(s32[4,2]{1,0:T(4,128)} %reduce_window_sum.18) | copy-start | bytes 100
  329.4 42.8 %copy-start.27 = (s32[4,2]{0,1:T(2,128)S(1)}, s32[4,2]{0,1:T(2,128)}, u32[]{:S(2)}) copy-start(s32[4,2]{0,1:T(2,128)} %copy-done.26) | copy-start | bytes 100
  329.5 42.8 %copy-start.28 = (f32[4,2]{0,1:T(2,128)S(1)}, f32[4,2]{0,1:T(2,128)}, u32[]{:S(2)}) copy-start(f32[4,2]{0,1:T(2,128)} %get-tuple-element.22) | copy-start | bytes 100
  329.5 111.8 %copy-start.33 = (f32[4096]{0:T(1024)S(1)}, f32[4096]{0:T(1024)}, u32[]{:S(2)}) copy-start(f32[4096]{0:T(1024)} %param.34) | copy-start | bytes 49156
  329.5 111.8 %copy-start.34 = (pred[4,2]{0,1:T(4,128)(4,1)S(1)}, pred[4,2]{0,1:T(4,128)(4,1)}, u32[]{:S(2)}) copy-start(pred[4,2]{0,1:T(4,128)(4,1)} %fusion.56) | copy-start | bytes 28
  (16 other events, 130.9 us)
Sparse Core Ops, SparseCore 0:
  100.0 67.8 all-reduce.8
  372.3 67.9 all-reduce.10
where the time goes:
time: 576 us; the launch traced here: 573 us
  blocking collectives  354 us (61%)
  waiting for transfers between devices  114 us (20%)
  matrix products  50.4 us (9%)
  other arithmetic  21.1 us (4%)
  local copies, waits for them, and re-layouts  17.6 us (3%)
  between operations  16 us (3%)
    unnamed x2, blocking collectives  149 us
    unnamed x4, waiting for transfers between devices  114 us
    psum x2, blocking collectives, on_device(): projected = lax.psum(mixer_partial_value, 'expert')  73.7 us
    all_gather x2, blocking collectives, on_device(): lax.all_gather(buffer[None], ('dp', 'expert'), axis=0, tiled=True)  63.9 us
    all_gather x2, blocking collectives, on_device(): lax.all_gather(normed, 'expert', axis=0, tiled=True)  63.2 us
  transfers between devices with their start and end apart: 2, of which 2 were waited for; matrix products, arithmetic and copies ran while one was open for 4% of the time, Pallas kernels for 0%

commit v1 on v0

v1 whole, which is shorter than its diff:
```python
import functools

import jax
import jax.numpy as jnp
from jax import lax
from jax.experimental import pallas as pl
from jax.experimental.pallas import tpu as pltpu
from jax.sharding import PartitionSpec as P

CAP = 2
EPS = 1e-05
MIB = 1 << 20
F32 = jnp.float32
BF16 = jnp.bfloat16
VMEM = pl.BlockSpec(memory_space=pltpu.VMEM)
SMEM = pl.BlockSpec(memory_space=pltpu.SMEM)


def silu(values):
    return values / (1.0 + jnp.exp(-values))


def softplus(values):
    return jnp.maximum(values, 0.0) + jnp.log1p(jnp.exp(-jnp.abs(values)))


def normalize(values, gain):
    return values * lax.rsqrt(jnp.mean(values * values, axis=-1, keepdims=True) + EPS) * gain


def held(array):
    return pltpu.with_memory_space_constraint(array, pltpu.VMEM)


def call(body, name, outs, specs, args, scratch=(), flops=0, moved=0, limit=8):
    return pl.pallas_call(
        body,
        name=name,
        out_shape=[jax.ShapeDtypeStruct(s, d) for s, d in outs],
        in_specs=specs,
        out_specs=[VMEM] * len(outs),
        scratch_shapes=list(scratch),
        cost_estimate=pl.CostEstimate(flops=flops, bytes_accessed=moved, transcendentals=0),
        compiler_params=pltpu.CompilerParams(vmem_limit_bytes=limit * MIB),
    )(*args)


def levels_of(count):
    levels, stride = [], 1
    while count // stride > 2:
        size = 4 if count // stride >= 8 else 2
        levels.append((stride, size))
        stride *= size
    return levels, stride


def partner(array, distance, count):
    return lax.ppermute(array, "expert", [(i, i ^ distance) for i in range(count)])


def other_core(array):
    return lax.ppermute(array, "dp", [(0, 1), (1, 0)])


def total(parts):
    result = parts[0].astype(F32)
    for part in parts[1:]:
        result = result + part.astype(F32)
    return result


def spread(block, levels, count):
    parts = [block]
    for position, (stride, size) in enumerate(reversed(levels)):
        whole = parts[0] if position == 0 else jnp.concatenate(parts, axis=0)
        parts = [whole] + [partner(whole, k * stride, count) for k in range(1, size)]
    return parts


def collect(parts, levels, count):
    for position, (stride, size) in enumerate(levels):
        if position > 0:
            parts = jnp.split(parts, size, axis=0)
        parts = total([parts[0]] + [partner(parts[k], k * stride, count) for k in range(1, size)])
        parts = parts.astype(BF16)
    return parts[0] if isinstance(parts, list) else parts


def add_everywhere(parts, levels, count):
    for position, (stride, size) in enumerate(levels):
        if position > 0:
            rows, columns = parts.shape
            split = parts.reshape(stride, size, rows // (stride * size), columns)
            parts = [
                jnp.stack([split[:, j ^ k] for j in range(size)], axis=1).reshape(rows, columns)
                for k in range(size)
            ]
        sent = [partner(parts[k], k * stride, count) for k in range(1, size)]
        parts = total([parts[0]] + sent).astype(BF16)
    return parts[0] if isinstance(parts, list) else parts


def joined(refs):
    if len(refs) == 1:
        return refs[0][...]
    return jnp.concatenate([r[...].astype(F32) for r in refs], axis=0).astype(BF16)


def place_rows(scratch, own, peer, upper):
    rows = own.shape[0]

    @pl.when(upper == 0)
    def _():
        scratch[0:rows, :] = own
        scratch[rows : 2 * rows, :] = peer

    @pl.when(upper != 0)
    def _():
        scratch[0:rows, :] = peer
        scratch[rows : 2 * rows, :] = own


def start_body(where, own, peer, gain, x_out, normed_out):
    place_rows(x_out, own[0].astype(F32), peer[0].astype(F32), where[1])
    normed_out[...] = normalize(x_out[...], gain[...]).astype(BF16)


def table_body(steps, rows, where, own, peer, select_out, combine_out):
    slots = 4 * CAP
    span = 2 * rows
    slot_a = lax.broadcasted_iota(jnp.int32, (slots, span), 0)
    row_a = lax.broadcasted_iota(jnp.int32, (slots, span), 1)
    row_b = lax.broadcasted_iota(jnp.int32, (span, slots), 0)
    slot_b = lax.broadcasted_iota(jnp.int32, (span, slots), 1)
    for step in range(steps):
        select = jnp.zeros((slots, span), F32)
        combine = jnp.zeros((span, slots), F32)
        for far in range(2):
            expert = (where[2] if far == 0 else 1 - where[2]).astype(F32)
            for block in range(2):
                count = jnp.int32(0)
                for j in range(rows):
                    at = (step * rows + j) * 4
                    entry = [
                        jnp.where(where[1] == block, own[at + m], peer[at + m]) for m in range(4)
                    ]
                    first = entry[0] == expert
                    second = entry[1] == expert
                    weight = jnp.where(first, entry[2], 0.0) + jnp.where(second, entry[3], 0.0)
                    named = jnp.where(first | second, 1, 0)
                    row = block * rows + j
                    slot = jnp.where(named == 1, (far * 2 + block) * CAP + count, -1)
                    select = jnp.where((slot_a == slot) & (row_a == row), 1.0, select)
                    combine = jnp.where((slot_b == slot) & (row_b == row), weight, combine)
                    count = count + named
        select_out[step] = select
        combine_out[step] = combine


def row_of(index, rows, levels, stride, me):
    within = index % rows
    half = (index // rows) % 2
    rest = index // (2 * rows)
    distance = 0
    for level_stride, size in reversed(levels):
        distance += (rest % size) * level_stride
        rest //= size
    return (((me ^ distance) & (stride - 1)) + half * stride) * rows + within


def first_taps_body(rows, levels, stride, where, prompts, conv, *taps):
    for index in range(taps[0].shape[0]):
        prompt = prompts[row_of(index, rows, levels, stride, where[0])]
        for j, tap in enumerate(taps):
            tap[index : index + 1, :] = conv[prompt, j : j + 1, :]


def x_body(parts, taps, *refs):
    rows_in, refs = refs[:parts], refs[parts:]
    held_taps, refs = refs[:taps], refs[taps:]
    in_proj, conv_weight, conv_bias, x_proj, x_out, act_out, *proj_outs = refs
    x_part = jnp.dot(joined(rows_in), in_proj[0], preferred_element_type=F32)
    x_out[...] = x_part
    mixed = x_part * conv_weight[taps : taps + 1, :]
    for j in range(taps):
        mixed = mixed + held_taps[j][...] * conv_weight[j : j + 1, :]
    act = silu(mixed + conv_bias[...]).astype(BF16)
    act_out[...] = act
    proj = lax.dot_general(
        act, x_proj[...], (((1,), (1,)), ((), ())), preferred_element_type=F32
    )
    size = proj.shape[0] // parts
    pieces = [proj[k * size : (k + 1) * size] for k in range(parts)]
    for k, out in enumerate(proj_outs):
        out[...] = jnp.concatenate([pieces[j ^ k] for j in range(parts)], axis=0).astype(BF16)


def z_body(parts, *refs):
    rows_in, (in_proj, z_out) = refs[:parts], refs[parts:]
    z_out[...] = silu(jnp.dot(joined(rows_in), in_proj[1], preferred_element_type=F32))


def taps_out_body(rows, levels, stride, where, *refs):
    *taps, out = refs
    for index in range(taps[0].shape[0]):
        row = row_of(index, rows, levels, stride, where[0])
        for j, tap in enumerate(taps):
            out[row, j : j + 1, :] = tap[index : index + 1, :]


def ssm_body(first, parts, rows, levels, stride, *refs):
    where, prompts, near, far, act_in, z_in, dt_proj, dt_bias, a_log, d_skip, out_proj, before = (
        refs[:12]
    )
    outs, (after, y) = refs[12 : 12 + parts], refs[12 + parts :]
    rank = dt_proj.shape[0]
    states = a_log.shape[0]
    projected = near[...].astype(F32) + far[...].astype(F32)
    step_in = projected[:, :rank]
    high = step_in.astype(BF16)
    low = (step_in - high.astype(F32)).astype(BF16)
    delta = softplus(
        jnp.dot(high, dt_proj[...], preferred_element_type=F32)
        + jnp.dot(low, dt_proj[...], preferred_element_type=F32)
        + dt_bias[...]
    )
    maps = jnp.transpose(projected[:, rank:])
    act = act_in[...].astype(F32)
    driven = delta * act
    decay = -jnp.exp(a_log[...])
    for index in range(delta.shape[0]):
        row = row_of(index, rows, levels, stride, where[0])
        held_state = before[prompts[row]] if first else before[row]
        state = (
            jnp.exp(delta[index : index + 1, :] * decay) * held_state
            + driven[index : index + 1, :] * maps[:states, index : index + 1]
        )
        after[row] = state
        y[index : index + 1, :] = jnp.sum(
            state * maps[states:, index : index + 1], axis=0, keepdims=True
        )
    gated = ((y[...] + d_skip[...] * act) * z_in[...]).astype(BF16)
    mixed = jnp.dot(gated, out_proj[...], preferred_element_type=F32)
    size = mixed.shape[0] // parts
    for k, out in enumerate(outs):
        out[...] = mixed[k * size : (k + 1) * size].astype(BF16)


def route_body(near, far, x_in, gain, select, h_out, own_out, other_out):
    h = x_in[...] + (near[...].astype(F32) + far[...].astype(F32))
    h_out[...] = h
    routed = normalize(h, gain[...])
    picked = select[:, 0:1] * routed[0:1, :]
    for r in range(1, h.shape[0]):
        picked = picked + select[:, r : r + 1] * routed[r : r + 1, :]
    half = picked.shape[0] // 2
    own_out[...] = picked[:half].astype(BF16)
    other_out[...] = picked[half:].astype(BF16)


def expert_body(parts, *refs):
    rows_in, (gate, up, down) = refs[:parts], refs[parts : parts + 3]
    outs = refs[parts + 3 :]
    rows = joined(rows_in)
    dims = (((1,), (1,)), ((), ()))
    gate_val = lax.dot_general(rows, gate[...], dims, preferred_element_type=F32)
    up_val = lax.dot_general(rows, up[...], dims, preferred_element_type=F32)
    hidden = (silu(gate_val) * up_val).astype(BF16)
    result = jnp.dot(hidden, down[...], preferred_element_type=F32)
    size = result.shape[0] // parts
    for k, out in enumerate(outs):
        out[...] = result[k * size : (k + 1) * size].astype(BF16)


def combined(h_in, near, far, combine):
    half = far.shape[0]
    result = h_in[...]
    near_rows = near[...].astype(F32)
    far_rows = far[...].astype(F32)
    mixture = combine[:, 0:1] * near_rows[0:1, :]
    for s in range(1, half):
        mixture = mixture + combine[:, s : s + 1] * near_rows[s : s + 1, :]
    for s in range(half):
        mixture = mixture + combine[:, half + s : half + s + 1] * far_rows[s : s + 1, :]
    return (result + mixture).astype(BF16).astype(F32)


def store_own(out, rows, values, upper):
    @pl.when(upper == 0)
    def _():
        out[...] = values[:rows].astype(BF16)

    @pl.when(upper != 0)
    def _():
        out[...] = values[rows:].astype(BF16)


def next_body(step, where, h_in, near, far, combine, own, peer, gain, out, x_out, normed_out):
    values = combined(h_in, near, far, combine)
    store_own(out, out.shape[0], values, where[1])
    place_rows(x_out, own[step + 1].astype(F32), peer[step + 1].astype(F32), where[1])
    x = values + x_out[...]
    x_out[...] = x
    normed_out[...] = normalize(x, gain[...]).astype(BF16)


def last_body(earlier, where, h_in, near, far, combine, *refs):
    before, out = refs[:earlier], refs[earlier]
    values = combined(h_in, near, far, combine)
    for step in range(earlier):
        out[step] = before[step][...]
    store_own(out.at[earlier], out.shape[1], values, where[1])


def on_device(
    layer_input,
    prompt_ssm,
    prompt_conv,
    sample_prompt,
    mamba_gain,
    in_proj,
    conv_weight,
    conv_bias,
    x_proj,
    dt_proj,
    dt_bias,
    a_log,
    d_skip,
    out_proj,
    moe_gain,
    route_ids,
    route_weights,
    w_gate,
    w_up,
    w_down,
):
    count = lax.axis_size("expert")
    levels, stride = levels_of(count)
    parts = levels[0][1] if levels else 1
    steps, rows, width = layer_input.shape
    group_rows = rows * count
    channels = in_proj.shape[2]
    taps = prompt_conv.shape[1]
    states = a_log.shape[0]
    slots = 2 * 2 * CAP
    me = lax.axis_index("expert")
    core = lax.axis_index("dp")
    where = jnp.stack([me, me // stride, core]).astype(jnp.int32)

    peer_input = partner(layer_input, stride, count)
    routes = jnp.concatenate([route_ids.astype(F32), route_weights], axis=2)
    peer_routes = partner(routes, stride, count)
    peer_ssm = other_core(prompt_ssm)
    peer_conv = other_core(prompt_conv)
    all_ssm = jnp.where(
        core == 0,
        jnp.concatenate([prompt_ssm, peer_ssm]),
        jnp.concatenate([peer_ssm, prompt_ssm]),
    )
    all_conv = jnp.where(
        core == 0,
        jnp.concatenate([prompt_conv, peer_conv]),
        jnp.concatenate([peer_conv, prompt_conv]),
    )
    mamba_gain = mamba_gain.reshape(1, width)
    moe_gain = moe_gain.reshape(1, width)
    conv_bias = conv_bias.reshape(1, channels)
    dt_bias = dt_bias.reshape(1, channels)
    d_skip = d_skip.reshape(1, channels)
    gate, up, down = w_gate[0], w_up[0], w_down[0]
    place = (rows, levels, stride)

    x, normed = call(
        start_body,
        "first_norm",
        [((2 * rows, width), F32), ((2 * rows, width), BF16)],
        [SMEM, VMEM, VMEM, VMEM],
        (where, layer_input, peer_input, mamba_gain),
    )
    select, combine = call(
        functools.partial(table_body, steps, rows),
        "route_tables",
        [((steps, slots, 2 * rows), F32), ((steps, 2 * rows, slots), F32)],
        [SMEM, SMEM, SMEM],
        (where, routes.reshape(-1), peer_routes.reshape(-1)),
    )
    window = call(
        functools.partial(first_taps_body, *place),
        "first_taps",
        [((group_rows, channels), F32)] * taps,
        [SMEM, SMEM, VMEM],
        (where, sample_prompt, all_conv),
    )
    state = all_ssm
    outputs = []
    for step in range(steps):
        last = step == steps - 1
        rows_in = spread(normed, levels, count)
        x_part, act, *proj = call(
            functools.partial(x_body, parts, taps),
            "mamba_x",
            [
                ((group_rows, channels), F32),
                ((group_rows, channels), BF16),
            ]
            + [((group_rows, x_proj.shape[0]), BF16)] * parts,
            [VMEM] * (parts + taps + 4),
            (*rows_in, *window, held(in_proj), conv_weight, conv_bias, held(x_proj)),
            flops=2 * group_rows * width * channels,
            moved=2 * width * channels,
        )
        window = [*window[1:], x_part]
        proj = add_everywhere(proj, levels, count)
        proj_far = partner(proj, stride, count)
        z_gate = call(
            functools.partial(z_body, parts),
            "mamba_z",
            [((group_rows, channels), F32)],
            [VMEM] * (parts + 1),
            (*rows_in, held(in_proj)),
            flops=2 * group_rows * width * channels,
            moved=2 * width * channels,
        )[0]
        if last:
            conv_state = call(
                functools.partial(taps_out_body, *place),
                "taps_out",
                [((group_rows, taps, channels), F32)],
                [SMEM] + [VMEM] * taps,
                (where, *window),
            )[0]
        *mixed, state = call(
            functools.partial(ssm_body, step == 0, parts, *place),
            "mamba_ssm",
            [((group_rows // parts, width), BF16)] * parts
            + [((group_rows, states, channels), F32)],
            [SMEM, SMEM] + [VMEM] * 10,
            (
                where,
                sample_prompt,
                proj,
                proj_far,
                act,
                z_gate,
                held(dt_proj),
                dt_bias,
                a_log,
                d_skip,
                held(out_proj),
                state,
            ),
            scratch=[pltpu.VMEM((group_rows, channels), F32)],
            flops=2 * group_rows * width * channels,
            moved=2 * width * channels,
        )
        mixed_near = collect(mixed, levels, count)
        mixed_far = partner(mixed_near, stride, count)
        h, own, other = call(
            route_body,
            "route",
            [
                ((2 * rows, width), F32),
                ((slots // 2, width), BF16),
                ((slots // 2, width), BF16),
            ],
            [VMEM] * 5,
            (mixed_near, mixed_far, x, moe_gain, select[step]),
        )
        picked = spread(jnp.concatenate([own, other_core(other)]), levels, count)
        total_slots = slots * (count // 2)
        returned = call(
            functools.partial(expert_body, parts),
            "experts",
            [((total_slots // parts, width), BF16)] * parts,
            [VMEM] * (parts + 3),
            (*picked, held(gate), held(up), held(down)),
            flops=6 * total_slots * width * gate.shape[0],
            moved=6 * width * gate.shape[0],
        )
        out_near = collect(returned, levels, count)
        summed = total([out_near, partner(out_near, stride, count)]).astype(BF16)
        out_far = other_core(summed[slots // 2 :])
        if last:
            layer_output = call(
                functools.partial(last_body, step),
                "last_output",
                [((steps, rows, width), BF16)],
                [SMEM] + [VMEM] * (4 + step),
                (where, h, summed, out_far, combine[step], *outputs),
            )[0]
        else:
            out, x, normed = call(
                functools.partial(next_body, step),
                "next_norm",
                [
                    ((rows, width), BF16),
                    ((2 * rows, width), F32),
                    ((2 * rows, width), BF16),
                ],
                [SMEM] + [VMEM] * 7,
                (where, h, summed, out_far, combine[step], layer_input, peer_input, mamba_gain),
            )
            outputs.append(out)
    return (layer_output, state, conv_state)


def solution(mesh):
    in_specs = (
        P(None, ("group", "dp", "expert"), None),
        P(("group", "dp"), None, "expert"),
        P(("group", "dp"), None, "expert"),
        P(("group", "dp")),
        P(),
        P(None, None, "expert"),
        P(None, "expert"),
        P("expert"),
        P(None, "expert"),
        P(None, "expert"),
        P("expert"),
        P(None, "expert"),
        P("expert"),
        P("expert", None),
        P(),
        P(None, ("group", "dp", "expert"), None),
        P(None, ("group", "dp", "expert"), None),
        P("dp", "expert", None),
        P("dp", "expert", None),
        P("dp", "expert", None),
    )
    out_specs = (
        P(None, ("group", "dp", "expert"), None),
        P(("group", "dp"), None, "expert"),
        P(("group", "dp"), None, "expert"),
    )
    return jax.shard_map(
        on_device, mesh=mesh, in_specs=in_specs, out_specs=out_specs, check_vma=False
    )
```

time: 576 us -> 159 us (0.28)
  blocking collectives: 354 us -> 0 us
  waiting for transfers between devices: 114 us -> 53.9 us
  starting transfers between devices: 0.08 us -> 59.2 us
  matrix products: 50.4 us -> 0 us
  Pallas kernels: 0 us -> 24.9 us
  other arithmetic: 21.1 us -> 0.41 us
  between operations: 16 us -> 1.16 us
    unnamed x2 -> x0, blocking collectives: 149 us -> none
    all_gather x6 -> x0, blocking collectives: 131 us -> none  [the longest x2 63.9 us: on_device(): lax.all_gather(buffer[None], ('dp', 'expert'), axis=0, tiled=True)]
    unnamed x4 -> x0, waiting for transfers between devices: 114 us -> none
    psum x2 -> x0, blocking collectives: 73.7 us -> none  [on_device(): projected = lax.psum(mixer_partial_value, 'expert')]
    ppermute x0 -> x44, starting transfers between devices: none -> 59.2 us  [the longest x38 58.5 us: partner(): lax.ppermute(array, 'expert', [(i, i ^ distance) for i in range(count)])]
    ppermute x0 -> x44, waiting for transfers between devices: none -> 53.9 us  [the longest x38 50.3 us: partner(): lax.ppermute(array, 'expert', [(i, i ^ distance) for i in range(count)])]
    dot_general x18 -> x0, matrix products: 50.4 us -> none  [the longest x2 10.9 us: expert_hidden(): lax.dot_general(rows_in, gate_rows, dims, preferred_element_type=jnp.floa...]
    pallas_call x0 -> x16, Pallas kernels: none -> 24.9 us  [call(): pl.pallas_call(body, name=name, out_shape=[jax.ShapeDtypeStruct(s, d) for...]
  transfers between devices with their start and end apart: 2 -> 44, of which waited for: 2 -> 37; matrix products, arithmetic and copies ran while one was open for 4% -> 1% of each run, Pallas kernels for 0% -> 3%
where the time goes in v1:
time: 159 us
  starting transfers between devices  59.2 us (37%)
  waiting for transfers between devices  53.9 us (34%)
  Pallas kernels  24.9 us (16%)
  local copies, waits for them, and re-layouts  19.2 us (12%)
    ppermute x38, starting transfers between devices, partner(): lax.ppermute(array, 'expert', [(i, i ^ distance) for i in range(count)])  58.5 us
    ppermute x38, waiting for transfers between devices, partner(): lax.ppermute(array, 'expert', [(i, i ^ distance) for i in range(count)])  50.3 us
    pallas_call x16, Pallas kernels, call(): pl.pallas_call(body, name=name, out_shape=[jax.ShapeDtypeStruct(s, d) for...  24.9 us
    unnamed x72, local copies, waits for them, and re-layouts  18.8 us
    ppermute x6, waiting for transfers between devices, other_core(): return lax.ppermute(array, 'dp', [(0, 1), (1, 0)])  3.58 us
  transfers between devices with their start and end apart: 44, of which 37 were waited for; matrix products, arithmetic and copies ran while one was open for 1% of the time, Pallas kernels for 3%

profile of v1, /device:TPU:0, one launch (start us, length us, event | category | flops | bytes accessed | tf_op | source)
XLA Modules:
  0.0 158.7 jit_solution(5376374463402203400)
XLA Ops:
  1.8 3.6 %collective-permute-start = (bf16[2,4,4096]{2,1,0:T(4,128)(2,1)}, bf16[2,4,4096]{2,1,0:T(4,128)(2,1)S(1)}, u32[]{:S(2)}, u32[]{:S(2)}) collective-permute-start(bf16[2,4,4096]{2,1,0:T(4,128)(2,1)} %own.3), channel_id=1, source_target_pairs={{0,4},{1,5},{2,6},{3,7},{4,0},{5,1},{6,2},{7,3},{8,12},{9,13},{10,... | collective-permute-start | bytes 196616 | tf_op jit(solution)/shard_map/ppermute | solution.py:58
  5.5 4.3 %collective-permute-done.peer = bf16[2,4,4096]{2,1,0:T(4,128)(2,1)S(1)} collective-permute-done((bf16[2,4,4096]{2,1,0:T(4,128)(2,1)}, bf16[2,4,4096]{2,1,0:T(4,128)(2,1)S(1)}, u32[]{:S(2)}, u32[]{:S(2)}) %collective-permute-start) | collective-permute-done | bytes 65568 | tf_op jit(solution)/shard_map/ppermute | solution.py:58
  19.4 3.4 %copy-done = bf16[2,4096,512]{2,1,0:T(8,128)(2,1)S(1)} copy-done((bf16[2,4096,512]{2,1,0:T(8,128)(2,1)S(1)}, bf16[2,4096,512]{2,1,0:T(8,128)(2,1)}, u32[]{:S(2)}) %copy-start) | copy-done | bytes 8388632
  32.5 3.6 %collective-permute-start.8 = (bf16[32,288]{1,0:T(8,128)(2,1)S(1)}, bf16[32,288]{1,0:T(8,128)(2,1)S(1)}, u32[]{:S(2)}, u32[]{:S(2)}) collective-permute-start(bf16[32,288]{1,0:T(8,128)(2,1)S(1)} %add_convert_fusion.7.refs_2_), channel_id=1, source_target_pairs={{0,4},{1,5},{2,6},{3,7},{4,0},{5,1},{6,2},{7,3},{8,12},{9,13},{10,... | collective-permute-start | bytes 55304 | tf_op jit(solution)/shard_map/ppermute | solution.py:58
  43.7 2.8 %collective-permute-start.14 = (f32[2,4,4]{1,2,0:T(4,128)S(1)}, f32[2,4,4]{1,2,0:T(4,128)S(1)}, u32[]{:S(2)}, u32[]{:S(2)}) collective-permute-start(f32[2,4,4]{1,2,0:T(4,128)S(1)} %pad_maximum_fusion.2), channel_id=1, source_target_pairs={{0,4},{1,5},{2,6},{3,7},{4,0},{5,1},{6,2},{7,3},{8,12},{9,13},{10,... | collective-permute-start | bytes 392 | tf_op jit(solution)/shard_map/ppermute | solution.py:58
  49.3 2.8 %collective-permute-start.13 = (bf16[8,4096]{1,0:T(8,128)(2,1)S(1)}, bf16[8,4096]{1,0:T(8,128)(2,1)S(1)}, u32[]{:S(2)}, u32[]{:S(2)}) collective-permute-start(bf16[8,4096]{1,0:T(8,128)(2,1)S(1)} %add_convert_fusion.5.near), channel_id=1, source_target_pairs={{0,4},{1,5},{2,6},{3,7},{4,0},{5,1},{6,2},{7,3},{8,12},{9,13},{10,... | collective-permute-start | bytes 196616 | tf_op jit(solution)/shard_map/ppermute | solution.py:58
  52.1 2.4 %collective-permute-done.13.far = bf16[8,4096]{1,0:T(8,128)(2,1)S(1)} collective-permute-done((bf16[8,4096]{1,0:T(8,128)(2,1)S(1)}, bf16[8,4096]{1,0:T(8,128)(2,1)S(1)}, u32[]{:S(2)}, u32[]{:S(2)}) %collective-permute-start.13) | collective-permute-done | bytes 65568 | tf_op jit(solution)/shard_map/ppermute | solution.py:58
  64.1 3.1 %copy-done.2 = bf16[1,896,4096]{2,1,0:T(8,128)(2,1)S(1)} copy-done((bf16[1,896,4096]{2,1,0:T(8,128)(2,1)S(1)}, bf16[1,896,4096]{2,1,0:T(8,128)(2,1)}, u32[]{:S(2)}) %copy-start.2) | copy-done | bytes 7340056
  67.2 3.1 %copy-done.3 = bf16[1,896,4096]{2,1,0:T(8,128)(2,1)S(1)} copy-done((bf16[1,896,4096]{2,1,0:T(8,128)(2,1)S(1)}, bf16[1,896,4096]{2,1,0:T(8,128)(2,1)}, u32[]{:S(2)}) %copy-start.3) | copy-done | bytes 7340056
  70.3 3.1 %copy-done.4 = bf16[1,896,4096]{2,1,0:T(8,128)(2,1)S(1)} copy-done((bf16[1,896,4096]{2,1,0:T(8,128)(2,1)S(1)}, bf16[1,896,4096]{2,1,0:T(8,128)(2,1)}, u32[]{:S(2)}) %copy-start.4) | copy-done | bytes 7340056
  73.4 5.7 %experts.2 = (bf16[8,4096]{1,0:T(8,128)(2,1)S(1)}, bf16[8,4096]{1,0:T(8,128)(2,1)S(1)}, bf16[8,4096]{1,0:T(8,128)(2,1)S(1)}, bf16[8,4096]{1,0:T(8,128)(2,1)S(1)}) custom-call(bf16[8,4096]{1,0:T(8,128)(2,1)S(1)} %pad_maximum_fusion.refs_0_, bf16[8,4096]{1,0:T(8,128)(2,1)S(1)} %collective-permute-done.16.refs_1_, ...), custom_call_target="tpu_custom_call" | custom-call | flops 704643072 | bytes 22020096 | tf_op jit(solution)/shard_map/experts/pallas_call | solution.py:36
  80.4 2.2 %collective-permute-start.21 = (bf16[8,4096]{1,0:T(8,128)(2,1)S(1)}, bf16[8,4096]{1,0:T(8,128)(2,1)S(1)}, u32[]{:S(2)}, u32[]{:S(2)}) collective-permute-start(bf16[8,4096]{1,0:T(8,128)(2,1)S(1)} %get-tuple-element.70), channel_id=1, source_target_pairs={{0,3},{1,2},{2,1},{3,0},{4,7},{5,6},{6,5},{7,4},{8,11},{9,10},{10,... | collective-permute-start | bytes 196616 | tf_op jit(solution)/shard_map/ppermute | solution.py:58
  87.5 3.3 %collective-permute-done.22 = bf16[8,4096]{1,0:T(8,128)(2,1)S(1)} collective-permute-done((bf16[8,4096]{1,0:T(8,128)(2,1)S(1)}, bf16[8,4096]{1,0:T(8,128)(2,1)S(1)}, u32[]{:S(2)}, u32[]{:S(2)}) %collective-permute-start.22) | collective-permute-done | bytes 65568 | tf_op jit(solution)/shard_map/ppermute | solution.py:58
  93.2 2.2 %collective-permute-start.26 = (bf16[8,4096]{1,0:T(8,128)(2,1)S(1)}, bf16[8,4096]{1,0:T(8,128)(2,1)S(1)}, u32[]{:S(2)}, u32[]{:S(2)}) collective-permute-start(bf16[8,4096]{1,0:T(8,128)(2,1)S(1)} %get-tuple-element.72.refs_0_), channel_id=1, source_target_pairs={{0,3},{1,2},{2,1},{3,0},{4,7},{5,6},{6,5},{7,4},{8,11},{9,10},{10,... | collective-permute-start | bytes 196616 | tf_op jit(solution)/shard_map/ppermute | solution.py:58
  96.8 2.1 %collective-permute-done.26.refs_3_ = bf16[8,4096]{1,0:T(8,128)(2,1)S(1)} collective-permute-done((bf16[8,4096]{1,0:T(8,128)(2,1)S(1)}, bf16[8,4096]{1,0:T(8,128)(2,1)S(1)}, u32[]{:S(2)}, u32[]{:S(2)}) %collective-permute-start.26) | collective-permute-done | bytes 65568 | tf_op jit(solution)/shard_map/ppermute | solution.py:58
  106.1 2.3 %collective-permute-done.29 = bf16[32,288]{1,0:T(8,128)(2,1)S(1)} collective-permute-done((bf16[32,288]{1,0:T(8,128)(2,1)S(1)}, bf16[32,288]{1,0:T(8,128)(2,1)S(1)}, u32[]{:S(2)}, u32[]{:S(2)}) %collective-permute-start.29) | collective-permute-done | bytes 18464 | tf_op jit(solution)/shard_map/ppermute | solution.py:58
  108.4 2.8 %collective-permute-start.30 = (bf16[32,288]{1,0:T(8,128)(2,1)S(1)}, bf16[32,288]{1,0:T(8,128)(2,1)S(1)}, u32[]{:S(2)}, u32[]{:S(2)}) collective-permute-start(bf16[32,288]{1,0:T(8,128)(2,1)S(1)} %add_convert_fusion.6.refs_2_), channel_id=1, source_target_pairs={{0,4},{1,5},{2,6},{3,7},{4,0},{5,1},{6,2},{7,3},{8,12},{9,13},{10,... | collective-permute-start | bytes 55304 | tf_op jit(solution)/shard_map/ppermute | solution.py:58
  113.5 2.2 %mamba_ssm.3 = (bf16[8,4096]{1,0:T(8,128)(2,1)S(1)}, bf16[8,4096]{1,0:T(8,128)(2,1)S(1)}, bf16[8,4096]{1,0:T(8,128)(2,1)S(1)}, bf16[8,4096]{1,0:T(8,128)(2,1)S(1)}, f32[32,16,512]{2,1,0:T(8,128)}) custom-call(s32[3]{0:T(128)S(1)} %pad_add_fusion.where.refs_0_, s32[32]{0:T(128)S(1)} %copy-done.23, bf16[32,288]{1,0:T(8,128)(2,1)S(1)} %add_convert_fusion.6.refs_2_, ...), custom_call_target="tpu_custom_call" | custom-call | flops 134217728 | bytes 4194304 | tf_op jit(solution)/shard_map/mamba_ssm/pallas_call | solution.py:36
  117.0 2.2 %collective-permute-start.33 = (bf16[8,4096]{1,0:T(8,128)(2,1)S(1)}, bf16[8,4096]{1,0:T(8,128)(2,1)S(1)}, u32[]{:S(2)}, u32[]{:S(2)}) collective-permute-start(bf16[8,4096]{1,0:T(8,128)(2,1)S(1)} %get-tuple-element.83), channel_id=1, source_target_pairs={{0,3},{1,2},{2,1},{3,0},{4,7},{5,6},{6,5},{7,4},{8,11},{9,10},{10,... | collective-permute-start | bytes 196616 | tf_op jit(solution)/shard_map/ppermute | solution.py:58
  125.0 3.2 %collective-permute-done.34.far = bf16[8,4096]{1,0:T(8,128)(2,1)S(1)} collective-permute-done((bf16[8,4096]{1,0:T(8,128)(2,1)S(1)}, bf16[8,4096]{1,0:T(8,128)(2,1)S(1)}, u32[]{:S(2)}, u32[]{:S(2)}) %collective-permute-start.34) | collective-permute-done | bytes 65568 | tf_op jit(solution)/shard_map/ppermute | solution.py:58
  133.3 2.2 %collective-permute-done.38.refs_3_ = bf16[8,4096]{1,0:T(8,128)(2,1)S(1)} collective-permute-done((bf16[8,4096]{1,0:T(8,128)(2,1)S(1)}, bf16[8,4096]{1,0:T(8,128)(2,1)S(1)}, u32[]{:S(2)}, u32[]{:S(2)}) %collective-permute-start.38) | collective-permute-done | bytes 65568 | tf_op jit(solution)/shard_map/ppermute | solution.py:58
  136.6 5.7 %experts.3 = (bf16[8,4096]{1,0:T(8,128)(2,1)S(1)}, bf16[8,4096]{1,0:T(8,128)(2,1)S(1)}, bf16[8,4096]{1,0:T(8,128)(2,1)S(1)}, bf16[8,4096]{1,0:T(8,128)(2,1)S(1)}) custom-call(bf16[8,4096]{1,0:T(8,128)(2,1)S(1)} %pad_maximum_fusion.1.refs_0_, bf16[8,4096]{1,0:T(8,128)(2,1)S(1)} %collective-permute-done.36.refs_1_, ...), custom_call_target="tpu_custom_call" | custom-call | flops 704643072 | bytes 22020096 | tf_op jit(solution)/shard_map/experts/pallas_call | solution.py:36
  149.7 3.3 %collective-permute-start.42 = (bf16[8,4096]{1,0:T(8,128)(2,1)S(1)}, bf16[8,4096]{1,0:T(8,128)(2,1)S(1)}, u32[]{:S(2)}, u32[]{:S(2)}) collective-permute-start(bf16[8,4096]{1,0:T(8,128)(2,1)S(1)} %add_convert_fusion.1), channel_id=1, source_target_pairs={{0,4},{1,5},{2,6},{3,7},{4,0},{5,1},{6,2},{7,3},{8,12},{9,13},{10,... | collective-permute-start | bytes 196616 | tf_op jit(solution)/shard_map/ppermute | solution.py:58
  153.1 2.8 %collective-permute-done.42 = bf16[8,4096]{1,0:T(8,128)(2,1)S(1)} collective-permute-done((bf16[8,4096]{1,0:T(8,128)(2,1)S(1)}, bf16[8,4096]{1,0:T(8,128)(2,1)S(1)}, u32[]{:S(2)}, u32[]{:S(2)}) %collective-permute-start.42) | collective-permute-done | bytes 65568 | tf_op jit(solution)/shard_map/ppermute | solution.py:58
  (179 shorter events, 83.3 us)
Async XLA Ops:
  1.4 14.2 %collective-permute-start.4 = (f32[2,3,512]{2,1,0:T(4,128)S(1)}, f32[2,3,512]{2,1,0:T(4,128)S(1)}, u32[]{:S(2)}, u32[]{:S(2)}) collective-permute-start(f32[2,3,512]{2,1,0:T(4,128)S(1)} %copy.24), channel_id=1, source_target_pairs={{0,8},{8,0},{1,9},{9,1},{2,10},{10,2},{3,11},{11,3},{4,12},{12,4},... | collective-permute-start | bytes 36872 | tf_op jit(solution)/shard_map/ppermute | solution.py:62
  1.8 8.0 %collective-permute-start = (bf16[2,4,4096]{2,1,0:T(4,128)(2,1)}, bf16[2,4,4096]{2,1,0:T(4,128)(2,1)S(1)}, u32[]{:S(2)}, u32[]{:S(2)}) collective-permute-start(bf16[2,4,4096]{2,1,0:T(4,128)(2,1)} %own.3), channel_id=1, source_target_pairs={{0,4},{1,5},{2,6},{3,7},{4,0},{5,1},{6,2},{7,3},{8,12},{9,13},{10,... | collective-permute-start | bytes 196616 | tf_op jit(solution)/shard_map/ppermute | solution.py:58
  12.1 5.6 %collective-permute-start.3 = (bf16[8,4096]{1,0:T(8,128)(2,1)S(1)}, bf16[8,4096]{1,0:T(8,128)(2,1)S(1)}, u32[]{:S(2)}, u32[]{:S(2)}) collective-permute-start(bf16[8,4096]{1,0:T(8,128)(2,1)S(1)} %get-tuple-element.49.refs_0_), channel_id=1, source_target_pairs={{0,3},{1,2},{2,1},{3,0},{4,7},{5,6},{6,5},{7,4},{8,11},{9,10},{10,... | collective-permute-start | bytes 196616 | tf_op jit(solution)/shard_map/ppermute | solution.py:58
  27.7 4.7 %collective-permute-start.7 = (bf16[32,288]{1,0:T(8,128)(2,1)S(1)}, bf16[32,288]{1,0:T(8,128)(2,1)S(1)}, u32[]{:S(2)}, u32[]{:S(2)}) collective-permute-start(bf16[32,288]{1,0:T(8,128)(2,1)S(1)} %get-tuple-element.56), channel_id=1, source_target_pairs={{0,3},{1,2},{2,1},{3,0},{4,7},{5,6},{6,5},{7,4},{8,11},{9,10},{10,... | collective-permute-start | bytes 55304 | tf_op jit(solution)/shard_map/ppermute | solution.py:58
  29.8 6.2 %collective-permute-start.9 = (f32[2,16,512]{2,1,0:T(8,128)S(1)}, f32[2,16,512]{2,1,0:T(8,128)S(1)}, u32[]{:S(2)}, u32[]{:S(2)}) collective-permute-start(f32[2,16,512]{2,1,0:T(8,128)S(1)} %copy-done.24), channel_id=1, source_target_pairs={{0,8},{8,0},{1,9},{9,1},{2,10},{10,2},{3,11},{11,3},{4,12},{12,4},... | collective-permute-start | bytes 196616 | tf_op jit(solution)/shard_map/ppermute | solution.py:62
  32.5 5.5 %collective-permute-start.8 = (bf16[32,288]{1,0:T(8,128)(2,1)S(1)}, bf16[32,288]{1,0:T(8,128)(2,1)S(1)}, u32[]{:S(2)}, u32[]{:S(2)}) collective-permute-start(bf16[32,288]{1,0:T(8,128)(2,1)S(1)} %add_convert_fusion.7.refs_2_), channel_id=1, source_target_pairs={{0,4},{1,5},{2,6},{3,7},{4,0},{5,1},{6,2},{7,3},{8,12},{9,13},{10,... | collective-permute-start | bytes 55304 | tf_op jit(solution)/shard_map/ppermute | solution.py:58
  40.1 9.1 %collective-permute-start.10 = (bf16[8,4096]{1,0:T(8,128)(2,1)S(1)}, bf16[8,4096]{1,0:T(8,128)(2,1)S(1)}, u32[]{:S(2)}, u32[]{:S(2)}) collective-permute-start(bf16[8,4096]{1,0:T(8,128)(2,1)S(1)} %get-tuple-element.59), channel_id=1, source_target_pairs={{0,1},{1,0},{2,3},{3,2},{4,5},{5,4},{6,7},{7,6},{8,9},{9,8},{10,11... | collective-permute-start | bytes 196616 | tf_op jit(solution)/shard_map/ppermute | solution.py:58
  41.6 7.6 %collective-permute-start.11 = (bf16[8,4096]{1,0:T(8,128)(2,1)S(1)}, bf16[8,4096]{1,0:T(8,128)(2,1)S(1)}, u32[]{:S(2)}, u32[]{:S(2)}) collective-permute-start(bf16[8,4096]{1,0:T(8,128)(2,1)S(1)} %get-tuple-element.60), channel_id=1, source_target_pairs={{0,2},{1,3},{2,0},{3,1},{4,6},{5,7},{6,4},{7,5},{8,10},{9,11},{10,... | collective-permute-start | bytes 196616 | tf_op jit(solution)/shard_map/ppermute | solution.py:58
  42.1 7.1 %collective-permute-start.12 = (bf16[8,4096]{1,0:T(8,128)(2,1)S(1)}, bf16[8,4096]{1,0:T(8,128)(2,1)S(1)}, u32[]{:S(2)}, u32[]{:S(2)}) collective-permute-start(bf16[8,4096]{1,0:T(8,128)(2,1)S(1)} %get-tuple-element.61), channel_id=1, source_target_pairs={{0,3},{1,2},{2,1},{3,0},{4,7},{5,6},{6,5},{7,4},{8,11},{9,10},{10,... | collective-permute-start | bytes 196616 | tf_op jit(solution)/shard_map/ppermute | solution.py:58
  49.3 5.2 %collective-permute-start.13 = (bf16[8,4096]{1,0:T(8,128)(2,1)S(1)}, bf16[8,4096]{1,0:T(8,128)(2,1)S(1)}, u32[]{:S(2)}, u32[]{:S(2)}) collective-permute-start(bf16[8,4096]{1,0:T(8,128)(2,1)S(1)} %add_convert_fusion.5.near), channel_id=1, source_target_pairs={{0,4},{1,5},{2,6},{3,7},{4,0},{5,1},{6,2},{7,3},{8,12},{9,13},{10,... | collective-permute-start | bytes 196616 | tf_op jit(solution)/shard_map/ppermute | solution.py:58
  56.1 5.6 %collective-permute-start.18 = (bf16[8,4096]{1,0:T(8,128)(2,1)S(1)}, bf16[8,4096]{1,0:T(8,128)(2,1)S(1)}, u32[]{:S(2)}, u32[]{:S(2)}) collective-permute-start(bf16[8,4096]{1,0:T(8,128)(2,1)S(1)} %pad_maximum_fusion.refs_0_), channel_id=1, source_target_pairs={{0,3},{1,2},{2,1},{3,0},{4,7},{5,6},{6,5},{7,4},{8,11},{9,10},{10,... | collective-permute-start | bytes 196616 | tf_op jit(solution)/shard_map/ppermute | solution.py:58
  58.1 5.3 %collective-permute-start.17 = (bf16[8,4096]{1,0:T(8,128)(2,1)S(1)}, bf16[8,4096]{1,0:T(8,128)(2,1)S(1)}, u32[]{:S(2)}, u32[]{:S(2)}) collective-permute-start(bf16[8,4096]{1,0:T(8,128)(2,1)S(1)} %pad_maximum_fusion.refs_0_), channel_id=1, source_target_pairs={{0,2},{1,3},{2,0},{3,1},{4,6},{5,7},{6,4},{7,5},{8,10},{9,11},{10,... | collective-permute-start | bytes 196616 | tf_op jit(solution)/shard_map/ppermute | solution.py:58
  79.0 5.0 %collective-permute-start.19 = (bf16[8,4096]{1,0:T(8,128)(2,1)S(1)}, bf16[8,4096]{1,0:T(8,128)(2,1)S(1)}, u32[]{:S(2)}, u32[]{:S(2)}) collective-permute-start(bf16[8,4096]{1,0:T(8,128)(2,1)S(1)} %get-tuple-element.68), channel_id=1, source_target_pairs={{0,1},{1,0},{2,3},{3,2},{4,5},{5,4},{6,7},{7,6},{8,9},{9,8},{10,11... | collective-permute-start | bytes 196616 | tf_op jit(solution)/shard_map/ppermute | solution.py:58
  80.4 5.2 %collective-permute-start.21 = (bf16[8,4096]{1,0:T(8,128)(2,1)S(1)}, bf16[8,4096]{1,0:T(8,128)(2,1)S(1)}, u32[]{:S(2)}, u32[]{:S(2)}) collective-permute-start(bf16[8,4096]{1,0:T(8,128)(2,1)S(1)} %get-tuple-element.70), channel_id=1, source_target_pairs={{0,3},{1,2},{2,1},{3,0},{4,7},{5,6},{6,5},{7,4},{8,11},{9,10},{10,... | collective-permute-start | bytes 196616 | tf_op jit(solution)/shard_map/ppermute | solution.py:58
  85.6 5.2 %collective-permute-start.22 = (bf16[8,4096]{1,0:T(8,128)(2,1)S(1)}, bf16[8,4096]{1,0:T(8,128)(2,1)S(1)}, u32[]{:S(2)}, u32[]{:S(2)}) collective-permute-start(bf16[8,4096]{1,0:T(8,128)(2,1)S(1)} %add_convert_fusion.4), channel_id=1, source_target_pairs={{0,4},{1,5},{2,6},{3,7},{4,0},{5,1},{6,2},{7,3},{8,12},{9,13},{10,... | collective-permute-start | bytes 196616 | tf_op jit(solution)/shard_map/ppermute | solution.py:58
  93.2 5.7 %collective-permute-start.26 = (bf16[8,4096]{1,0:T(8,128)(2,1)S(1)}, bf16[8,4096]{1,0:T(8,128)(2,1)S(1)}, u32[]{:S(2)}, u32[]{:S(2)}) collective-permute-start(bf16[8,4096]{1,0:T(8,128)(2,1)S(1)} %get-tuple-element.72.refs_0_), channel_id=1, source_target_pairs={{0,3},{1,2},{2,1},{3,0},{4,7},{5,6},{6,5},{7,4},{8,11},{9,10},{10,... | collective-permute-start | bytes 196616 | tf_op jit(solution)/shard_map/ppermute | solution.py:58
  103.7 4.7 %collective-permute-start.29 = (bf16[32,288]{1,0:T(8,128)(2,1)S(1)}, bf16[32,288]{1,0:T(8,128)(2,1)S(1)}, u32[]{:S(2)}, u32[]{:S(2)}) collective-permute-start(bf16[32,288]{1,0:T(8,128)(2,1)S(1)} %get-tuple-element.77), channel_id=1, source_target_pairs={{0,3},{1,2},{2,1},{3,0},{4,7},{5,6},{6,5},{7,4},{8,11},{9,10},{10,... | collective-permute-start | bytes 55304 | tf_op jit(solution)/shard_map/ppermute | solution.py:58
  108.4 5.0 %collective-permute-start.30 = (bf16[32,288]{1,0:T(8,128)(2,1)S(1)}, bf16[32,288]{1,0:T(8,128)(2,1)S(1)}, u32[]{:S(2)}, u32[]{:S(2)}) collective-permute-start(bf16[32,288]{1,0:T(8,128)(2,1)S(1)} %add_convert_fusion.6.refs_2_), channel_id=1, source_target_pairs={{0,4},{1,5},{2,6},{3,7},{4,0},{5,1},{6,2},{7,3},{8,12},{9,13},{10,... | collective-permute-start | bytes 55304 | tf_op jit(solution)/shard_map/ppermute | solution.py:58
  116.7 5.0 %collective-permute-start.32 = (bf16[8,4096]{1,0:T(8,128)(2,1)S(1)}, bf16[8,4096]{1,0:T(8,128)(2,1)S(1)}, u32[]{:S(2)}, u32[]{:S(2)}) collective-permute-start(bf16[8,4096]{1,0:T(8,128)(2,1)S(1)} %get-tuple-element.82), channel_id=1, source_target_pairs={{0,2},{1,3},{2,0},{3,1},{4,6},{5,7},{6,4},{7,5},{8,10},{9,11},{10,... | collective-permute-start | bytes 196616 | tf_op jit(solution)/shard_map/ppermute | solution.py:58
  117.0 5.9 %collective-permute-start.33 = (bf16[8,4096]{1,0:T(8,128)(2,1)S(1)}, bf16[8,4096]{1,0:T(8,128)(2,1)S(1)}, u32[]{:S(2)}, u32[]{:S(2)}) collective-permute-start(bf16[8,4096]{1,0:T(8,128)(2,1)S(1)} %get-tuple-element.83), channel_id=1, source_target_pairs={{0,3},{1,2},{2,1},{3,0},{4,7},{5,6},{6,5},{7,4},{8,11},{9,10},{10,... | collective-permute-start | bytes 196616 | tf_op jit(solution)/shard_map/ppermute | solution.py:58
  122.9 5.2 %collective-permute-start.34 = (bf16[8,4096]{1,0:T(8,128)(2,1)S(1)}, bf16[8,4096]{1,0:T(8,128)(2,1)S(1)}, u32[]{:S(2)}, u32[]{:S(2)}) collective-permute-start(bf16[8,4096]{1,0:T(8,128)(2,1)S(1)} %add_convert_fusion.2.near), channel_id=1, source_target_pairs={{0,4},{1,5},{2,6},{3,7},{4,0},{5,1},{6,2},{7,3},{8,12},{9,13},{10,... | collective-permute-start | bytes 196616 | tf_op jit(solution)/shard_map/ppermute | solution.py:58
  129.7 5.8 %collective-permute-start.38 = (bf16[8,4096]{1,0:T(8,128)(2,1)S(1)}, bf16[8,4096]{1,0:T(8,128)(2,1)S(1)}, u32[]{:S(2)}, u32[]{:S(2)}) collective-permute-start(bf16[8,4096]{1,0:T(8,128)(2,1)S(1)} %pad_maximum_fusion.1.refs_0_), channel_id=1, source_target_pairs={{0,3},{1,2},{2,1},{3,0},{4,7},{5,6},{6,5},{7,4},{8,11},{9,10},{10,... | collective-permute-start | bytes 196616 | tf_op jit(solution)/shard_map/ppermute | solution.py:58
  144.5 5.2 %collective-permute-start.41 = (bf16[8,4096]{1,0:T(8,128)(2,1)S(1)}, bf16[8,4096]{1,0:T(8,128)(2,1)S(1)}, u32[]{:S(2)}, u32[]{:S(2)}) collective-permute-start(bf16[8,4096]{1,0:T(8,128)(2,1)S(1)} %get-tuple-element.91), channel_id=1, source_target_pairs={{0,3},{1,2},{2,1},{3,0},{4,7},{5,6},{6,5},{7,4},{8,11},{9,10},{10,... | collective-permute-start | bytes 196616 | tf_op jit(solution)/shard_map/ppermute | solution.py:58
  149.7 6.1 %collective-permute-start.42 = (bf16[8,4096]{1,0:T(8,128)(2,1)S(1)}, bf16[8,4096]{1,0:T(8,128)(2,1)S(1)}, u32[]{:S(2)}, u32[]{:S(2)}) collective-permute-start(bf16[8,4096]{1,0:T(8,128)(2,1)S(1)} %add_convert_fusion.1), channel_id=1, source_target_pairs={{0,4},{1,5},{2,6},{3,7},{4,0},{5,1},{6,2},{7,3},{8,12},{9,13},{10,... | collective-permute-start | bytes 196616 | tf_op jit(solution)/shard_map/ppermute | solution.py:58
  (55 other events, 711.3 us)

commit v2 on v1

--- a/solution.py
+++ b/solution.py
@@ -10,6 +10,7 @@
 CAP = 2
 EPS = 1e-05
 MIB = 1 << 20
+BESIDE = 10**10
 F32 = jnp.float32
 BF16 = jnp.bfloat16
 VMEM = pl.BlockSpec(memory_space=pltpu.VMEM)
@@ -33,6 +34,7 @@
 
 
 def call(body, name, outs, specs, args, scratch=(), flops=0, moved=0, limit=8):
+    flops = max(flops, BESIDE)
     return pl.pallas_call(
         body,
         name=name,
@@ -396,6 +398,10 @@
     for step in range(steps):
         last = step == steps - 1
         rows_in = spread(normed, levels, count)
+        if step == 0:
+            rows_in, select, combine, window, state = lax.optimization_barrier(
+                (rows_in, select, combine, window, state)
+            )
         x_part, act, *proj = call(
             functools.partial(x_body, parts, taps),
             "mamba_x",
@@ -429,6 +435,7 @@
                 [SMEM] + [VMEM] * taps,
                 (where, *window),
             )[0]
+            proj_far, conv_state = lax.optimization_barrier((proj_far, conv_state))
         *mixed, state = call(
             functools.partial(ssm_body, step == 0, parts, *place),
             "mamba_ssm",

time: 159 us -> 143 us (0.90)
  local copies, waits for them, and re-layouts: 19.2 us -> 1.99 us
  starting transfers between devices: 59.2 us -> 45.2 us
  waiting for transfers between devices: 53.9 us -> 67.5 us
    unnamed x72 -> x44, local copies, waits for them, and re-layouts: 18.8 us -> 1.57 us
    ppermute x38, starting transfers between devices: 58.5 us -> 44.4 us  [partner(): lax.ppermute(array, 'expert', [(i, i ^ distance) for i in range(count)])]
    ppermute x38, waiting for transfers between devices: 50.3 us -> 63.5 us  [partner(): lax.ppermute(array, 'expert', [(i, i ^ distance) for i in range(count)])]
  transfers between devices with their start and end apart: 44 -> 44, of which waited for: 37 -> 40; matrix products, arithmetic and copies ran while one was open for 1% -> 1% of each run, Pallas kernels for 3% -> 3%
where the time goes in v2:
time: 143 us
  waiting for transfers between devices  67.5 us (47%)
  starting transfers between devices  45.2 us (32%)
  Pallas kernels  24.9 us (17%)
  local copies, waits for them, and re-layouts  1.99 us (1%)
  other arithmetic  1.77 us (1%)
    ppermute x38, waiting for transfers between devices, partner(): lax.ppermute(array, 'expert', [(i, i ^ distance) for i in range(count)])  63.5 us
    ppermute x38, starting transfers between devices, partner(): lax.ppermute(array, 'expert', [(i, i ^ distance) for i in range(count)])  44.4 us
    pallas_call x16, Pallas kernels, call(): pl.pallas_call(body, name=name, out_shape=[jax.ShapeDtypeStruct(s, d) for...  24.9 us
    ppermute x6, waiting for transfers between devices, other_core(): return lax.ppermute(array, 'dp', [(0, 1), (1, 0)])  4.03 us
  transfers between devices with their start and end apart: 44, of which 40 were waited for; matrix products, arithmetic and copies ran while one was open for 1% of the time, Pallas kernels for 3%

profile of v2, /device:TPU:0, one launch (start us, length us, event | category | flops | bytes accessed | tf_op | source)
XLA Modules:
  0.0 142.5 jit_solution(6930682416432807255)
XLA Ops:
  2.0 4.0 %collective-permute-start.4 = (f32[2,4,4]{1,2,0:T(4,128)S(1)}, f32[2,4,4]{1,2,0:T(4,128)S(1)}, u32[]{:S(2)}, u32[]{:S(2)}) collective-permute-start(f32[2,4,4]{1,2,0:T(4,128)S(1)} %pad_maximum_fusion.2), channel_id=1, source_target_pairs={{0,4},{1,5},{2,6},{3,7},{4,0},{5,1},{6,2},{7,3},{8,12},{9,13},{10,... | collective-permute-start | bytes 392 | tf_op jit(solution)/shard_map/ppermute | solution.py:60
  9.3 4.8 %collective-permute-done.peer = bf16[2,4,4096]{2,1,0:T(4,128)(2,1)S(1)} collective-permute-done((bf16[2,4,4096]{2,1,0:T(4,128)(2,1)}, bf16[2,4,4096]{2,1,0:T(4,128)(2,1)S(1)}, u32[]{:S(2)}, u32[]{:S(2)}) %collective-permute-start) | collective-permute-done | bytes 65568 | tf_op jit(solution)/shard_map/ppermute | solution.py:60
  24.0 3.0 %collective-permute-start.9 = (bf16[32,288]{1,0:T(8,128)(2,1)S(1)}, bf16[32,288]{1,0:T(8,128)(2,1)S(1)}, u32[]{:S(2)}, u32[]{:S(2)}) collective-permute-start(bf16[32,288]{1,0:T(8,128)(2,1)S(1)} %get-tuple-element.77), channel_id=1, source_target_pairs={{0,3},{1,2},{2,1},{3,0},{4,7},{5,6},{6,5},{7,4},{8,11},{9,10},{10,... | collective-permute-start | bytes 55304 | tf_op jit(solution)/shard_map/ppermute | solution.py:60
  31.0 2.9 %collective-permute-done.10.refs_3_ = bf16[32,288]{1,0:T(8,128)(2,1)S(1)} collective-permute-done((bf16[32,288]{1,0:T(8,128)(2,1)S(1)}, bf16[32,288]{1,0:T(8,128)(2,1)S(1)}, u32[]{:S(2)}, u32[]{:S(2)}) %collective-permute-start.10) | collective-permute-done | bytes 18464 | tf_op jit(solution)/shard_map/ppermute | solution.py:60
  34.0 2.1 %mamba_ssm.2 = (bf16[8,4096]{1,0:T(8,128)(2,1)S(1)}, bf16[8,4096]{1,0:T(8,128)(2,1)S(1)}, bf16[8,4096]{1,0:T(8,128)(2,1)S(1)}, bf16[8,4096]{1,0:T(8,128)(2,1)S(1)}, f32[32,16,512]{2,1,0:T(8,128)S(1)}) custom-call(s32[3]{0:T(128)S(1)} %pad_add_fusion.where.refs_0_, s32[32]{0:T(128)S(1)} %copy-done.11, bf16[32,288]{1,0:T(8,128)(2,1)S(1)} %add_convert_fusion.7.refs_2_, ...), custom_call_target="tpu_custom_call" | custom-call | flops 10000000000 | bytes 4194304 | tf_op jit(solution)/shard_map/mamba_ssm/pallas_call | solution.py:38
  41.8 2.7 %collective-permute-done.13 = bf16[8,4096]{1,0:T(8,128)(2,1)S(1)} collective-permute-done((bf16[8,4096]{1,0:T(8,128)(2,1)S(1)}, bf16[8,4096]{1,0:T(8,128)(2,1)S(1)}, u32[]{:S(2)}, u32[]{:S(2)}) %collective-permute-start.13) | collective-permute-done | bytes 65568 | tf_op jit(solution)/shard_map/ppermute | solution.py:60
  44.6 5.5 %collective-permute-done.14.far = bf16[8,4096]{1,0:T(8,128)(2,1)S(1)} collective-permute-done((bf16[8,4096]{1,0:T(8,128)(2,1)S(1)}, bf16[8,4096]{1,0:T(8,128)(2,1)S(1)}, u32[]{:S(2)}, u32[]{:S(2)}) %collective-permute-start.14) | collective-permute-done | bytes 65568 | tf_op jit(solution)/shard_map/ppermute | solution.py:60
  52.2 1.9 %collective-permute-start.17 = (bf16[8,4096]{1,0:T(8,128)(2,1)S(1)}, bf16[8,4096]{1,0:T(8,128)(2,1)S(1)}, u32[]{:S(2)}, u32[]{:S(2)}) collective-permute-start(bf16[8,4096]{1,0:T(8,128)(2,1)S(1)} %pad_maximum_fusion.refs_0_), channel_id=1, source_target_pairs={{0,2},{1,3},{2,0},{3,1},{4,6},{5,7},{6,4},{7,5},{8,10},{9,11},{10,... | collective-permute-start | bytes 196616 | tf_op jit(solution)/shard_map/ppermute | solution.py:60
  55.2 2.4 %collective-permute-done.18.refs_3_ = bf16[8,4096]{1,0:T(8,128)(2,1)S(1)} collective-permute-done((bf16[8,4096]{1,0:T(8,128)(2,1)S(1)}, bf16[8,4096]{1,0:T(8,128)(2,1)S(1)}, u32[]{:S(2)}, u32[]{:S(2)}) %collective-permute-start.18) | collective-permute-done | bytes 65568 | tf_op jit(solution)/shard_map/ppermute | solution.py:60
  58.4 5.7 %experts.2 = (bf16[8,4096]{1,0:T(8,128)(2,1)S(1)}, bf16[8,4096]{1,0:T(8,128)(2,1)S(1)}, bf16[8,4096]{1,0:T(8,128)(2,1)S(1)}, bf16[8,4096]{1,0:T(8,128)(2,1)S(1)}) custom-call(bf16[8,4096]{1,0:T(8,128)(2,1)S(1)} %pad_maximum_fusion.refs_0_, bf16[8,4096]{1,0:T(8,128)(2,1)S(1)} %collective-permute-done.16.refs_1_, ...), custom_call_target="tpu_custom_call" | custom-call | flops 10000000000 | bytes 22020096 | tf_op jit(solution)/shard_map/experts/pallas_call | solution.py:38
  65.3 2.3 %collective-permute-start.21 = (bf16[8,4096]{1,0:T(8,128)(2,1)S(1)}, bf16[8,4096]{1,0:T(8,128)(2,1)S(1)}, u32[]{:S(2)}, u32[]{:S(2)}) collective-permute-start(bf16[8,4096]{1,0:T(8,128)(2,1)S(1)} %get-tuple-element.92), channel_id=1, source_target_pairs={{0,3},{1,2},{2,1},{3,0},{4,7},{5,6},{6,5},{7,4},{8,11},{9,10},{10,... | collective-permute-start | bytes 196616 | tf_op jit(solution)/shard_map/ppermute | solution.py:60
  72.2 3.6 %collective-permute-done.22 = bf16[8,4096]{1,0:T(8,128)(2,1)S(1)} collective-permute-done((bf16[8,4096]{1,0:T(8,128)(2,1)S(1)}, bf16[8,4096]{1,0:T(8,128)(2,1)S(1)}, u32[]{:S(2)}, u32[]{:S(2)}) %collective-permute-start.22) | collective-permute-done | bytes 65568 | tf_op jit(solution)/shard_map/ppermute | solution.py:60
  78.2 2.3 %collective-permute-start.26 = (bf16[8,4096]{1,0:T(8,128)(2,1)S(1)}, bf16[8,4096]{1,0:T(8,128)(2,1)S(1)}, u32[]{:S(2)}, u32[]{:S(2)}) collective-permute-start(bf16[8,4096]{1,0:T(8,128)(2,1)S(1)} %get-tuple-element.94.refs_0_), channel_id=1, source_target_pairs={{0,3},{1,2},{2,1},{3,0},{4,7},{5,6},{6,5},{7,4},{8,11},{9,10},{10,... | collective-permute-start | bytes 196616 | tf_op jit(solution)/shard_map/ppermute | solution.py:60
  87.1 1.9 %collective-permute-start.28 = (bf16[32,288]{1,0:T(8,128)(2,1)S(1)}, bf16[32,288]{1,0:T(8,128)(2,1)S(1)}, u32[]{:S(2)}, u32[]{:S(2)}) collective-permute-start(bf16[32,288]{1,0:T(8,128)(2,1)S(1)} %get-tuple-element.98), channel_id=1, source_target_pairs={{0,2},{1,3},{2,0},{3,1},{4,6},{5,7},{6,4},{7,5},{8,10},{9,11},{10,... | collective-permute-start | bytes 55304 | tf_op jit(solution)/shard_map/ppermute | solution.py:60
  91.1 2.6 %collective-permute-done.29 = bf16[32,288]{1,0:T(8,128)(2,1)S(1)} collective-permute-done((bf16[32,288]{1,0:T(8,128)(2,1)S(1)}, bf16[32,288]{1,0:T(8,128)(2,1)S(1)}, u32[]{:S(2)}, u32[]{:S(2)}) %collective-permute-start.29) | collective-permute-done | bytes 18464 | tf_op jit(solution)/shard_map/ppermute | solution.py:60
  94.7 3.9 %collective-permute-done.30.refs_3_ = bf16[32,288]{1,0:T(8,128)(2,1)S(1)} collective-permute-done((bf16[32,288]{1,0:T(8,128)(2,1)S(1)}, bf16[32,288]{1,0:T(8,128)(2,1)S(1)}, u32[]{:S(2)}, u32[]{:S(2)}) %collective-permute-start.30) | collective-permute-done | bytes 18464 | tf_op jit(solution)/shard_map/ppermute | solution.py:60
  98.5 2.2 %mamba_ssm.3 = (bf16[8,4096]{1,0:T(8,128)(2,1)S(1)}, bf16[8,4096]{1,0:T(8,128)(2,1)S(1)}, bf16[8,4096]{1,0:T(8,128)(2,1)S(1)}, bf16[8,4096]{1,0:T(8,128)(2,1)S(1)}, f32[32,16,512]{2,1,0:T(8,128)}) custom-call(s32[3]{0:T(128)S(1)} %pad_add_fusion.where.refs_0_, s32[32]{0:T(128)S(1)} %copy-done.11, bf16[32,288]{1,0:T(8,128)(2,1)S(1)} %add_convert_fusion.6.refs_2_, ...), custom_call_target="tpu_custom_call" | custom-call | flops 10000000000 | bytes 4194304 | tf_op jit(solution)/shard_map/mamba_ssm/pallas_call | solution.py:38
  102.1 2.2 %collective-permute-start.33 = (bf16[8,4096]{1,0:T(8,128)(2,1)S(1)}, bf16[8,4096]{1,0:T(8,128)(2,1)S(1)}, u32[]{:S(2)}, u32[]{:S(2)}) collective-permute-start(bf16[8,4096]{1,0:T(8,128)(2,1)S(1)} %get-tuple-element.107), channel_id=1, source_target_pairs={{0,3},{1,2},{2,1},{3,0},{4,7},{5,6},{6,5},{7,4},{8,11},{9,10},{10,... | collective-permute-start | bytes 196616 | tf_op jit(solution)/shard_map/ppermute | solution.py:60
  106.0 1.9 %collective-permute-done.33 = bf16[8,4096]{1,0:T(8,128)(2,1)S(1)} collective-permute-done((bf16[8,4096]{1,0:T(8,128)(2,1)S(1)}, bf16[8,4096]{1,0:T(8,128)(2,1)S(1)}, u32[]{:S(2)}, u32[]{:S(2)}) %collective-permute-start.33) | collective-permute-done | bytes 65568 | tf_op jit(solution)/shard_map/ppermute | solution.py:60
  109.5 4.4 %collective-permute-done.34.far = bf16[8,4096]{1,0:T(8,128)(2,1)S(1)} collective-permute-done((bf16[8,4096]{1,0:T(8,128)(2,1)S(1)}, bf16[8,4096]{1,0:T(8,128)(2,1)S(1)}, u32[]{:S(2)}, u32[]{:S(2)}) %collective-permute-start.34) | collective-permute-done | bytes 65568 | tf_op jit(solution)/shard_map/ppermute | solution.py:60
  119.0 2.4 %collective-permute-done.38.refs_3_ = bf16[8,4096]{1,0:T(8,128)(2,1)S(1)} collective-permute-done((bf16[8,4096]{1,0:T(8,128)(2,1)S(1)}, bf16[8,4096]{1,0:T(8,128)(2,1)S(1)}, u32[]{:S(2)}, u32[]{:S(2)}) %collective-permute-start.38) | collective-permute-done | bytes 65568 | tf_op jit(solution)/shard_map/ppermute | solution.py:60
  122.2 5.7 %experts.3 = (bf16[8,4096]{1,0:T(8,128)(2,1)S(1)}, bf16[8,4096]{1,0:T(8,128)(2,1)S(1)}, bf16[8,4096]{1,0:T(8,128)(2,1)S(1)}, bf16[8,4096]{1,0:T(8,128)(2,1)S(1)}) custom-call(bf16[8,4096]{1,0:T(8,128)(2,1)S(1)} %pad_maximum_fusion.1.refs_0_, bf16[8,4096]{1,0:T(8,128)(2,1)S(1)} %collective-permute-done.36.refs_1_, ...), custom_call_target="tpu_custom_call" | custom-call | flops 10000000000 | bytes 22020096 | tf_op jit(solution)/shard_map/experts/pallas_call | solution.py:38
  129.4 2.0 %collective-permute-start.41 = (bf16[8,4096]{1,0:T(8,128)(2,1)S(1)}, bf16[8,4096]{1,0:T(8,128)(2,1)S(1)}, u32[]{:S(2)}, u32[]{:S(2)}) collective-permute-start(bf16[8,4096]{1,0:T(8,128)(2,1)S(1)} %get-tuple-element.115), channel_id=1, source_target_pairs={{0,3},{1,2},{2,1},{3,0},{4,7},{5,6},{6,5},{7,4},{8,11},{9,10},{10,... | collective-permute-start | bytes 196616 | tf_op jit(solution)/shard_map/ppermute | solution.py:60
  135.3 4.6 %collective-permute-done.42 = bf16[8,4096]{1,0:T(8,128)(2,1)S(1)} collective-permute-done((bf16[8,4096]{1,0:T(8,128)(2,1)S(1)}, bf16[8,4096]{1,0:T(8,128)(2,1)S(1)}, u32[]{:S(2)}, u32[]{:S(2)}) %collective-permute-start.42) | collective-permute-done | bytes 65568 | tf_op jit(solution)/shard_map/ppermute | solution.py:60
  (151 shorter events, 64.6 us)
Async XLA Ops:
  2.0 5.6 %collective-permute-start.4 = (f32[2,4,4]{1,2,0:T(4,128)S(1)}, f32[2,4,4]{1,2,0:T(4,128)S(1)}, u32[]{:S(2)}, u32[]{:S(2)}) collective-permute-start(f32[2,4,4]{1,2,0:T(4,128)S(1)} %pad_maximum_fusion.2), channel_id=1, source_target_pairs={{0,4},{1,5},{2,6},{3,7},{4,0},{5,1},{6,2},{7,3},{8,12},{9,13},{10,... | collective-permute-start | bytes 392 | tf_op jit(solution)/shard_map/ppermute | solution.py:60
  6.8 11.6 %collective-permute-start.6 = (f32[2,16,512]{2,1,0:T(8,128)}, f32[2,16,512]{2,1,0:T(8,128)S(1)}, u32[]{:S(2)}, u32[]{:S(2)}) collective-permute-start(f32[2,16,512]{2,1,0:T(8,128)} %param.21), channel_id=1, source_target_pairs={{0,8},{8,0},{1,9},{9,1},{2,10},{10,2},{3,11},{11,3},{4,12},{12,4},... | collective-permute-start | bytes 196616 | tf_op jit(solution)/shard_map/ppermute | solution.py:64
  7.3 6.8 %collective-permute-start = (bf16[2,4,4096]{2,1,0:T(4,128)(2,1)}, bf16[2,4,4096]{2,1,0:T(4,128)(2,1)S(1)}, u32[]{:S(2)}, u32[]{:S(2)}) collective-permute-start(bf16[2,4,4096]{2,1,0:T(4,128)(2,1)} %own.3), channel_id=1, source_target_pairs={{0,4},{1,5},{2,6},{3,7},{4,0},{5,1},{6,2},{7,3},{8,12},{9,13},{10,... | collective-permute-start | bytes 196616 | tf_op jit(solution)/shard_map/ppermute | solution.py:60
  14.8 5.2 %collective-permute-start.3 = (bf16[8,4096]{1,0:T(8,128)(2,1)S(1)}, bf16[8,4096]{1,0:T(8,128)(2,1)S(1)}, u32[]{:S(2)}, u32[]{:S(2)}) collective-permute-start(bf16[8,4096]{1,0:T(8,128)(2,1)S(1)} %get-tuple-element.67.refs_0_), channel_id=1, source_target_pairs={{0,3},{1,2},{2,1},{3,0},{4,7},{5,6},{6,5},{7,4},{8,11},{9,10},{10,... | collective-permute-start | bytes 196616 | tf_op jit(solution)/shard_map/ppermute | solution.py:60
  16.0 4.8 %collective-permute-start.2 = (bf16[8,4096]{1,0:T(8,128)(2,1)S(1)}, bf16[8,4096]{1,0:T(8,128)(2,1)S(1)}, u32[]{:S(2)}, u32[]{:S(2)}) collective-permute-start(bf16[8,4096]{1,0:T(8,128)(2,1)S(1)} %get-tuple-element.67.refs_0_), channel_id=1, source_target_pairs={{0,2},{1,3},{2,0},{3,1},{4,6},{5,7},{6,4},{7,5},{8,10},{9,11},{10,... | collective-permute-start | bytes 196616 | tf_op jit(solution)/shard_map/ppermute | solution.py:60
  24.0 5.0 %collective-permute-start.9 = (bf16[32,288]{1,0:T(8,128)(2,1)S(1)}, bf16[32,288]{1,0:T(8,128)(2,1)S(1)}, u32[]{:S(2)}, u32[]{:S(2)}) collective-permute-start(bf16[32,288]{1,0:T(8,128)(2,1)S(1)} %get-tuple-element.77), channel_id=1, source_target_pairs={{0,3},{1,2},{2,1},{3,0},{4,7},{5,6},{6,5},{7,4},{8,11},{9,10},{10,... | collective-permute-start | bytes 55304 | tf_op jit(solution)/shard_map/ppermute | solution.py:60
  29.1 4.8 %collective-permute-start.10 = (bf16[32,288]{1,0:T(8,128)(2,1)S(1)}, bf16[32,288]{1,0:T(8,128)(2,1)S(1)}, u32[]{:S(2)}, u32[]{:S(2)}) collective-permute-start(bf16[32,288]{1,0:T(8,128)(2,1)S(1)} %add_convert_fusion.7.refs_2_), channel_id=1, source_target_pairs={{0,4},{1,5},{2,6},{3,7},{4,0},{5,1},{6,2},{7,3},{8,12},{9,13},{10,... | collective-permute-start | bytes 55304 | tf_op jit(solution)/shard_map/ppermute | solution.py:60
  39.3 5.2 %collective-permute-start.13 = (bf16[8,4096]{1,0:T(8,128)(2,1)S(1)}, bf16[8,4096]{1,0:T(8,128)(2,1)S(1)}, u32[]{:S(2)}, u32[]{:S(2)}) collective-permute-start(bf16[8,4096]{1,0:T(8,128)(2,1)S(1)} %get-tuple-element.83), channel_id=1, source_target_pairs={{0,3},{1,2},{2,1},{3,0},{4,7},{5,6},{6,5},{7,4},{8,11},{9,10},{10,... | collective-permute-start | bytes 196616 | tf_op jit(solution)/shard_map/ppermute | solution.py:60
  44.5 5.6 %collective-permute-start.14 = (bf16[8,4096]{1,0:T(8,128)(2,1)S(1)}, bf16[8,4096]{1,0:T(8,128)(2,1)S(1)}, u32[]{:S(2)}, u32[]{:S(2)}) collective-permute-start(bf16[8,4096]{1,0:T(8,128)(2,1)S(1)} %add_convert_fusion.5.near), channel_id=1, source_target_pairs={{0,4},{1,5},{2,6},{3,7},{4,0},{5,1},{6,2},{7,3},{8,12},{9,13},{10,... | collective-permute-start | bytes 196616 | tf_op jit(solution)/shard_map/ppermute | solution.py:60
  51.7 5.9 %collective-permute-start.18 = (bf16[8,4096]{1,0:T(8,128)(2,1)S(1)}, bf16[8,4096]{1,0:T(8,128)(2,1)S(1)}, u32[]{:S(2)}, u32[]{:S(2)}) collective-permute-start(bf16[8,4096]{1,0:T(8,128)(2,1)S(1)} %pad_maximum_fusion.refs_0_), channel_id=1, source_target_pairs={{0,3},{1,2},{2,1},{3,0},{4,7},{5,6},{6,5},{7,4},{8,11},{9,10},{10,... | collective-permute-start | bytes 196616 | tf_op jit(solution)/shard_map/ppermute | solution.py:60
  52.2 5.4 %collective-permute-start.17 = (bf16[8,4096]{1,0:T(8,128)(2,1)S(1)}, bf16[8,4096]{1,0:T(8,128)(2,1)S(1)}, u32[]{:S(2)}, u32[]{:S(2)}) collective-permute-start(bf16[8,4096]{1,0:T(8,128)(2,1)S(1)} %pad_maximum_fusion.refs_0_), channel_id=1, source_target_pairs={{0,2},{1,3},{2,0},{3,1},{4,6},{5,7},{6,4},{7,5},{8,10},{9,11},{10,... | collective-permute-start | bytes 196616 | tf_op jit(solution)/shard_map/ppermute | solution.py:60
  64.1 5.0 %collective-permute-start.19 = (bf16[8,4096]{1,0:T(8,128)(2,1)S(1)}, bf16[8,4096]{1,0:T(8,128)(2,1)S(1)}, u32[]{:S(2)}, u32[]{:S(2)}) collective-permute-start(bf16[8,4096]{1,0:T(8,128)(2,1)S(1)} %get-tuple-element.90), channel_id=1, source_target_pairs={{0,1},{1,0},{2,3},{3,2},{4,5},{5,4},{6,7},{7,6},{8,9},{9,8},{10,11... | collective-permute-start | bytes 196616 | tf_op jit(solution)/shard_map/ppermute | solution.py:60
  65.3 5.3 %collective-permute-start.21 = (bf16[8,4096]{1,0:T(8,128)(2,1)S(1)}, bf16[8,4096]{1,0:T(8,128)(2,1)S(1)}, u32[]{:S(2)}, u32[]{:S(2)}) collective-permute-start(bf16[8,4096]{1,0:T(8,128)(2,1)S(1)} %get-tuple-element.92), channel_id=1, source_target_pairs={{0,3},{1,2},{2,1},{3,0},{4,7},{5,6},{6,5},{7,4},{8,11},{9,10},{10,... | collective-permute-start | bytes 196616 | tf_op jit(solution)/shard_map/ppermute | solution.py:60
  70.6 5.2 %collective-permute-start.22 = (bf16[8,4096]{1,0:T(8,128)(2,1)S(1)}, bf16[8,4096]{1,0:T(8,128)(2,1)S(1)}, u32[]{:S(2)}, u32[]{:S(2)}) collective-permute-start(bf16[8,4096]{1,0:T(8,128)(2,1)S(1)} %add_convert_fusion.4), channel_id=1, source_target_pairs={{0,4},{1,5},{2,6},{3,7},{4,0},{5,1},{6,2},{7,3},{8,12},{9,13},{10,... | collective-permute-start | bytes 196616 | tf_op jit(solution)/shard_map/ppermute | solution.py:60
  78.2 5.3 %collective-permute-start.26 = (bf16[8,4096]{1,0:T(8,128)(2,1)S(1)}, bf16[8,4096]{1,0:T(8,128)(2,1)S(1)}, u32[]{:S(2)}, u32[]{:S(2)}) collective-permute-start(bf16[8,4096]{1,0:T(8,128)(2,1)S(1)} %get-tuple-element.94.refs_0_), channel_id=1, source_target_pairs={{0,3},{1,2},{2,1},{3,0},{4,7},{5,6},{6,5},{7,4},{8,11},{9,10},{10,... | collective-permute-start | bytes 196616 | tf_op jit(solution)/shard_map/ppermute | solution.py:60
  89.0 4.7 %collective-permute-start.29 = (bf16[32,288]{1,0:T(8,128)(2,1)S(1)}, bf16[32,288]{1,0:T(8,128)(2,1)S(1)}, u32[]{:S(2)}, u32[]{:S(2)}) collective-permute-start(bf16[32,288]{1,0:T(8,128)(2,1)S(1)} %get-tuple-element.99), channel_id=1, source_target_pairs={{0,3},{1,2},{2,1},{3,0},{4,7},{5,6},{6,5},{7,4},{8,11},{9,10},{10,... | collective-permute-start | bytes 55304 | tf_op jit(solution)/shard_map/ppermute | solution.py:60
  93.8 4.8 %collective-permute-start.30 = (bf16[32,288]{1,0:T(8,128)(2,1)S(1)}, bf16[32,288]{1,0:T(8,128)(2,1)S(1)}, u32[]{:S(2)}, u32[]{:S(2)}) collective-permute-start(bf16[32,288]{1,0:T(8,128)(2,1)S(1)} %add_convert_fusion.6.refs_2_), channel_id=1, source_target_pairs={{0,4},{1,5},{2,6},{3,7},{4,0},{5,1},{6,2},{7,3},{8,12},{9,13},{10,... | collective-permute-start | bytes 55304 | tf_op jit(solution)/shard_map/ppermute | solution.py:60
  102.1 5.9 %collective-permute-start.33 = (bf16[8,4096]{1,0:T(8,128)(2,1)S(1)}, bf16[8,4096]{1,0:T(8,128)(2,1)S(1)}, u32[]{:S(2)}, u32[]{:S(2)}) collective-permute-start(bf16[8,4096]{1,0:T(8,128)(2,1)S(1)} %get-tuple-element.107), channel_id=1, source_target_pairs={{0,3},{1,2},{2,1},{3,0},{4,7},{5,6},{6,5},{7,4},{8,11},{9,10},{10,... | collective-permute-start | bytes 196616 | tf_op jit(solution)/shard_map/ppermute | solution.py:60
  108.0 5.9 %collective-permute-start.34 = (bf16[8,4096]{1,0:T(8,128)(2,1)S(1)}, bf16[8,4096]{1,0:T(8,128)(2,1)S(1)}, u32[]{:S(2)}, u32[]{:S(2)}) collective-permute-start(bf16[8,4096]{1,0:T(8,128)(2,1)S(1)} %add_convert_fusion.2.near), channel_id=1, source_target_pairs={{0,4},{1,5},{2,6},{3,7},{4,0},{5,1},{6,2},{7,3},{8,12},{9,13},{10,... | collective-permute-start | bytes 196616 | tf_op jit(solution)/shard_map/ppermute | solution.py:60
  115.5 5.9 %collective-permute-start.38 = (bf16[8,4096]{1,0:T(8,128)(2,1)S(1)}, bf16[8,4096]{1,0:T(8,128)(2,1)S(1)}, u32[]{:S(2)}, u32[]{:S(2)}) collective-permute-start(bf16[8,4096]{1,0:T(8,128)(2,1)S(1)} %pad_maximum_fusion.1.refs_0_), channel_id=1, source_target_pairs={{0,3},{1,2},{2,1},{3,0},{4,7},{5,6},{6,5},{7,4},{8,11},{9,10},{10,... | collective-permute-start | bytes 196616 | tf_op jit(solution)/shard_map/ppermute | solution.py:60
  116.5 5.0 %collective-permute-start.37 = (bf16[8,4096]{1,0:T(8,128)(2,1)S(1)}, bf16[8,4096]{1,0:T(8,128)(2,1)S(1)}, u32[]{:S(2)}, u32[]{:S(2)}) collective-permute-start(bf16[8,4096]{1,0:T(8,128)(2,1)S(1)} %pad_maximum_fusion.1.refs_0_), channel_id=1, source_target_pairs={{0,2},{1,3},{2,0},{3,1},{4,6},{5,7},{6,4},{7,5},{8,10},{9,11},{10,... | collective-permute-start | bytes 196616 | tf_op jit(solution)/shard_map/ppermute | solution.py:60
  127.9 5.0 %collective-permute-start.39 = (bf16[8,4096]{1,0:T(8,128)(2,1)S(1)}, bf16[8,4096]{1,0:T(8,128)(2,1)S(1)}, u32[]{:S(2)}, u32[]{:S(2)}) collective-permute-start(bf16[8,4096]{1,0:T(8,128)(2,1)S(1)} %get-tuple-element.113), channel_id=1, source_target_pairs={{0,1},{1,0},{2,3},{3,2},{4,5},{5,4},{6,7},{7,6},{8,9},{9,8},{10,11... | collective-permute-start | bytes 196616 | tf_op jit(solution)/shard_map/ppermute | solution.py:60
  129.4 5.2 %collective-permute-start.41 = (bf16[8,4096]{1,0:T(8,128)(2,1)S(1)}, bf16[8,4096]{1,0:T(8,128)(2,1)S(1)}, u32[]{:S(2)}, u32[]{:S(2)}) collective-permute-start(bf16[8,4096]{1,0:T(8,128)(2,1)S(1)} %get-tuple-element.115), channel_id=1, source_target_pairs={{0,3},{1,2},{2,1},{3,0},{4,7},{5,6},{6,5},{7,4},{8,11},{9,10},{10,... | collective-permute-start | bytes 196616 | tf_op jit(solution)/shard_map/ppermute | solution.py:60
  134.6 5.2 %collective-permute-start.42 = (bf16[8,4096]{1,0:T(8,128)(2,1)S(1)}, bf16[8,4096]{1,0:T(8,128)(2,1)S(1)}, u32[]{:S(2)}, u32[]{:S(2)}) collective-permute-start(bf16[8,4096]{1,0:T(8,128)(2,1)S(1)} %add_convert_fusion.1), channel_id=1, source_target_pairs={{0,4},{1,5},{2,6},{3,7},{4,0},{5,1},{6,2},{7,3},{8,12},{9,13},{10,... | collective-permute-start | bytes 196616 | tf_op jit(solution)/shard_map/ppermute | solution.py:60
  (41 other events, 288.4 us)

commit v3 on v2

--- a/solution.py
+++ b/solution.py
@@ -15,6 +15,7 @@
 BF16 = jnp.bfloat16
 VMEM = pl.BlockSpec(memory_space=pltpu.VMEM)
 SMEM = pl.BlockSpec(memory_space=pltpu.SMEM)
+ANY = pl.BlockSpec(memory_space=pl.ANY)
 
 
 def silu(values):
@@ -31,6 +32,10 @@
 
 def held(array):
     return pltpu.with_memory_space_constraint(array, pltpu.VMEM)
+
+
+def in_hbm(array):
+    return pltpu.with_memory_space_constraint(array, pltpu.HBM)
 
 
 def call(body, name, outs, specs, args, scratch=(), flops=0, moved=0, limit=8):
@@ -64,6 +69,11 @@
     return lax.ppermute(array, "dp", [(0, 1), (1, 0)])
 
 
+def across(array, distance, count):
+    pairs = [(i, count + (i ^ distance)) for i in range(count)]
+    return lax.ppermute(array, ("dp", "expert"), pairs + [(b, a) for a, b in pairs])
+
+
 def total(parts):
     result = parts[0].astype(F32)
     for part in parts[1:]:
@@ -79,27 +89,35 @@
     return parts
 
 
-def collect(parts, levels, count):
+def collect(parts, levels, count, beside=()):
     for position, (stride, size) in enumerate(levels):
         if position > 0:
             parts = jnp.split(parts, size, axis=0)
-        parts = total([parts[0]] + [partner(parts[k], k * stride, count) for k in range(1, size)])
-        parts = parts.astype(BF16)
-    return parts[0] if isinstance(parts, list) else parts
+        parts = [parts[0]] + [partner(parts[k], k * stride, count) for k in range(1, size)]
+        if position == 0 and beside:
+            parts[1], beside = lax.optimization_barrier((parts[1], beside))
+        parts = total(parts).astype(BF16)
+    return parts, beside
 
 
 def add_everywhere(parts, levels, count):
     for position, (stride, size) in enumerate(levels):
-        if position > 0:
+        if position == 0:
+            parts = [across(parts[k], k * stride, count) for k in range(size)]
+        else:
             rows, columns = parts.shape
             split = parts.reshape(stride, size, rows // (stride * size), columns)
             parts = [
                 jnp.stack([split[:, j ^ k] for j in range(size)], axis=1).reshape(rows, columns)
                 for k in range(size)
             ]
-        sent = [partner(parts[k], k * stride, count) for k in range(1, size)]
-        parts = total([parts[0]] + sent).astype(BF16)
-    return parts[0] if isinstance(parts, list) else parts
+            parts = [parts[0]] + [partner(parts[k], k * stride, count) for k in range(1, size)]
+        parts = total(parts).astype(BF16)
+    return parts
+
+
+def back_from_halves(array, stride, count):
+    return across(array, 0, count), across(array, stride, count)
 
 
 def joined(refs):
@@ -122,9 +140,22 @@
         scratch[rows : 2 * rows, :] = own
 
 
-def start_body(where, own, peer, gain, x_out, normed_out):
-    place_rows(x_out, own[0].astype(F32), peer[0].astype(F32), where[1])
-    normed_out[...] = normalize(x_out[...], gain[...]).astype(BF16)
+def start_body(where, own, peer, gain, x_out, normed_out, own_here, gain_here, arrived):
+    copies = [
+        pltpu.make_async_copy(own, own_here, arrived.at[0]),
+        pltpu.make_async_copy(gain, gain_here, arrived.at[1]),
+    ]
+    for copy in copies:
+        copy.start()
+    for copy in copies:
+        copy.wait()
+    place_rows(x_out, own_here[0].astype(F32), peer[0].astype(F32), where[1])
+    normed_out[...] = normalize(x_out[...], gain_here[...]).astype(BF16)
+
+
+def later_body(steps, where, own, peer, *outs):
+    for step in range(1, steps):
+        place_rows(outs[step - 1], own[step].astype(F32), peer[step].astype(F32), where[1])
 
 
 def table_body(steps, rows, where, own, peer, select_out, combine_out):
@@ -142,13 +173,15 @@
             for block in range(2):
                 count = jnp.int32(0)
                 for j in range(rows):
-                    at = (step * rows + j) * 4
+                    at = (step * rows + j) * 6
                     entry = [
-                        jnp.where(where[1] == block, own[at + m], peer[at + m]) for m in range(4)
+                        jnp.where(where[1] == block, own[at + m], peer[at + m]) for m in range(6)
                     ]
                     first = entry[0] == expert
                     second = entry[1] == expert
-                    weight = jnp.where(first, entry[2], 0.0) + jnp.where(second, entry[3], 0.0)
+                    weight = jnp.where(first, entry[2] + entry[4], 0.0) + jnp.where(
+                        second, entry[3] + entry[5], 0.0
+                    )
                     named = jnp.where(first | second, 1, 0)
                     row = block * rows + j
                     slot = jnp.where(named == 1, (far * 2 + block) * CAP + count, -1)
@@ -217,7 +250,8 @@
     outs, (after, y) = refs[12 : 12 + parts], refs[12 + parts :]
     rank = dt_proj.shape[0]
     states = a_log.shape[0]
-    projected = near[...].astype(F32) + far[...].astype(F32)
+    width = rank + 2 * states
+    projected = near[:, :width].astype(F32) + far[:, :width].astype(F32)
     step_in = projected[:, :rank]
     high = step_in.astype(BF16)
     low = (step_in - high.astype(F32)).astype(BF16)
@@ -297,11 +331,10 @@
         out[...] = values[rows:].astype(BF16)
 
 
-def next_body(step, where, h_in, near, far, combine, own, peer, gain, out, x_out, normed_out):
+def next_body(where, h_in, near, far, combine, added, gain, out, x_out, normed_out):
     values = combined(h_in, near, far, combine)
     store_own(out, out.shape[0], values, where[1])
-    place_rows(x_out, own[step + 1].astype(F32), peer[step + 1].astype(F32), where[1])
-    x = values + x_out[...]
+    x = values + added[...]
     x_out[...] = x
     normed_out[...] = normalize(x, gain[...]).astype(BF16)
 
@@ -350,8 +383,33 @@
     where = jnp.stack([me, me // stride, core]).astype(jnp.int32)
 
     peer_input = partner(layer_input, stride, count)
-    routes = jnp.concatenate([route_ids.astype(F32), route_weights], axis=2)
-    peer_routes = partner(routes, stride, count)
+    x, normed = call(
+        start_body,
+        "first_norm",
+        [((2 * rows, width), F32), ((2 * rows, width), BF16)],
+        [SMEM, ANY, VMEM, ANY],
+        (where, in_hbm(layer_input), peer_input, in_hbm(mamba_gain.reshape(1, width))),
+        scratch=[
+            pltpu.VMEM(layer_input.shape, BF16),
+            pltpu.VMEM((1, width), F32),
+            pltpu.SemaphoreType.DMA((2,)),
+        ],
+    )
+    mamba_gain = held(mamba_gain.reshape(1, width))
+    moe_gain = held(moe_gain.reshape(1, width))
+    normed, layer_input, prompt_ssm, prompt_conv, route_ids, route_weights = (
+        lax.optimization_barrier(
+            (normed, layer_input, prompt_ssm, prompt_conv, route_ids, route_weights)
+        )
+    )
+    rows_in = spread(normed, levels, count)
+    high = lax.reduce_precision(route_weights, 8, 7)
+    routes = jnp.concatenate(
+        [route_ids.astype(BF16), high.astype(BF16), (route_weights - high).astype(BF16)], axis=2
+    ).reshape(-1)
+    extra = -(-routes.size // group_rows)
+    routes = other_core(routes)
+    routes = jnp.pad(routes, (0, extra * group_rows - routes.size)).reshape(group_rows, extra)
     peer_ssm = other_core(prompt_ssm)
     peer_conv = other_core(prompt_conv)
     all_ssm = jnp.where(
@@ -364,28 +422,14 @@
         jnp.concatenate([prompt_conv, peer_conv]),
         jnp.concatenate([peer_conv, prompt_conv]),
     )
-    mamba_gain = mamba_gain.reshape(1, width)
-    moe_gain = moe_gain.reshape(1, width)
-    conv_bias = conv_bias.reshape(1, channels)
-    dt_bias = dt_bias.reshape(1, channels)
-    d_skip = d_skip.reshape(1, channels)
+    conv_weight = held(conv_weight)
+    conv_bias = held(conv_bias.reshape(1, channels))
+    dt_bias = held(dt_bias.reshape(1, channels))
+    d_skip = held(d_skip.reshape(1, channels))
+    a_log = held(a_log)
     gate, up, down = w_gate[0], w_up[0], w_down[0]
     place = (rows, levels, stride)
 
-    x, normed = call(
-        start_body,
-        "first_norm",
-        [((2 * rows, width), F32), ((2 * rows, width), BF16)],
-        [SMEM, VMEM, VMEM, VMEM],
-        (where, layer_input, peer_input, mamba_gain),
-    )
-    select, combine = call(
-        functools.partial(table_body, steps, rows),
-        "route_tables",
-        [((steps, slots, 2 * rows), F32), ((steps, 2 * rows, slots), F32)],
-        [SMEM, SMEM, SMEM],
-        (where, routes.reshape(-1), peer_routes.reshape(-1)),
-    )
     window = call(
         functools.partial(first_taps_body, *place),
         "first_taps",
@@ -397,10 +441,9 @@
     outputs = []
     for step in range(steps):
         last = step == steps - 1
-        rows_in = spread(normed, levels, count)
         if step == 0:
-            rows_in, select, combine, window, state = lax.optimization_barrier(
-                (rows_in, select, combine, window, state)
+            rows_in, routes, window, state = lax.optimization_barrier(
+                (rows_in, routes, window, state)
             )
         x_part, act, *proj = call(
             functools.partial(x_body, parts, taps),
@@ -417,7 +460,9 @@
         )
         window = [*window[1:], x_part]
         proj = add_everywhere(proj, levels, count)
-        proj_far = partner(proj, stride, count)
+        if step == 0:
+            proj = jnp.concatenate([proj, routes], axis=1)
+        proj, proj_far = back_from_halves(proj, stride, count)
         z_gate = call(
             functools.partial(z_body, parts),
             "mamba_z",
@@ -460,7 +505,28 @@
             flops=2 * group_rows * width * channels,
             moved=2 * width * channels,
         )
-        mixed_near = collect(mixed, levels, count)
+        beside = (proj, proj_far, layer_input, peer_input) if step == 0 else ()
+        mixed_near, beside = collect(mixed, levels, count, beside)
+        if step == 0:
+            near_routes, far_routes, later_own, later_peer = beside
+            select, combine = call(
+                functools.partial(table_body, steps, rows),
+                "route_tables",
+                [((steps, slots, 2 * rows), F32), ((steps, 2 * rows, slots), F32)],
+                [SMEM, SMEM, SMEM],
+                (
+                    where,
+                    near_routes[:, x_proj.shape[0] :].astype(F32).reshape(-1),
+                    far_routes[:, x_proj.shape[0] :].astype(F32).reshape(-1),
+                ),
+            )
+            later = call(
+                functools.partial(later_body, steps),
+                "later_inputs",
+                [((2 * rows, width), F32)] * (steps - 1),
+                [SMEM, VMEM, VMEM],
+                (where, later_own, later_peer),
+            )
         mixed_far = partner(mixed_near, stride, count)
         h, own, other = call(
             route_body,
@@ -484,7 +550,7 @@
             flops=6 * total_slots * width * gate.shape[0],
             moved=6 * width * gate.shape[0],
         )
-        out_near = collect(returned, levels, count)
+        out_near, _ = collect(returned, levels, count)
         summed = total([out_near, partner(out_near, stride, count)]).astype(BF16)
         out_far = other_core(summed[slots // 2 :])
         if last:
@@ -497,17 +563,18 @@
             )[0]
         else:
             out, x, normed = call(
-                functools.partial(next_body, step),
+                next_body,
                 "next_norm",
                 [
                     ((rows, width), BF16),
                     ((2 * rows, width), F32),
                     ((2 * rows, width), BF16),
                 ],
-                [SMEM] + [VMEM] * 7,
-                (where, h, summed, out_far, combine[step], layer_input, peer_input, mamba_gain),
+                [SMEM] + [VMEM] * 6,
+                (where, h, summed, out_far, combine[step], later[step], mamba_gain),
             )
             outputs.append(out)
+            rows_in = spread(normed, levels, count)
     return (layer_output, state, conv_state)
 
 

time: 143 us -> 137 us (0.958)
  waiting for transfers between devices: 67.5 us -> 50.9 us
  starting transfers between devices: 45.2 us -> 56.5 us
    ppermute x38 -> x29, waiting for transfers between devices: 63.5 us -> 39.7 us  [partner(): lax.ppermute(array, 'expert', [(i, i ^ distance) for i in range(count)])]
    ppermute x0 -> x12, starting transfers between devices: none -> 12.3 us  [across(): lax.ppermute(array, ('dp', 'expert'), pairs + [(b, a) for a, b in pairs])]
    ppermute x0 -> x12, waiting for transfers between devices: none -> 6.51 us  [across(): lax.ppermute(array, ('dp', 'expert'), pairs + [(b, a) for a, b in pairs])]
    pallas_call x16 -> x17, Pallas kernels: 24.9 us -> 26.3 us  [call(): pl.pallas_call(body, name=name, out_shape=[jax.ShapeDtypeStruct(s, d) for...]
    ppermute x38 -> x29, starting transfers between devices: 44.4 us -> 43 us  [partner(): lax.ppermute(array, 'expert', [(i, i ^ distance) for i in range(count)])]
    ppermute x6 -> x7, waiting for transfers between devices: 4.03 us -> 4.65 us  [other_core(): return lax.ppermute(array, 'dp', [(0, 1), (1, 0)])]
  transfers between devices with their start and end apart: 44 -> 48, of which waited for: 40 -> 40; matrix products, arithmetic and copies ran while one was open for 1% -> 1% of each run, Pallas kernels for 3% -> 3%
where the time goes in v3:
time: 137 us
  starting transfers between devices  56.5 us (41%)
  waiting for transfers between devices  50.9 us (37%)
  Pallas kernels  26.3 us (19%)
  local copies, waits for them, and re-layouts  1.84 us (1%)
    ppermute x29, starting transfers between devices, partner(): lax.ppermute(array, 'expert', [(i, i ^ distance) for i in range(count)])  43 us
    ppermute x29, waiting for transfers between devices, partner(): lax.ppermute(array, 'expert', [(i, i ^ distance) for i in range(count)])  39.7 us
    pallas_call x17, Pallas kernels, call(): pl.pallas_call(body, name=name, out_shape=[jax.ShapeDtypeStruct(s, d) for...  26.3 us
    ppermute x12, starting transfers between devices, across(): lax.ppermute(array, ('dp', 'expert'), pairs + [(b, a) for a, b in pairs])  12.3 us
    ppermute x12, waiting for transfers between devices, across(): lax.ppermute(array, ('dp', 'expert'), pairs + [(b, a) for a, b in pairs])  6.51 us
    ppermute x7, waiting for transfers between devices, other_core(): return lax.ppermute(array, 'dp', [(0, 1), (1, 0)])  4.65 us
  transfers between devices with their start and end apart: 48, of which 40 were waited for; matrix products, arithmetic and copies ran while one was open for 1% of the time, Pallas kernels for 3%

profile of v3, /device:TPU:0, one launch (start us, length us, event | category | flops | bytes accessed | tf_op | source)
XLA Modules:
  0.0 137.3 jit_solution(13902355031087576511)
XLA Ops:
  0.6 4.1 %collective-permute-start = (bf16[2,4,4096]{2,1,0:T(4,128)(2,1)}, bf16[2,4,4096]{2,1,0:T(4,128)(2,1)S(1)}, u32[]{:S(2)}, u32[]{:S(2)}) collective-permute-start(bf16[2,4,4096]{2,1,0:T(4,128)(2,1)} %own.2), channel_id=1, source_target_pairs={{0,4},{1,5},{2,6},{3,7},{4,0},{5,1},{6,2},{7,3},{8,12},{9,13},{10,... | collective-permute-start | bytes 196616 | tf_op jit(solution)/shard_map/ppermute | solution.py:65
  4.8 3.8 %collective-permute-done.peer = bf16[2,4,4096]{2,1,0:T(4,128)(2,1)S(1)} collective-permute-done((bf16[2,4,4096]{2,1,0:T(4,128)(2,1)}, bf16[2,4,4096]{2,1,0:T(4,128)(2,1)S(1)}, u32[]{:S(2)}, u32[]{:S(2)}) %collective-permute-start) | collective-permute-done | bytes 65568 | tf_op jit(solution)/shard_map/ppermute | solution.py:65
  16.4 2.2 %collective-permute-done.1.refs_1_ = bf16[8,4096]{1,0:T(8,128)(2,1)S(1)} collective-permute-done((bf16[8,4096]{1,0:T(8,128)(2,1)S(1)}, bf16[8,4096]{1,0:T(8,128)(2,1)S(1)}, u32[]{:S(2)}, u32[]{:S(2)}) %collective-permute-start.1) | collective-permute-done | bytes 65568 | tf_op jit(solution)/shard_map/ppermute | solution.py:65
  25.9 3.1 %collective-permute-start.12 = (bf16[32,290]{1,0:T(8,128)(2,1)S(1)}, bf16[32,290]{1,0:T(8,128)(2,1)S(1)}, u32[]{:S(2)}, u32[]{:S(2)}) collective-permute-start(bf16[32,290]{1,0:T(8,128)(2,1)S(1)} %pad_maximum_fusion.2), channel_id=1, source_target_pairs={{0,12},{1,13},{2,14},{3,15},{4,8},{5,9},{6,10},{7,11},{12,0},{13,1... | collective-permute-start | bytes 55688 | tf_op jit(solution)/shard_map/ppermute | solution.py:74
  30.5 2.1 %mamba_ssm.2 = (bf16[8,4096]{1,0:T(8,128)(2,1)S(1)}, bf16[8,4096]{1,0:T(8,128)(2,1)S(1)}, bf16[8,4096]{1,0:T(8,128)(2,1)S(1)}, bf16[8,4096]{1,0:T(8,128)(2,1)S(1)}, f32[32,16,512]{2,1,0:T(8,128)S(1)}) custom-call(s32[3]{0:T(128)S(1)} %pad_add_fusion.where.refs_0_, s32[32]{0:T(128)S(1)} %copy-done.13, bf16[32,290]{1,0:T(8,128)(2,1)S(1)} %collective-permute-done.11.refs_2_, ...), custom_call_target="tpu_custom_call" | custom-call | flops 10000000000 | bytes 4194304 | tf_op jit(solution)/shard_map/mamba_ssm/pallas_call | solution.py:43
  38.3 1.9 %collective-permute-done.15 = bf16[8,4096]{1,0:T(8,128)(2,1)S(1)} collective-permute-done((bf16[8,4096]{1,0:T(8,128)(2,1)S(1)}, bf16[8,4096]{1,0:T(8,128)(2,1)S(1)}, u32[]{:S(2)}, u32[]{:S(2)}) %collective-permute-start.15) | collective-permute-done | bytes 65568 | tf_op jit(solution)/shard_map/ppermute | solution.py:65
  40.2 2.2 %collective-permute-start.16 = (bf16[8,4096]{1,0:T(8,128)(2,1)S(1)}, bf16[8,4096]{1,0:T(8,128)(2,1)S(1)}, u32[]{:S(2)}, u32[]{:S(2)}) collective-permute-start(bf16[8,4096]{1,0:T(8,128)(2,1)S(1)} %add_convert_fusion.5.near), channel_id=1, source_target_pairs={{0,4},{1,5},{2,6},{3,7},{4,0},{5,1},{6,2},{7,3},{8,12},{9,13},{10,... | collective-permute-start | bytes 196616 | tf_op jit(solution)/shard_map/ppermute | solution.py:65
  43.2 3.0 %collective-permute-done.16.far = bf16[8,4096]{1,0:T(8,128)(2,1)S(1)} collective-permute-done((bf16[8,4096]{1,0:T(8,128)(2,1)S(1)}, bf16[8,4096]{1,0:T(8,128)(2,1)S(1)}, u32[]{:S(2)}, u32[]{:S(2)}) %collective-permute-start.16) | collective-permute-done | bytes 65568 | tf_op jit(solution)/shard_map/ppermute | solution.py:65
  51.3 2.4 %collective-permute-done.20.refs_3_ = bf16[8,4096]{1,0:T(8,128)(2,1)S(1)} collective-permute-done((bf16[8,4096]{1,0:T(8,128)(2,1)S(1)}, bf16[8,4096]{1,0:T(8,128)(2,1)S(1)}, u32[]{:S(2)}, u32[]{:S(2)}) %collective-permute-start.20) | collective-permute-done | bytes 65568 | tf_op jit(solution)/shard_map/ppermute | solution.py:65
  54.6 5.7 %experts.2 = (bf16[8,4096]{1,0:T(8,128)(2,1)S(1)}, bf16[8,4096]{1,0:T(8,128)(2,1)S(1)}, bf16[8,4096]{1,0:T(8,128)(2,1)S(1)}, bf16[8,4096]{1,0:T(8,128)(2,1)S(1)}) custom-call(bf16[8,4096]{1,0:T(8,128)(2,1)S(1)} %pad_maximum_fusion.refs_0_, bf16[8,4096]{1,0:T(8,128)(2,1)S(1)} %collective-permute-done.18.refs_1_, ...), custom_call_target="tpu_custom_call" | custom-call | flops 10000000000 | bytes 22020096 | tf_op jit(solution)/shard_map/experts/pallas_call | solution.py:43
  61.7 2.1 %collective-permute-start.23 = (bf16[8,4096]{1,0:T(8,128)(2,1)S(1)}, bf16[8,4096]{1,0:T(8,128)(2,1)S(1)}, u32[]{:S(2)}, u32[]{:S(2)}) collective-permute-start(bf16[8,4096]{1,0:T(8,128)(2,1)S(1)} %get-tuple-element.110), channel_id=1, source_target_pairs={{0,3},{1,2},{2,1},{3,0},{4,7},{5,6},{6,5},{7,4},{8,11},{9,10},{10,... | collective-permute-start | bytes 196616 | tf_op jit(solution)/shard_map/ppermute | solution.py:65
  66.9 3.1 %collective-permute-start.24 = (bf16[8,4096]{1,0:T(8,128)(2,1)S(1)}, bf16[8,4096]{1,0:T(8,128)(2,1)S(1)}, u32[]{:S(2)}, u32[]{:S(2)}) collective-permute-start(bf16[8,4096]{1,0:T(8,128)(2,1)S(1)} %add_convert_fusion.4), channel_id=1, source_target_pairs={{0,4},{1,5},{2,6},{3,7},{4,0},{5,1},{6,2},{7,3},{8,12},{9,13},{10,... | collective-permute-start | bytes 196616 | tf_op jit(solution)/shard_map/ppermute | solution.py:65
  74.6 2.0 %collective-permute-start.28 = (bf16[8,4096]{1,0:T(8,128)(2,1)S(1)}, bf16[8,4096]{1,0:T(8,128)(2,1)S(1)}, u32[]{:S(2)}, u32[]{:S(2)}) collective-permute-start(bf16[8,4096]{1,0:T(8,128)(2,1)S(1)} %get-tuple-element.114.refs_0_), channel_id=1, source_target_pairs={{0,3},{1,2},{2,1},{3,0},{4,7},{5,6},{6,5},{7,4},{8,11},{9,10},{10,... | collective-permute-start | bytes 196616 | tf_op jit(solution)/shard_map/ppermute | solution.py:65
  78.2 1.9 %collective-permute-done.28.refs_3_ = bf16[8,4096]{1,0:T(8,128)(2,1)S(1)} collective-permute-done((bf16[8,4096]{1,0:T(8,128)(2,1)S(1)}, bf16[8,4096]{1,0:T(8,128)(2,1)S(1)}, u32[]{:S(2)}, u32[]{:S(2)}) %collective-permute-start.28) | collective-permute-done | bytes 65568 | tf_op jit(solution)/shard_map/ppermute | solution.py:65
  86.9 2.1 %collective-permute-done.32 = bf16[32,288]{1,0:T(8,128)(2,1)S(1)} collective-permute-done((bf16[32,288]{1,0:T(8,128)(2,1)S(1)}, bf16[32,288]{1,0:T(8,128)(2,1)S(1)}, u32[]{:S(2)}, u32[]{:S(2)}) %collective-permute-start.32) | collective-permute-done | bytes 18464 | tf_op jit(solution)/shard_map/ppermute | solution.py:74
  89.1 1.8 %collective-permute-start.34 = (bf16[32,288]{1,0:T(8,128)(2,1)S(1)}, bf16[32,288]{1,0:T(8,128)(2,1)S(1)}, u32[]{:S(2)}, u32[]{:S(2)}) collective-permute-start(bf16[32,288]{1,0:T(8,128)(2,1)S(1)} %add_convert_fusion.6), channel_id=1, source_target_pairs={{0,12},{1,13},{2,14},{3,15},{4,8},{5,9},{6,10},{7,11},{12,0},{13,1... | collective-permute-start | bytes 55304 | tf_op jit(solution)/shard_map/ppermute | solution.py:74
  93.3 2.2 %mamba_ssm.3 = (bf16[8,4096]{1,0:T(8,128)(2,1)S(1)}, bf16[8,4096]{1,0:T(8,128)(2,1)S(1)}, bf16[8,4096]{1,0:T(8,128)(2,1)S(1)}, bf16[8,4096]{1,0:T(8,128)(2,1)S(1)}, f32[32,16,512]{2,1,0:T(8,128)}) custom-call(s32[3]{0:T(128)S(1)} %pad_add_fusion.where.refs_0_, s32[32]{0:T(128)S(1)} %copy-done.13, bf16[32,288]{1,0:T(8,128)(2,1)S(1)} %collective-permute-done.33.refs_2_, ...), custom_call_target="tpu_custom_call" | custom-call | flops 10000000000 | bytes 4194304 | tf_op jit(solution)/shard_map/mamba_ssm/pallas_call | solution.py:43
  102.8 2.8 %collective-permute-start.38 = (bf16[8,4096]{1,0:T(8,128)(2,1)S(1)}, bf16[8,4096]{1,0:T(8,128)(2,1)S(1)}, u32[]{:S(2)}, u32[]{:S(2)}) collective-permute-start(bf16[8,4096]{1,0:T(8,128)(2,1)S(1)} %add_convert_fusion.2.near), channel_id=1, source_target_pairs={{0,4},{1,5},{2,6},{3,7},{4,0},{5,1},{6,2},{7,3},{8,12},{9,13},{10,... | collective-permute-start | bytes 196616 | tf_op jit(solution)/shard_map/ppermute | solution.py:65
  105.6 3.1 %collective-permute-done.38.far = bf16[8,4096]{1,0:T(8,128)(2,1)S(1)} collective-permute-done((bf16[8,4096]{1,0:T(8,128)(2,1)S(1)}, bf16[8,4096]{1,0:T(8,128)(2,1)S(1)}, u32[]{:S(2)}, u32[]{:S(2)}) %collective-permute-start.38) | collective-permute-done | bytes 65568 | tf_op jit(solution)/shard_map/ppermute | solution.py:65
  113.9 2.4 %collective-permute-done.42.refs_3_ = bf16[8,4096]{1,0:T(8,128)(2,1)S(1)} collective-permute-done((bf16[8,4096]{1,0:T(8,128)(2,1)S(1)}, bf16[8,4096]{1,0:T(8,128)(2,1)S(1)}, u32[]{:S(2)}, u32[]{:S(2)}) %collective-permute-start.42) | collective-permute-done | bytes 65568 | tf_op jit(solution)/shard_map/ppermute | solution.py:65
  117.2 5.6 %experts.3 = (bf16[8,4096]{1,0:T(8,128)(2,1)S(1)}, bf16[8,4096]{1,0:T(8,128)(2,1)S(1)}, bf16[8,4096]{1,0:T(8,128)(2,1)S(1)}, bf16[8,4096]{1,0:T(8,128)(2,1)S(1)}) custom-call(bf16[8,4096]{1,0:T(8,128)(2,1)S(1)} %pad_maximum_fusion.1.refs_0_, bf16[8,4096]{1,0:T(8,128)(2,1)S(1)} %collective-permute-done.40.refs_1_, ...), custom_call_target="tpu_custom_call" | custom-call | flops 10000000000 | bytes 22020096 | tf_op jit(solution)/shard_map/experts/pallas_call | solution.py:43
  124.2 2.2 %collective-permute-start.45 = (bf16[8,4096]{1,0:T(8,128)(2,1)S(1)}, bf16[8,4096]{1,0:T(8,128)(2,1)S(1)}, u32[]{:S(2)}, u32[]{:S(2)}) collective-permute-start(bf16[8,4096]{1,0:T(8,128)(2,1)S(1)} %get-tuple-element.135), channel_id=1, source_target_pairs={{0,3},{1,2},{2,1},{3,0},{4,7},{5,6},{6,5},{7,4},{8,11},{9,10},{10,... | collective-permute-start | bytes 196616 | tf_op jit(solution)/shard_map/ppermute | solution.py:65
  129.4 2.4 %collective-permute-start.46 = (bf16[8,4096]{1,0:T(8,128)(2,1)S(1)}, bf16[8,4096]{1,0:T(8,128)(2,1)S(1)}, u32[]{:S(2)}, u32[]{:S(2)}) collective-permute-start(bf16[8,4096]{1,0:T(8,128)(2,1)S(1)} %add_convert_fusion.1), channel_id=1, source_target_pairs={{0,4},{1,5},{2,6},{3,7},{4,0},{5,1},{6,2},{7,3},{8,12},{9,13},{10,... | collective-permute-start | bytes 196616 | tf_op jit(solution)/shard_map/ppermute | solution.py:65
  131.8 2.8 %collective-permute-done.46 = bf16[8,4096]{1,0:T(8,128)(2,1)S(1)} collective-permute-done((bf16[8,4096]{1,0:T(8,128)(2,1)S(1)}, bf16[8,4096]{1,0:T(8,128)(2,1)S(1)}, u32[]{:S(2)}, u32[]{:S(2)}) %collective-permute-start.46) | collective-permute-done | bytes 65568 | tf_op jit(solution)/shard_map/ppermute | solution.py:65
  (175 shorter events, 69.0 us)
Async XLA Ops:
  0.6 8.0 %collective-permute-start = (bf16[2,4,4096]{2,1,0:T(4,128)(2,1)}, bf16[2,4,4096]{2,1,0:T(4,128)(2,1)S(1)}, u32[]{:S(2)}, u32[]{:S(2)}) collective-permute-start(bf16[2,4,4096]{2,1,0:T(4,128)(2,1)} %own.2), channel_id=1, source_target_pairs={{0,4},{1,5},{2,6},{3,7},{4,0},{5,1},{6,2},{7,3},{8,12},{9,13},{10,... | collective-permute-start | bytes 196616 | tf_op jit(solution)/shard_map/ppermute | solution.py:65
  10.2 6.2 %collective-permute-start.3 = (bf16[8,4096]{1,0:T(8,128)(2,1)S(1)}, bf16[8,4096]{1,0:T(8,128)(2,1)S(1)}, u32[]{:S(2)}, u32[]{:S(2)}) collective-permute-start(bf16[8,4096]{1,0:T(8,128)(2,1)S(1)} %get-tuple-element.80.refs_0_), channel_id=1, source_target_pairs={{0,3},{1,2},{2,1},{3,0},{4,7},{5,6},{6,5},{7,4},{8,11},{9,10},{10,... | collective-permute-start | bytes 196616 | tf_op jit(solution)/shard_map/ppermute | solution.py:65
  11.9 4.5 %collective-permute-start.2 = (bf16[8,4096]{1,0:T(8,128)(2,1)S(1)}, bf16[8,4096]{1,0:T(8,128)(2,1)S(1)}, u32[]{:S(2)}, u32[]{:S(2)}) collective-permute-start(bf16[8,4096]{1,0:T(8,128)(2,1)S(1)} %get-tuple-element.80.refs_0_), channel_id=1, source_target_pairs={{0,2},{1,3},{2,0},{3,1},{4,6},{5,7},{6,4},{7,5},{8,10},{9,11},{10,... | collective-permute-start | bytes 196616 | tf_op jit(solution)/shard_map/ppermute | solution.py:65
  25.9 4.6 %collective-permute-start.12 = (bf16[32,290]{1,0:T(8,128)(2,1)S(1)}, bf16[32,290]{1,0:T(8,128)(2,1)S(1)}, u32[]{:S(2)}, u32[]{:S(2)}) collective-permute-start(bf16[32,290]{1,0:T(8,128)(2,1)S(1)} %pad_maximum_fusion.2), channel_id=1, source_target_pairs={{0,12},{1,13},{2,14},{3,15},{4,8},{5,9},{6,10},{7,11},{12,0},{13,1... | collective-permute-start | bytes 55688 | tf_op jit(solution)/shard_map/ppermute | solution.py:74
  32.6 5.0 %collective-permute-start.13 = (bf16[8,4096]{1,0:T(8,128)(2,1)S(1)}, bf16[8,4096]{1,0:T(8,128)(2,1)S(1)}, u32[]{:S(2)}, u32[]{:S(2)}) collective-permute-start(bf16[8,4096]{1,0:T(8,128)(2,1)S(1)} %get-tuple-element.95), channel_id=1, source_target_pairs={{0,1},{1,0},{2,3},{3,2},{4,5},{5,4},{6,7},{7,6},{8,9},{9,8},{10,11... | collective-permute-start | bytes 196616 | tf_op jit(solution)/shard_map/ppermute | solution.py:65
  33.6 4.6 %collective-permute-start.14 = (bf16[8,4096]{1,0:T(8,128)(2,1)S(1)}, bf16[8,4096]{1,0:T(8,128)(2,1)S(1)}, u32[]{:S(2)}, u32[]{:S(2)}) collective-permute-start(bf16[8,4096]{1,0:T(8,128)(2,1)S(1)} %get-tuple-element.98), channel_id=1, source_target_pairs={{0,2},{1,3},{2,0},{3,1},{4,6},{5,7},{6,4},{7,5},{8,10},{9,11},{10,... | collective-permute-start | bytes 196616 | tf_op jit(solution)/shard_map/ppermute | solution.py:65
  34.7 5.4 %collective-permute-start.15 = (bf16[8,4096]{1,0:T(8,128)(2,1)S(1)}, bf16[8,4096]{1,0:T(8,128)(2,1)S(1)}, u32[]{:S(2)}, u32[]{:S(2)}) collective-permute-start(bf16[8,4096]{1,0:T(8,128)(2,1)S(1)} %get-tuple-element.99), channel_id=1, source_target_pairs={{0,3},{1,2},{2,1},{3,0},{4,7},{5,6},{6,5},{7,4},{8,11},{9,10},{10,... | collective-permute-start | bytes 196616 | tf_op jit(solution)/shard_map/ppermute | solution.py:65
  40.2 6.0 %collective-permute-start.16 = (bf16[8,4096]{1,0:T(8,128)(2,1)S(1)}, bf16[8,4096]{1,0:T(8,128)(2,1)S(1)}, u32[]{:S(2)}, u32[]{:S(2)}) collective-permute-start(bf16[8,4096]{1,0:T(8,128)(2,1)S(1)} %add_convert_fusion.5.near), channel_id=1, source_target_pairs={{0,4},{1,5},{2,6},{3,7},{4,0},{5,1},{6,2},{7,3},{8,12},{9,13},{10,... | collective-permute-start | bytes 196616 | tf_op jit(solution)/shard_map/ppermute | solution.py:65
  47.8 5.9 %collective-permute-start.20 = (bf16[8,4096]{1,0:T(8,128)(2,1)S(1)}, bf16[8,4096]{1,0:T(8,128)(2,1)S(1)}, u32[]{:S(2)}, u32[]{:S(2)}) collective-permute-start(bf16[8,4096]{1,0:T(8,128)(2,1)S(1)} %pad_maximum_fusion.refs_0_), channel_id=1, source_target_pairs={{0,3},{1,2},{2,1},{3,0},{4,7},{5,6},{6,5},{7,4},{8,11},{9,10},{10,... | collective-permute-start | bytes 196616 | tf_op jit(solution)/shard_map/ppermute | solution.py:65
  48.5 5.3 %collective-permute-start.19 = (bf16[8,4096]{1,0:T(8,128)(2,1)S(1)}, bf16[8,4096]{1,0:T(8,128)(2,1)S(1)}, u32[]{:S(2)}, u32[]{:S(2)}) collective-permute-start(bf16[8,4096]{1,0:T(8,128)(2,1)S(1)} %pad_maximum_fusion.refs_0_), channel_id=1, source_target_pairs={{0,2},{1,3},{2,0},{3,1},{4,6},{5,7},{6,4},{7,5},{8,10},{9,11},{10,... | collective-permute-start | bytes 196616 | tf_op jit(solution)/shard_map/ppermute | solution.py:65
  60.3 5.0 %collective-permute-start.21 = (bf16[8,4096]{1,0:T(8,128)(2,1)S(1)}, bf16[8,4096]{1,0:T(8,128)(2,1)S(1)}, u32[]{:S(2)}, u32[]{:S(2)}) collective-permute-start(bf16[8,4096]{1,0:T(8,128)(2,1)S(1)} %get-tuple-element.108), channel_id=1, source_target_pairs={{0,1},{1,0},{2,3},{3,2},{4,5},{5,4},{6,7},{7,6},{8,9},{9,8},{10,11... | collective-permute-start | bytes 196616 | tf_op jit(solution)/shard_map/ppermute | solution.py:65
  61.7 5.2 %collective-permute-start.23 = (bf16[8,4096]{1,0:T(8,128)(2,1)S(1)}, bf16[8,4096]{1,0:T(8,128)(2,1)S(1)}, u32[]{:S(2)}, u32[]{:S(2)}) collective-permute-start(bf16[8,4096]{1,0:T(8,128)(2,1)S(1)} %get-tuple-element.110), channel_id=1, source_target_pairs={{0,3},{1,2},{2,1},{3,0},{4,7},{5,6},{6,5},{7,4},{8,11},{9,10},{10,... | collective-permute-start | bytes 196616 | tf_op jit(solution)/shard_map/ppermute | solution.py:65
  66.9 5.4 %collective-permute-start.24 = (bf16[8,4096]{1,0:T(8,128)(2,1)S(1)}, bf16[8,4096]{1,0:T(8,128)(2,1)S(1)}, u32[]{:S(2)}, u32[]{:S(2)}) collective-permute-start(bf16[8,4096]{1,0:T(8,128)(2,1)S(1)} %add_convert_fusion.4), channel_id=1, source_target_pairs={{0,4},{1,5},{2,6},{3,7},{4,0},{5,1},{6,2},{7,3},{8,12},{9,13},{10,... | collective-permute-start | bytes 196616 | tf_op jit(solution)/shard_map/ppermute | solution.py:65
  74.6 5.5 %collective-permute-start.28 = (bf16[8,4096]{1,0:T(8,128)(2,1)S(1)}, bf16[8,4096]{1,0:T(8,128)(2,1)S(1)}, u32[]{:S(2)}, u32[]{:S(2)}) collective-permute-start(bf16[8,4096]{1,0:T(8,128)(2,1)S(1)} %get-tuple-element.114.refs_0_), channel_id=1, source_target_pairs={{0,3},{1,2},{2,1},{3,0},{4,7},{5,6},{6,5},{7,4},{8,11},{9,10},{10,... | collective-permute-start | bytes 196616 | tf_op jit(solution)/shard_map/ppermute | solution.py:65
  76.7 4.3 %collective-permute-start.27 = (bf16[8,4096]{1,0:T(8,128)(2,1)S(1)}, bf16[8,4096]{1,0:T(8,128)(2,1)S(1)}, u32[]{:S(2)}, u32[]{:S(2)}) collective-permute-start(bf16[8,4096]{1,0:T(8,128)(2,1)S(1)} %get-tuple-element.114.refs_0_), channel_id=1, source_target_pairs={{0,2},{1,3},{2,0},{3,1},{4,6},{5,7},{6,4},{7,5},{8,10},{9,11},{10,... | collective-permute-start | bytes 196616 | tf_op jit(solution)/shard_map/ppermute | solution.py:65
  95.6 4.6 %collective-permute-start.35 = (bf16[8,4096]{1,0:T(8,128)(2,1)S(1)}, bf16[8,4096]{1,0:T(8,128)(2,1)S(1)}, u32[]{:S(2)}, u32[]{:S(2)}) collective-permute-start(bf16[8,4096]{1,0:T(8,128)(2,1)S(1)} %get-tuple-element.125), channel_id=1, source_target_pairs={{0,1},{1,0},{2,3},{3,2},{4,5},{5,4},{6,7},{7,6},{8,9},{9,8},{10,11... | collective-permute-start | bytes 196616 | tf_op jit(solution)/shard_map/ppermute | solution.py:65
  96.5 4.9 %collective-permute-start.36 = (bf16[8,4096]{1,0:T(8,128)(2,1)S(1)}, bf16[8,4096]{1,0:T(8,128)(2,1)S(1)}, u32[]{:S(2)}, u32[]{:S(2)}) collective-permute-start(bf16[8,4096]{1,0:T(8,128)(2,1)S(1)} %get-tuple-element.126), channel_id=1, source_target_pairs={{0,2},{1,3},{2,0},{3,1},{4,6},{5,7},{6,4},{7,5},{8,10},{9,11},{10,... | collective-permute-start | bytes 196616 | tf_op jit(solution)/shard_map/ppermute | solution.py:65
  97.5 5.3 %collective-permute-start.37 = (bf16[8,4096]{1,0:T(8,128)(2,1)S(1)}, bf16[8,4096]{1,0:T(8,128)(2,1)S(1)}, u32[]{:S(2)}, u32[]{:S(2)}) collective-permute-start(bf16[8,4096]{1,0:T(8,128)(2,1)S(1)} %get-tuple-element.127), channel_id=1, source_target_pairs={{0,3},{1,2},{2,1},{3,0},{4,7},{5,6},{6,5},{7,4},{8,11},{9,10},{10,... | collective-permute-start | bytes 196616 | tf_op jit(solution)/shard_map/ppermute | solution.py:65
  102.8 5.9 %collective-permute-start.38 = (bf16[8,4096]{1,0:T(8,128)(2,1)S(1)}, bf16[8,4096]{1,0:T(8,128)(2,1)S(1)}, u32[]{:S(2)}, u32[]{:S(2)}) collective-permute-start(bf16[8,4096]{1,0:T(8,128)(2,1)S(1)} %add_convert_fusion.2.near), channel_id=1, source_target_pairs={{0,4},{1,5},{2,6},{3,7},{4,0},{5,1},{6,2},{7,3},{8,12},{9,13},{10,... | collective-permute-start | bytes 196616 | tf_op jit(solution)/shard_map/ppermute | solution.py:65
  110.3 5.9 %collective-permute-start.42 = (bf16[8,4096]{1,0:T(8,128)(2,1)S(1)}, bf16[8,4096]{1,0:T(8,128)(2,1)S(1)}, u32[]{:S(2)}, u32[]{:S(2)}) collective-permute-start(bf16[8,4096]{1,0:T(8,128)(2,1)S(1)} %pad_maximum_fusion.1.refs_0_), channel_id=1, source_target_pairs={{0,3},{1,2},{2,1},{3,0},{4,7},{5,6},{6,5},{7,4},{8,11},{9,10},{10,... | collective-permute-start | bytes 196616 | tf_op jit(solution)/shard_map/ppermute | solution.py:65
  111.2 5.2 %collective-permute-start.41 = (bf16[8,4096]{1,0:T(8,128)(2,1)S(1)}, bf16[8,4096]{1,0:T(8,128)(2,1)S(1)}, u32[]{:S(2)}, u32[]{:S(2)}) collective-permute-start(bf16[8,4096]{1,0:T(8,128)(2,1)S(1)} %pad_maximum_fusion.1.refs_0_), channel_id=1, source_target_pairs={{0,2},{1,3},{2,0},{3,1},{4,6},{5,7},{6,4},{7,5},{8,10},{9,11},{10,... | collective-permute-start | bytes 196616 | tf_op jit(solution)/shard_map/ppermute | solution.py:65
  122.8 5.0 %collective-permute-start.43 = (bf16[8,4096]{1,0:T(8,128)(2,1)S(1)}, bf16[8,4096]{1,0:T(8,128)(2,1)S(1)}, u32[]{:S(2)}, u32[]{:S(2)}) collective-permute-start(bf16[8,4096]{1,0:T(8,128)(2,1)S(1)} %get-tuple-element.133), channel_id=1, source_target_pairs={{0,1},{1,0},{2,3},{3,2},{4,5},{5,4},{6,7},{7,6},{8,9},{9,8},{10,11... | collective-permute-start | bytes 196616 | tf_op jit(solution)/shard_map/ppermute | solution.py:65
  124.2 5.2 %collective-permute-start.45 = (bf16[8,4096]{1,0:T(8,128)(2,1)S(1)}, bf16[8,4096]{1,0:T(8,128)(2,1)S(1)}, u32[]{:S(2)}, u32[]{:S(2)}) collective-permute-start(bf16[8,4096]{1,0:T(8,128)(2,1)S(1)} %get-tuple-element.135), channel_id=1, source_target_pairs={{0,3},{1,2},{2,1},{3,0},{4,7},{5,6},{6,5},{7,4},{8,11},{9,10},{10,... | collective-permute-start | bytes 196616 | tf_op jit(solution)/shard_map/ppermute | solution.py:65
  129.4 5.2 %collective-permute-start.46 = (bf16[8,4096]{1,0:T(8,128)(2,1)S(1)}, bf16[8,4096]{1,0:T(8,128)(2,1)S(1)}, u32[]{:S(2)}, u32[]{:S(2)}) collective-permute-start(bf16[8,4096]{1,0:T(8,128)(2,1)S(1)} %add_convert_fusion.1), channel_id=1, source_target_pairs={{0,4},{1,5},{2,6},{3,7},{4,0},{5,1},{6,2},{7,3},{8,12},{9,13},{10,... | collective-permute-start | bytes 196616 | tf_op jit(solution)/shard_map/ppermute | solution.py:65
  (50 other events, 254.0 us)

commit v4 on v3

--- a/solution.py
+++ b/solution.py
@@ -38,8 +38,7 @@
     return pltpu.with_memory_space_constraint(array, pltpu.HBM)
 
 
-def call(body, name, outs, specs, args, scratch=(), flops=0, moved=0, limit=8):
-    flops = max(flops, BESIDE)
+def call(body, name, outs, specs, args, scratch=(), flops=BESIDE, moved=0, limit=8):
     return pl.pallas_call(
         body,
         name=name,
@@ -140,25 +139,35 @@
         scratch[rows : 2 * rows, :] = own
 
 
-def start_body(where, own, peer, gain, x_out, normed_out, own_here, gain_here, arrived):
+def half_of(stride):
+    return jnp.where(lax.axis_index("expert") >= stride, 1, 0)
+
+
+def fetch_body(in_proj, own, gain, in_x_out, own_out, gain_out, arrived):
     copies = [
-        pltpu.make_async_copy(own, own_here, arrived.at[0]),
-        pltpu.make_async_copy(gain, gain_here, arrived.at[1]),
+        pltpu.make_async_copy(in_proj.at[0], in_x_out, arrived.at[0]),
+        pltpu.make_async_copy(own, own_out, arrived.at[1]),
+        pltpu.make_async_copy(gain, gain_out, arrived.at[2]),
     ]
     for copy in copies:
         copy.start()
     for copy in copies:
         copy.wait()
-    place_rows(x_out, own_here[0].astype(F32), peer[0].astype(F32), where[1])
-    normed_out[...] = normalize(x_out[...], gain_here[...]).astype(BF16)
-
-
-def later_body(steps, where, own, peer, *outs):
+
+
+def start_body(stride, own, peer, gain, x_out, normed_out):
+    place_rows(x_out, own[0].astype(F32), peer[0].astype(F32), half_of(stride))
+    normed_out[...] = normalize(x_out[...], gain[...]).astype(BF16)
+
+
+def later_body(steps, stride, own, peer, *outs):
     for step in range(1, steps):
-        place_rows(outs[step - 1], own[step].astype(F32), peer[step].astype(F32), where[1])
-
-
-def table_body(steps, rows, where, own, peer, select_out, combine_out):
+        place_rows(outs[step - 1], own[step].astype(F32), peer[step].astype(F32), half_of(stride))
+
+
+def table_body(steps, rows, stride, own, peer, select_out, combine_out):
+    upper = half_of(stride)
+    core = lax.axis_index("dp")
     slots = 4 * CAP
     span = 2 * rows
     slot_a = lax.broadcasted_iota(jnp.int32, (slots, span), 0)
@@ -169,13 +178,13 @@
         select = jnp.zeros((slots, span), F32)
         combine = jnp.zeros((span, slots), F32)
         for far in range(2):
-            expert = (where[2] if far == 0 else 1 - where[2]).astype(F32)
+            expert = (core if far == 0 else 1 - core).astype(F32)
             for block in range(2):
                 count = jnp.int32(0)
                 for j in range(rows):
                     at = (step * rows + j) * 6
                     entry = [
-                        jnp.where(where[1] == block, own[at + m], peer[at + m]) for m in range(6)
+                        jnp.where(upper == block, own[at + m], peer[at + m]) for m in range(6)
                     ]
                     first = entry[0] == expert
                     second = entry[1] == expert
@@ -203,9 +212,12 @@
     return (((me ^ distance) & (stride - 1)) + half * stride) * rows + within
 
 
-def first_taps_body(rows, levels, stride, where, prompts, conv, *taps):
+def first_state_body(rows, levels, stride, prompts, ssm, conv, state, *taps):
+    me = lax.axis_index("expert")
     for index in range(taps[0].shape[0]):
-        prompt = prompts[row_of(index, rows, levels, stride, where[0])]
+        row = row_of(index, rows, levels, stride, me)
+        prompt = prompts[row]
+        state[row] = ssm[prompt]
         for j, tap in enumerate(taps):
             tap[index : index + 1, :] = conv[prompt, j : j + 1, :]
 
@@ -214,7 +226,7 @@
     rows_in, refs = refs[:parts], refs[parts:]
     held_taps, refs = refs[:taps], refs[taps:]
     in_proj, conv_weight, conv_bias, x_proj, x_out, act_out, *proj_outs = refs
-    x_part = jnp.dot(joined(rows_in), in_proj[0], preferred_element_type=F32)
+    x_part = jnp.dot(joined(rows_in), in_proj[...], preferred_element_type=F32)
     x_out[...] = x_part
     mixed = x_part * conv_weight[taps : taps + 1, :]
     for j in range(taps):
@@ -235,19 +247,19 @@
     z_out[...] = silu(jnp.dot(joined(rows_in), in_proj[1], preferred_element_type=F32))
 
 
-def taps_out_body(rows, levels, stride, where, *refs):
+def taps_out_body(rows, levels, stride, *refs):
     *taps, out = refs
+    me = lax.axis_index("expert")
     for index in range(taps[0].shape[0]):
-        row = row_of(index, rows, levels, stride, where[0])
+        row = row_of(index, rows, levels, stride, me)
         for j, tap in enumerate(taps):
             out[row, j : j + 1, :] = tap[index : index + 1, :]
 
 
-def ssm_body(first, parts, rows, levels, stride, *refs):
-    where, prompts, near, far, act_in, z_in, dt_proj, dt_bias, a_log, d_skip, out_proj, before = (
-        refs[:12]
-    )
-    outs, (after, y) = refs[12 : 12 + parts], refs[12 + parts :]
+def ssm_body(parts, rows, levels, stride, *refs):
+    near, far, act_in, z_in, dt_proj, dt_bias, a_log, d_skip, out_proj, before = refs[:10]
+    outs, (after, y) = refs[10 : 10 + parts], refs[10 + parts :]
+    me = lax.axis_index("expert")
     rank = dt_proj.shape[0]
     states = a_log.shape[0]
     width = rank + 2 * states
@@ -265,10 +277,9 @@
     driven = delta * act
     decay = -jnp.exp(a_log[...])
     for index in range(delta.shape[0]):
-        row = row_of(index, rows, levels, stride, where[0])
-        held_state = before[prompts[row]] if first else before[row]
+        row = row_of(index, rows, levels, stride, me)
         state = (
-            jnp.exp(delta[index : index + 1, :] * decay) * held_state
+            jnp.exp(delta[index : index + 1, :] * decay) * before[row]
             + driven[index : index + 1, :] * maps[:states, index : index + 1]
         )
         after[row] = state
@@ -299,9 +310,15 @@
     outs = refs[parts + 3 :]
     rows = joined(rows_in)
     dims = (((1,), (1,)), ((), ()))
-    gate_val = lax.dot_general(rows, gate[...], dims, preferred_element_type=F32)
-    up_val = lax.dot_general(rows, up[...], dims, preferred_element_type=F32)
-    hidden = (silu(gate_val) * up_val).astype(BF16)
+    units = gate.shape[0]
+    block = 128 if units % 128 == 0 else units
+    hidden = []
+    for start in range(0, units, block):
+        some = slice(start, start + block)
+        up_val = lax.dot_general(up[some, :], rows, dims, preferred_element_type=F32)
+        gate_val = lax.dot_general(rows, gate[some, :], dims, preferred_element_type=F32)
+        hidden.append((silu(gate_val) * jnp.transpose(up_val)).astype(BF16))
+    hidden = hidden[0] if len(hidden) == 1 else jnp.concatenate(hidden, axis=1)
     result = jnp.dot(hidden, down[...], preferred_element_type=F32)
     size = result.shape[0] // parts
     for k, out in enumerate(outs):
@@ -331,20 +348,20 @@
         out[...] = values[rows:].astype(BF16)
 
 
-def next_body(where, h_in, near, far, combine, added, gain, out, x_out, normed_out):
+def next_body(stride, h_in, near, far, combine, added, gain, out, x_out, normed_out):
     values = combined(h_in, near, far, combine)
-    store_own(out, out.shape[0], values, where[1])
+    store_own(out, out.shape[0], values, half_of(stride))
     x = values + added[...]
     x_out[...] = x
     normed_out[...] = normalize(x, gain[...]).astype(BF16)
 
 
-def last_body(earlier, where, h_in, near, far, combine, *refs):
+def last_body(earlier, stride, h_in, near, far, combine, *refs):
     before, out = refs[:earlier], refs[earlier]
     values = combined(h_in, near, far, combine)
     for step in range(earlier):
         out[step] = before[step][...]
-    store_own(out.at[earlier], out.shape[1], values, where[1])
+    store_own(out.at[earlier], out.shape[1], values, half_of(stride))
 
 
 def on_device(
@@ -378,24 +395,25 @@
     taps = prompt_conv.shape[1]
     states = a_log.shape[0]
     slots = 2 * 2 * CAP
-    me = lax.axis_index("expert")
     core = lax.axis_index("dp")
-    where = jnp.stack([me, me // stride, core]).astype(jnp.int32)
 
     peer_input = partner(layer_input, stride, count)
+    in_x, own_input, mamba_gain = call(
+        fetch_body,
+        "fetch",
+        [((width, channels), BF16), (layer_input.shape, BF16), ((1, width), F32)],
+        [ANY] * 3,
+        (in_hbm(in_proj), in_hbm(layer_input), in_hbm(mamba_gain.reshape(1, width))),
+        scratch=[pltpu.SemaphoreType.DMA((3,))],
+        limit=16,
+    )
     x, normed = call(
-        start_body,
+        functools.partial(start_body, stride),
         "first_norm",
         [((2 * rows, width), F32), ((2 * rows, width), BF16)],
-        [SMEM, ANY, VMEM, ANY],
-        (where, in_hbm(layer_input), peer_input, in_hbm(mamba_gain.reshape(1, width))),
-        scratch=[
-            pltpu.VMEM(layer_input.shape, BF16),
-            pltpu.VMEM((1, width), F32),
-            pltpu.SemaphoreType.DMA((2,)),
-        ],
-    )
-    mamba_gain = held(mamba_gain.reshape(1, width))
+        [VMEM] * 3,
+        (own_input, peer_input, mamba_gain),
+    )
     moe_gain = held(moe_gain.reshape(1, width))
     normed, layer_input, prompt_ssm, prompt_conv, route_ids, route_weights = (
         lax.optimization_barrier(
@@ -430,14 +448,13 @@
     gate, up, down = w_gate[0], w_up[0], w_down[0]
     place = (rows, levels, stride)
 
-    window = call(
-        functools.partial(first_taps_body, *place),
-        "first_taps",
-        [((group_rows, channels), F32)] * taps,
-        [SMEM, SMEM, VMEM],
-        (where, sample_prompt, all_conv),
-    )
-    state = all_ssm
+    state, *window = call(
+        functools.partial(first_state_body, *place),
+        "first_state",
+        [((group_rows, states, channels), F32)] + [((group_rows, channels), F32)] * taps,
+        [SMEM, VMEM, VMEM],
+        (sample_prompt, all_ssm, all_conv),
+    )
     outputs = []
     for step in range(steps):
         last = step == steps - 1
@@ -454,9 +471,7 @@
             ]
             + [((group_rows, x_proj.shape[0]), BF16)] * parts,
             [VMEM] * (parts + taps + 4),
-            (*rows_in, *window, held(in_proj), conv_weight, conv_bias, held(x_proj)),
-            flops=2 * group_rows * width * channels,
-            moved=2 * width * channels,
+            (*rows_in, *window, held(in_x), conv_weight, conv_bias, held(x_proj)),
         )
         window = [*window[1:], x_part]
         proj = add_everywhere(proj, levels, count)
@@ -469,27 +484,23 @@
             [((group_rows, channels), F32)],
             [VMEM] * (parts + 1),
             (*rows_in, held(in_proj)),
-            flops=2 * group_rows * width * channels,
-            moved=2 * width * channels,
         )[0]
         if last:
             conv_state = call(
                 functools.partial(taps_out_body, *place),
                 "taps_out",
                 [((group_rows, taps, channels), F32)],
-                [SMEM] + [VMEM] * taps,
-                (where, *window),
+                [VMEM] * taps,
+                (*window,),
             )[0]
             proj_far, conv_state = lax.optimization_barrier((proj_far, conv_state))
         *mixed, state = call(
-            functools.partial(ssm_body, step == 0, parts, *place),
+            functools.partial(ssm_body, parts, *place),
             "mamba_ssm",
             [((group_rows // parts, width), BF16)] * parts
             + [((group_rows, states, channels), F32)],
-            [SMEM, SMEM] + [VMEM] * 10,
+            [VMEM] * 10,
             (
-                where,
-                sample_prompt,
                 proj,
                 proj_far,
                 act,
@@ -502,30 +513,27 @@
                 state,
             ),
             scratch=[pltpu.VMEM((group_rows, channels), F32)],
-            flops=2 * group_rows * width * channels,
-            moved=2 * width * channels,
         )
-        beside = (proj, proj_far, layer_input, peer_input) if step == 0 else ()
+        beside = (proj, proj_far, own_input, peer_input) if step == 0 else ()
         mixed_near, beside = collect(mixed, levels, count, beside)
         if step == 0:
             near_routes, far_routes, later_own, later_peer = beside
             select, combine = call(
-                functools.partial(table_body, steps, rows),
+                functools.partial(table_body, steps, rows, stride),
                 "route_tables",
                 [((steps, slots, 2 * rows), F32), ((steps, 2 * rows, slots), F32)],
-                [SMEM, SMEM, SMEM],
+                [SMEM, SMEM],
                 (
-                    where,
                     near_routes[:, x_proj.shape[0] :].astype(F32).reshape(-1),
                     far_routes[:, x_proj.shape[0] :].astype(F32).reshape(-1),
                 ),
             )
             later = call(
-                functools.partial(later_body, steps),
+                functools.partial(later_body, steps, stride),
                 "later_inputs",
                 [((2 * rows, width), F32)] * (steps - 1),
-                [SMEM, VMEM, VMEM],
-                (where, later_own, later_peer),
+                [VMEM, VMEM],
+                (later_own, later_peer),
             )
         mixed_far = partner(mixed_near, stride, count)
         h, own, other = call(
@@ -547,31 +555,29 @@
             [((total_slots // parts, width), BF16)] * parts,
             [VMEM] * (parts + 3),
             (*picked, held(gate), held(up), held(down)),
-            flops=6 * total_slots * width * gate.shape[0],
-            moved=6 * width * gate.shape[0],
         )
         out_near, _ = collect(returned, levels, count)
         summed = total([out_near, partner(out_near, stride, count)]).astype(BF16)
         out_far = other_core(summed[slots // 2 :])
         if last:
             layer_output = call(
-                functools.partial(last_body, step),
+                functools.partial(last_body, step, stride),
                 "last_output",
                 [((steps, rows, width), BF16)],
-                [SMEM] + [VMEM] * (4 + step),
-                (where, h, summed, out_far, combine[step], *outputs),
+                [VMEM] * (4 + step),
+                (h, summed, out_far, combine[step], *outputs),
             )[0]
         else:
             out, x, normed = call(
-                next_body,
+                functools.partial(next_body, stride),
                 "next_norm",
                 [
                     ((rows, width), BF16),
                     ((2 * rows, width), F32),
                     ((2 * rows, width), BF16),
                 ],
-                [SMEM] + [VMEM] * 6,
-                (where, h, summed, out_far, combine[step], later[step], mamba_gain),
+                [VMEM] * 6,
+                (h, summed, out_far, combine[step], later[step], mamba_gain),
             )
             outputs.append(out)
             rows_in = spread(normed, levels, count)

time: 137 us -> 133 us (0.971)
  starting transfers between devices: 56.5 us -> 51.7 us
  Pallas kernels: 26.3 us -> 22.3 us
  waiting for transfers between devices: 50.9 us -> 53.5 us
  local copies, waits for them, and re-layouts: 1.84 us -> 3.6 us
    pallas_call x17 -> x18, Pallas kernels: 26.3 us -> 22.3 us  [call(): pl.pallas_call(body, name=name, out_shape=[jax.ShapeDtypeStruct(s, d) for...]
    ppermute x29, starting transfers between devices: 43 us -> 39.9 us  [partner(): lax.ppermute(array, 'expert', [(i, i ^ distance) for i in range(count)])]
    ppermute x12, waiting for transfers between devices: 6.51 us -> 8.67 us  [across(): lax.ppermute(array, ('dp', 'expert'), pairs + [(b, a) for a, b in pairs])]
    unnamed x53 -> x57, local copies, waits for them, and re-layouts: 1.27 us -> 3.03 us
    ppermute x12, starting transfers between devices: 12.3 us -> 10.7 us  [across(): lax.ppermute(array, ('dp', 'expert'), pairs + [(b, a) for a, b in pairs])]
  transfers between devices with their start and end apart: 48 -> 48, of which waited for: 40 -> 38; matrix products, arithmetic and copies ran while one was open for 1% -> 1% of each run, Pallas kernels for 3% -> 4%
where the time goes in v4:
time: 133 us
  waiting for transfers between devices  53.5 us (40%)
  starting transfers between devices  51.7 us (39%)
  Pallas kernels  22.3 us (17%)
  local copies, waits for them, and re-layouts  3.6 us (3%)
    ppermute x29, starting transfers between devices, partner(): lax.ppermute(array, 'expert', [(i, i ^ distance) for i in range(count)])  39.9 us
    ppermute x29, waiting for transfers between devices, partner(): lax.ppermute(array, 'expert', [(i, i ^ distance) for i in range(count)])  39.6 us
    pallas_call x18, Pallas kernels, call(): pl.pallas_call(body, name=name, out_shape=[jax.ShapeDtypeStruct(s, d) for...  22.3 us
    ppermute x12, starting transfers between devices, across(): lax.ppermute(array, ('dp', 'expert'), pairs + [(b, a) for a, b in pairs])  10.7 us
    ppermute x12, waiting for transfers between devices, across(): lax.ppermute(array, ('dp', 'expert'), pairs + [(b, a) for a, b in pairs])  8.67 us
    ppermute x7, waiting for transfers between devices, other_core(): return lax.ppermute(array, 'dp', [(0, 1), (1, 0)])  5.15 us
    unnamed x57, local copies, waits for them, and re-layouts  3.03 us
  transfers between devices with their start and end apart: 48, of which 38 were waited for; matrix products, arithmetic and copies ran while one was open for 1% of the time, Pallas kernels for 4%

profile of v4, /device:TPU:0, one launch (start us, length us, event | category | flops | bytes accessed | tf_op | source)
XLA Modules:
  0.0 132.8 jit_solution(10607072042796278201)
XLA Ops:
  0.6 4.1 %collective-permute-start = (bf16[2,4,4096]{2,1,0:T(4,128)(2,1)}, bf16[2,4,4096]{2,1,0:T(4,128)(2,1)S(1)}, u32[]{:S(2)}, u32[]{:S(2)}) collective-permute-start(bf16[2,4,4096]{2,1,0:T(4,128)(2,1)} %own.1), channel_id=1, source_target_pairs={{0,4},{1,5},{2,6},{3,7},{4,0},{5,1},{6,2},{7,3},{8,12},{9,13},{10,... | collective-permute-start | bytes 196616 | tf_op jit(solution)/shard_map/ppermute | solution.py:64
  4.7 2.2 %fetch.1 = (bf16[4096,512]{1,0:T(8,128)(2,1)S(1)}, bf16[2,4,4096]{2,1,0:T(4,128)(2,1)S(1)}, f32[1,4096]{1,0:T(1,128)S(1)}) custom-call(bf16[2,4096,512]{2,1,0:T(8,128)(2,1)} %refs_4_.6, bf16[2,4,4096]{2,1,0:T(4,128)(2,1)} %own.1, f32[1,4096]{1,0:T(1,128)} %bitcast.40), custom_call_target="tpu_custom_call" | custom-call | flops 10000000000 | tf_op jit(solution)/shard_map/fetch/pallas_call | solution.py:42
  7.0 2.0 %copy-done.11 = bf16[4096,512]{1,0:T(8,128)(2,1)} copy-done((bf16[4096,512]{1,0:T(8,128)(2,1)}, bf16[4096,512]{1,0:T(8,128)(2,1)S(1)}, u32[]{:S(2)}) %copy-start.11) | copy-done | bytes 4194328
  9.2 2.6 %collective-permute-start.3 = (bf16[8,4096]{1,0:T(8,128)(2,1)S(1)}, bf16[8,4096]{1,0:T(8,128)(2,1)S(1)}, u32[]{:S(2)}, u32[]{:S(2)}) collective-permute-start(bf16[8,4096]{1,0:T(8,128)(2,1)S(1)} %get-tuple-element.86.refs_0_), channel_id=1, source_target_pairs={{0,3},{1,2},{2,1},{3,0},{4,7},{5,6},{6,5},{7,4},{8,11},{9,10},{10,... | collective-permute-start | bytes 196616 | tf_op jit(solution)/shard_map/ppermute | solution.py:64
  23.1 2.2 %collective-permute-done.10 = bf16[32,288]{1,0:T(8,128)(2,1)S(1)} collective-permute-done((bf16[32,288]{1,0:T(8,128)(2,1)S(1)}, bf16[32,288]{1,0:T(8,128)(2,1)S(1)}, u32[]{:S(2)}, u32[]{:S(2)}) %collective-permute-start.10) | collective-permute-done | bytes 18464 | tf_op jit(solution)/shard_map/ppermute | solution.py:73
  25.5 2.0 %collective-permute-start.12 = (bf16[32,290]{1,0:T(8,128)(2,1)S(1)}, bf16[32,290]{1,0:T(8,128)(2,1)S(1)}, u32[]{:S(2)}, u32[]{:S(2)}) collective-permute-start(bf16[32,290]{1,0:T(8,128)(2,1)S(1)} %pad_maximum_fusion.2), channel_id=1, source_target_pairs={{0,12},{1,13},{2,14},{3,15},{4,8},{5,9},{6,10},{7,11},{12,0},{13,1... | collective-permute-start | bytes 55688 | tf_op jit(solution)/shard_map/ppermute | solution.py:73
  32.8 2.1 %collective-permute-start.15 = (bf16[8,4096]{1,0:T(8,128)(2,1)S(1)}, bf16[8,4096]{1,0:T(8,128)(2,1)S(1)}, u32[]{:S(2)}, u32[]{:S(2)}) collective-permute-start(bf16[8,4096]{1,0:T(8,128)(2,1)S(1)} %get-tuple-element.105), channel_id=1, source_target_pairs={{0,3},{1,2},{2,1},{3,0},{4,7},{5,6},{6,5},{7,4},{8,11},{9,10},{10,... | collective-permute-start | bytes 196616 | tf_op jit(solution)/shard_map/ppermute | solution.py:64
  38.4 1.9 %collective-permute-start.16 = (bf16[8,4096]{1,0:T(8,128)(2,1)S(1)}, bf16[8,4096]{1,0:T(8,128)(2,1)S(1)}, u32[]{:S(2)}, u32[]{:S(2)}) collective-permute-start(bf16[8,4096]{1,0:T(8,128)(2,1)S(1)} %add_convert_fusion.5.near), channel_id=1, source_target_pairs={{0,4},{1,5},{2,6},{3,7},{4,0},{5,1},{6,2},{7,3},{8,12},{9,13},{10,... | collective-permute-start | bytes 196616 | tf_op jit(solution)/shard_map/ppermute | solution.py:64
  41.2 2.5 %collective-permute-done.16.far = bf16[8,4096]{1,0:T(8,128)(2,1)S(1)} collective-permute-done((bf16[8,4096]{1,0:T(8,128)(2,1)S(1)}, bf16[8,4096]{1,0:T(8,128)(2,1)S(1)}, u32[]{:S(2)}, u32[]{:S(2)}) %collective-permute-start.16) | collective-permute-done | bytes 65568 | tf_op jit(solution)/shard_map/ppermute | solution.py:64
  48.8 1.9 %collective-permute-done.20.refs_3_ = bf16[8,4096]{1,0:T(8,128)(2,1)S(1)} collective-permute-done((bf16[8,4096]{1,0:T(8,128)(2,1)S(1)}, bf16[8,4096]{1,0:T(8,128)(2,1)S(1)}, u32[]{:S(2)}, u32[]{:S(2)}) %collective-permute-start.20) | collective-permute-done | bytes 65568 | tf_op jit(solution)/shard_map/ppermute | solution.py:64
  53.0 4.9 %experts.2 = (bf16[8,4096]{1,0:T(8,128)(2,1)S(1)}, bf16[8,4096]{1,0:T(8,128)(2,1)S(1)}, bf16[8,4096]{1,0:T(8,128)(2,1)S(1)}, bf16[8,4096]{1,0:T(8,128)(2,1)S(1)}) custom-call(bf16[8,4096]{1,0:T(8,128)(2,1)S(1)} %pad_maximum_fusion.refs_0_, bf16[8,4096]{1,0:T(8,128)(2,1)S(1)} %collective-permute-done.18.refs_1_, ...), custom_call_target="tpu_custom_call" | custom-call | flops 10000000000 | tf_op jit(solution)/shard_map/experts/pallas_call | solution.py:42
  62.8 2.0 %collective-permute-done.23 = bf16[8,4096]{1,0:T(8,128)(2,1)S(1)} collective-permute-done((bf16[8,4096]{1,0:T(8,128)(2,1)S(1)}, bf16[8,4096]{1,0:T(8,128)(2,1)S(1)}, u32[]{:S(2)}, u32[]{:S(2)}) %collective-permute-start.23) | collective-permute-done | bytes 65568 | tf_op jit(solution)/shard_map/ppermute | solution.py:64
  64.8 2.2 %collective-permute-start.24 = (bf16[8,4096]{1,0:T(8,128)(2,1)S(1)}, bf16[8,4096]{1,0:T(8,128)(2,1)S(1)}, u32[]{:S(2)}, u32[]{:S(2)}) collective-permute-start(bf16[8,4096]{1,0:T(8,128)(2,1)S(1)} %add_convert_fusion.4), channel_id=1, source_target_pairs={{0,4},{1,5},{2,6},{3,7},{4,0},{5,1},{6,2},{7,3},{8,12},{9,13},{10,... | collective-permute-start | bytes 196616 | tf_op jit(solution)/shard_map/ppermute | solution.py:64
  67.1 3.7 %collective-permute-done.24 = bf16[8,4096]{1,0:T(8,128)(2,1)S(1)} collective-permute-done((bf16[8,4096]{1,0:T(8,128)(2,1)S(1)}, bf16[8,4096]{1,0:T(8,128)(2,1)S(1)}, u32[]{:S(2)}, u32[]{:S(2)}) %collective-permute-start.24) | collective-permute-done | bytes 65568 | tf_op jit(solution)/shard_map/ppermute | solution.py:64
  74.3 1.9 %collective-permute-start.26 = (bf16[8,4096]{1,0:T(8,128)(2,1)S(1)}, bf16[8,4096]{1,0:T(8,128)(2,1)S(1)}, u32[]{:S(2)}, u32[]{:S(2)}) collective-permute-start(bf16[8,4096]{1,0:T(8,128)(2,1)S(1)} %get-tuple-element.120.refs_0_), channel_id=1, source_target_pairs={{0,1},{1,0},{2,3},{3,2},{4,5},{5,4},{6,7},{7,6},{8,9},{9,8},{10,11... | collective-permute-start | bytes 196616 | tf_op jit(solution)/shard_map/ppermute | solution.py:64
  76.2 2.3 %collective-permute-done.28.refs_3_ = bf16[8,4096]{1,0:T(8,128)(2,1)S(1)} collective-permute-done((bf16[8,4096]{1,0:T(8,128)(2,1)S(1)}, bf16[8,4096]{1,0:T(8,128)(2,1)S(1)}, u32[]{:S(2)}, u32[]{:S(2)}) %collective-permute-start.28) | collective-permute-done | bytes 65568 | tf_op jit(solution)/shard_map/ppermute | solution.py:64
  97.4 2.0 %collective-permute-done.37 = bf16[8,4096]{1,0:T(8,128)(2,1)S(1)} collective-permute-done((bf16[8,4096]{1,0:T(8,128)(2,1)S(1)}, bf16[8,4096]{1,0:T(8,128)(2,1)S(1)}, u32[]{:S(2)}, u32[]{:S(2)}) %collective-permute-start.37) | collective-permute-done | bytes 65568 | tf_op jit(solution)/shard_map/ppermute | solution.py:64
  99.5 2.0 %collective-permute-start.38 = (bf16[8,4096]{1,0:T(8,128)(2,1)S(1)}, bf16[8,4096]{1,0:T(8,128)(2,1)S(1)}, u32[]{:S(2)}, u32[]{:S(2)}) collective-permute-start(bf16[8,4096]{1,0:T(8,128)(2,1)S(1)} %add_convert_fusion.2.near), channel_id=1, source_target_pairs={{0,4},{1,5},{2,6},{3,7},{4,0},{5,1},{6,2},{7,3},{8,12},{9,13},{10,... | collective-permute-start | bytes 196616 | tf_op jit(solution)/shard_map/ppermute | solution.py:64
  101.5 3.9 %collective-permute-done.38.far = bf16[8,4096]{1,0:T(8,128)(2,1)S(1)} collective-permute-done((bf16[8,4096]{1,0:T(8,128)(2,1)S(1)}, bf16[8,4096]{1,0:T(8,128)(2,1)S(1)}, u32[]{:S(2)}, u32[]{:S(2)}) %collective-permute-start.38) | collective-permute-done | bytes 65568 | tf_op jit(solution)/shard_map/ppermute | solution.py:64
  107.7 2.0 %collective-permute-start.41 = (bf16[8,4096]{1,0:T(8,128)(2,1)S(1)}, bf16[8,4096]{1,0:T(8,128)(2,1)S(1)}, u32[]{:S(2)}, u32[]{:S(2)}) collective-permute-start(bf16[8,4096]{1,0:T(8,128)(2,1)S(1)} %pad_maximum_fusion.1.refs_0_), channel_id=1, source_target_pairs={{0,2},{1,3},{2,0},{3,1},{4,6},{5,7},{6,4},{7,5},{8,10},{9,11},{10,... | collective-permute-start | bytes 196616 | tf_op jit(solution)/shard_map/ppermute | solution.py:64
  110.5 2.4 %collective-permute-done.42.refs_3_ = bf16[8,4096]{1,0:T(8,128)(2,1)S(1)} collective-permute-done((bf16[8,4096]{1,0:T(8,128)(2,1)S(1)}, bf16[8,4096]{1,0:T(8,128)(2,1)S(1)}, u32[]{:S(2)}, u32[]{:S(2)}) %collective-permute-start.42) | collective-permute-done | bytes 65568 | tf_op jit(solution)/shard_map/ppermute | solution.py:64
  114.0 4.8 %experts.3 = (bf16[8,4096]{1,0:T(8,128)(2,1)S(1)}, bf16[8,4096]{1,0:T(8,128)(2,1)S(1)}, bf16[8,4096]{1,0:T(8,128)(2,1)S(1)}, bf16[8,4096]{1,0:T(8,128)(2,1)S(1)}) custom-call(bf16[8,4096]{1,0:T(8,128)(2,1)S(1)} %pad_maximum_fusion.1.refs_0_, bf16[8,4096]{1,0:T(8,128)(2,1)S(1)} %collective-permute-done.40.refs_1_, ...), custom_call_target="tpu_custom_call" | custom-call | flops 10000000000 | tf_op jit(solution)/shard_map/experts/pallas_call | solution.py:42
  120.2 2.1 %collective-permute-start.45 = (bf16[8,4096]{1,0:T(8,128)(2,1)S(1)}, bf16[8,4096]{1,0:T(8,128)(2,1)S(1)}, u32[]{:S(2)}, u32[]{:S(2)}) collective-permute-start(bf16[8,4096]{1,0:T(8,128)(2,1)S(1)} %get-tuple-element.141), channel_id=1, source_target_pairs={{0,3},{1,2},{2,1},{3,0},{4,7},{5,6},{6,5},{7,4},{8,11},{9,10},{10,... | collective-permute-start | bytes 196616 | tf_op jit(solution)/shard_map/ppermute | solution.py:64
  126.8 3.8 %collective-permute-done.46 = bf16[8,4096]{1,0:T(8,128)(2,1)S(1)} collective-permute-done((bf16[8,4096]{1,0:T(8,128)(2,1)S(1)}, bf16[8,4096]{1,0:T(8,128)(2,1)S(1)}, u32[]{:S(2)}, u32[]{:S(2)}) %collective-permute-start.46) | collective-permute-done | bytes 65568 | tf_op jit(solution)/shard_map/ppermute | solution.py:64
  (180 shorter events, 68.0 us)
Async XLA Ops:
  0.6 8.3 %collective-permute-start = (bf16[2,4,4096]{2,1,0:T(4,128)(2,1)}, bf16[2,4,4096]{2,1,0:T(4,128)(2,1)S(1)}, u32[]{:S(2)}, u32[]{:S(2)}) collective-permute-start(bf16[2,4,4096]{2,1,0:T(4,128)(2,1)} %own.1), channel_id=1, source_target_pairs={{0,4},{1,5},{2,6},{3,7},{4,0},{5,1},{6,2},{7,3},{8,12},{9,13},{10,... | collective-permute-start | bytes 196616 | tf_op jit(solution)/shard_map/ppermute | solution.py:64
  9.2 6.7 %collective-permute-start.3 = (bf16[8,4096]{1,0:T(8,128)(2,1)S(1)}, bf16[8,4096]{1,0:T(8,128)(2,1)S(1)}, u32[]{:S(2)}, u32[]{:S(2)}) collective-permute-start(bf16[8,4096]{1,0:T(8,128)(2,1)S(1)} %get-tuple-element.86.refs_0_), channel_id=1, source_target_pairs={{0,3},{1,2},{2,1},{3,0},{4,7},{5,6},{6,5},{7,4},{8,11},{9,10},{10,... | collective-permute-start | bytes 196616 | tf_op jit(solution)/shard_map/ppermute | solution.py:64
  25.5 4.4 %collective-permute-start.12 = (bf16[32,290]{1,0:T(8,128)(2,1)S(1)}, bf16[32,290]{1,0:T(8,128)(2,1)S(1)}, u32[]{:S(2)}, u32[]{:S(2)}) collective-permute-start(bf16[32,290]{1,0:T(8,128)(2,1)S(1)} %pad_maximum_fusion.2), channel_id=1, source_target_pairs={{0,12},{1,13},{2,14},{3,15},{4,8},{5,9},{6,10},{7,11},{12,0},{13,1... | collective-permute-start | bytes 55688 | tf_op jit(solution)/shard_map/ppermute | solution.py:73
  31.4 4.4 %collective-permute-start.13 = (bf16[8,4096]{1,0:T(8,128)(2,1)S(1)}, bf16[8,4096]{1,0:T(8,128)(2,1)S(1)}, u32[]{:S(2)}, u32[]{:S(2)}) collective-permute-start(bf16[8,4096]{1,0:T(8,128)(2,1)S(1)} %get-tuple-element.102), channel_id=1, source_target_pairs={{0,1},{1,0},{2,3},{3,2},{4,5},{5,4},{6,7},{7,6},{8,9},{9,8},{10,11... | collective-permute-start | bytes 196616 | tf_op jit(solution)/shard_map/ppermute | solution.py:64
  32.8 4.5 %collective-permute-start.14 = (bf16[8,4096]{1,0:T(8,128)(2,1)S(1)}, bf16[8,4096]{1,0:T(8,128)(2,1)S(1)}, u32[]{:S(2)}, u32[]{:S(2)}) collective-permute-start(bf16[8,4096]{1,0:T(8,128)(2,1)S(1)} %get-tuple-element.104), channel_id=1, source_target_pairs={{0,2},{1,3},{2,0},{3,1},{4,6},{5,7},{6,4},{7,5},{8,10},{9,11},{10,... | collective-permute-start | bytes 196616 | tf_op jit(solution)/shard_map/ppermute | solution.py:64
  32.8 5.6 %collective-permute-start.15 = (bf16[8,4096]{1,0:T(8,128)(2,1)S(1)}, bf16[8,4096]{1,0:T(8,128)(2,1)S(1)}, u32[]{:S(2)}, u32[]{:S(2)}) collective-permute-start(bf16[8,4096]{1,0:T(8,128)(2,1)S(1)} %get-tuple-element.105), channel_id=1, source_target_pairs={{0,3},{1,2},{2,1},{3,0},{4,7},{5,6},{6,5},{7,4},{8,11},{9,10},{10,... | collective-permute-start | bytes 196616 | tf_op jit(solution)/shard_map/ppermute | solution.py:64
  38.4 5.2 %collective-permute-start.16 = (bf16[8,4096]{1,0:T(8,128)(2,1)S(1)}, bf16[8,4096]{1,0:T(8,128)(2,1)S(1)}, u32[]{:S(2)}, u32[]{:S(2)}) collective-permute-start(bf16[8,4096]{1,0:T(8,128)(2,1)S(1)} %add_convert_fusion.5.near), channel_id=1, source_target_pairs={{0,4},{1,5},{2,6},{3,7},{4,0},{5,1},{6,2},{7,3},{8,12},{9,13},{10,... | collective-permute-start | bytes 196616 | tf_op jit(solution)/shard_map/ppermute | solution.py:64
  45.3 5.5 %collective-permute-start.20 = (bf16[8,4096]{1,0:T(8,128)(2,1)S(1)}, bf16[8,4096]{1,0:T(8,128)(2,1)S(1)}, u32[]{:S(2)}, u32[]{:S(2)}) collective-permute-start(bf16[8,4096]{1,0:T(8,128)(2,1)S(1)} %pad_maximum_fusion.refs_0_), channel_id=1, source_target_pairs={{0,3},{1,2},{2,1},{3,0},{4,7},{5,6},{6,5},{7,4},{8,11},{9,10},{10,... | collective-permute-start | bytes 196616 | tf_op jit(solution)/shard_map/ppermute | solution.py:64
  47.2 5.0 %collective-permute-start.19 = (bf16[8,4096]{1,0:T(8,128)(2,1)S(1)}, bf16[8,4096]{1,0:T(8,128)(2,1)S(1)}, u32[]{:S(2)}, u32[]{:S(2)}) collective-permute-start(bf16[8,4096]{1,0:T(8,128)(2,1)S(1)} %pad_maximum_fusion.refs_0_), channel_id=1, source_target_pairs={{0,2},{1,3},{2,0},{3,1},{4,6},{5,7},{6,4},{7,5},{8,10},{9,11},{10,... | collective-permute-start | bytes 196616 | tf_op jit(solution)/shard_map/ppermute | solution.py:64
  57.8 5.0 %collective-permute-start.21 = (bf16[8,4096]{1,0:T(8,128)(2,1)S(1)}, bf16[8,4096]{1,0:T(8,128)(2,1)S(1)}, u32[]{:S(2)}, u32[]{:S(2)}) collective-permute-start(bf16[8,4096]{1,0:T(8,128)(2,1)S(1)} %get-tuple-element.114), channel_id=1, source_target_pairs={{0,1},{1,0},{2,3},{3,2},{4,5},{5,4},{6,7},{7,6},{8,9},{9,8},{10,11... | collective-permute-start | bytes 196616 | tf_op jit(solution)/shard_map/ppermute | solution.py:64
  59.6 5.2 %collective-permute-start.23 = (bf16[8,4096]{1,0:T(8,128)(2,1)S(1)}, bf16[8,4096]{1,0:T(8,128)(2,1)S(1)}, u32[]{:S(2)}, u32[]{:S(2)}) collective-permute-start(bf16[8,4096]{1,0:T(8,128)(2,1)S(1)} %get-tuple-element.116), channel_id=1, source_target_pairs={{0,3},{1,2},{2,1},{3,0},{4,7},{5,6},{6,5},{7,4},{8,11},{9,10},{10,... | collective-permute-start | bytes 196616 | tf_op jit(solution)/shard_map/ppermute | solution.py:64
  64.8 5.9 %collective-permute-start.24 = (bf16[8,4096]{1,0:T(8,128)(2,1)S(1)}, bf16[8,4096]{1,0:T(8,128)(2,1)S(1)}, u32[]{:S(2)}, u32[]{:S(2)}) collective-permute-start(bf16[8,4096]{1,0:T(8,128)(2,1)S(1)} %add_convert_fusion.4), channel_id=1, source_target_pairs={{0,4},{1,5},{2,6},{3,7},{4,0},{5,1},{6,2},{7,3},{8,12},{9,13},{10,... | collective-permute-start | bytes 196616 | tf_op jit(solution)/shard_map/ppermute | solution.py:64
  72.6 5.8 %collective-permute-start.28 = (bf16[8,4096]{1,0:T(8,128)(2,1)S(1)}, bf16[8,4096]{1,0:T(8,128)(2,1)S(1)}, u32[]{:S(2)}, u32[]{:S(2)}) collective-permute-start(bf16[8,4096]{1,0:T(8,128)(2,1)S(1)} %get-tuple-element.120.refs_0_), channel_id=1, source_target_pairs={{0,3},{1,2},{2,1},{3,0},{4,7},{5,6},{6,5},{7,4},{8,11},{9,10},{10,... | collective-permute-start | bytes 196616 | tf_op jit(solution)/shard_map/ppermute | solution.py:64
  73.7 4.8 %collective-permute-start.27 = (bf16[8,4096]{1,0:T(8,128)(2,1)S(1)}, bf16[8,4096]{1,0:T(8,128)(2,1)S(1)}, u32[]{:S(2)}, u32[]{:S(2)}) collective-permute-start(bf16[8,4096]{1,0:T(8,128)(2,1)S(1)} %get-tuple-element.120.refs_0_), channel_id=1, source_target_pairs={{0,2},{1,3},{2,0},{3,1},{4,6},{5,7},{6,4},{7,5},{8,10},{9,11},{10,... | collective-permute-start | bytes 196616 | tf_op jit(solution)/shard_map/ppermute | solution.py:64
  74.3 4.9 %collective-permute-start.26 = (bf16[8,4096]{1,0:T(8,128)(2,1)S(1)}, bf16[8,4096]{1,0:T(8,128)(2,1)S(1)}, u32[]{:S(2)}, u32[]{:S(2)}) collective-permute-start(bf16[8,4096]{1,0:T(8,128)(2,1)S(1)} %get-tuple-element.120.refs_0_), channel_id=1, source_target_pairs={{0,1},{1,0},{2,3},{3,2},{4,5},{5,4},{6,7},{7,6},{8,9},{9,8},{10,11... | collective-permute-start | bytes 196616 | tf_op jit(solution)/shard_map/ppermute | solution.py:64
  91.8 4.4 %collective-permute-start.35 = (bf16[8,4096]{1,0:T(8,128)(2,1)S(1)}, bf16[8,4096]{1,0:T(8,128)(2,1)S(1)}, u32[]{:S(2)}, u32[]{:S(2)}) collective-permute-start(bf16[8,4096]{1,0:T(8,128)(2,1)S(1)} %get-tuple-element.131), channel_id=1, source_target_pairs={{0,1},{1,0},{2,3},{3,2},{4,5},{5,4},{6,7},{7,6},{8,9},{9,8},{10,11... | collective-permute-start | bytes 196616 | tf_op jit(solution)/shard_map/ppermute | solution.py:64
  92.9 4.5 %collective-permute-start.36 = (bf16[8,4096]{1,0:T(8,128)(2,1)S(1)}, bf16[8,4096]{1,0:T(8,128)(2,1)S(1)}, u32[]{:S(2)}, u32[]{:S(2)}) collective-permute-start(bf16[8,4096]{1,0:T(8,128)(2,1)S(1)} %get-tuple-element.132), channel_id=1, source_target_pairs={{0,2},{1,3},{2,0},{3,1},{4,6},{5,7},{6,4},{7,5},{8,10},{9,11},{10,... | collective-permute-start | bytes 196616 | tf_op jit(solution)/shard_map/ppermute | solution.py:64
  94.3 5.2 %collective-permute-start.37 = (bf16[8,4096]{1,0:T(8,128)(2,1)S(1)}, bf16[8,4096]{1,0:T(8,128)(2,1)S(1)}, u32[]{:S(2)}, u32[]{:S(2)}) collective-permute-start(bf16[8,4096]{1,0:T(8,128)(2,1)S(1)} %get-tuple-element.133), channel_id=1, source_target_pairs={{0,3},{1,2},{2,1},{3,0},{4,7},{5,6},{6,5},{7,4},{8,11},{9,10},{10,... | collective-permute-start | bytes 196616 | tf_op jit(solution)/shard_map/ppermute | solution.py:64
  99.5 5.9 %collective-permute-start.38 = (bf16[8,4096]{1,0:T(8,128)(2,1)S(1)}, bf16[8,4096]{1,0:T(8,128)(2,1)S(1)}, u32[]{:S(2)}, u32[]{:S(2)}) collective-permute-start(bf16[8,4096]{1,0:T(8,128)(2,1)S(1)} %add_convert_fusion.2.near), channel_id=1, source_target_pairs={{0,4},{1,5},{2,6},{3,7},{4,0},{5,1},{6,2},{7,3},{8,12},{9,13},{10,... | collective-permute-start | bytes 196616 | tf_op jit(solution)/shard_map/ppermute | solution.py:64
  107.0 5.9 %collective-permute-start.42 = (bf16[8,4096]{1,0:T(8,128)(2,1)S(1)}, bf16[8,4096]{1,0:T(8,128)(2,1)S(1)}, u32[]{:S(2)}, u32[]{:S(2)}) collective-permute-start(bf16[8,4096]{1,0:T(8,128)(2,1)S(1)} %pad_maximum_fusion.1.refs_0_), channel_id=1, source_target_pairs={{0,3},{1,2},{2,1},{3,0},{4,7},{5,6},{6,5},{7,4},{8,11},{9,10},{10,... | collective-permute-start | bytes 196616 | tf_op jit(solution)/shard_map/ppermute | solution.py:64
  107.7 5.5 %collective-permute-start.41 = (bf16[8,4096]{1,0:T(8,128)(2,1)S(1)}, bf16[8,4096]{1,0:T(8,128)(2,1)S(1)}, u32[]{:S(2)}, u32[]{:S(2)}) collective-permute-start(bf16[8,4096]{1,0:T(8,128)(2,1)S(1)} %pad_maximum_fusion.1.refs_0_), channel_id=1, source_target_pairs={{0,2},{1,3},{2,0},{3,1},{4,6},{5,7},{6,4},{7,5},{8,10},{9,11},{10,... | collective-permute-start | bytes 196616 | tf_op jit(solution)/shard_map/ppermute | solution.py:64
  118.8 5.0 %collective-permute-start.43 = (bf16[8,4096]{1,0:T(8,128)(2,1)S(1)}, bf16[8,4096]{1,0:T(8,128)(2,1)S(1)}, u32[]{:S(2)}, u32[]{:S(2)}) collective-permute-start(bf16[8,4096]{1,0:T(8,128)(2,1)S(1)} %get-tuple-element.139), channel_id=1, source_target_pairs={{0,1},{1,0},{2,3},{3,2},{4,5},{5,4},{6,7},{7,6},{8,9},{9,8},{10,11... | collective-permute-start | bytes 196616 | tf_op jit(solution)/shard_map/ppermute | solution.py:64
  120.2 5.2 %collective-permute-start.45 = (bf16[8,4096]{1,0:T(8,128)(2,1)S(1)}, bf16[8,4096]{1,0:T(8,128)(2,1)S(1)}, u32[]{:S(2)}, u32[]{:S(2)}) collective-permute-start(bf16[8,4096]{1,0:T(8,128)(2,1)S(1)} %get-tuple-element.141), channel_id=1, source_target_pairs={{0,3},{1,2},{2,1},{3,0},{4,7},{5,6},{6,5},{7,4},{8,11},{9,10},{10,... | collective-permute-start | bytes 196616 | tf_op jit(solution)/shard_map/ppermute | solution.py:64
  125.4 5.2 %collective-permute-start.46 = (bf16[8,4096]{1,0:T(8,128)(2,1)S(1)}, bf16[8,4096]{1,0:T(8,128)(2,1)S(1)}, u32[]{:S(2)}, u32[]{:S(2)}) collective-permute-start(bf16[8,4096]{1,0:T(8,128)(2,1)S(1)} %add_convert_fusion.1), channel_id=1, source_target_pairs={{0,4},{1,5},{2,6},{3,7},{4,0},{5,1},{6,2},{7,3},{8,12},{9,13},{10,... | collective-permute-start | bytes 196616 | tf_op jit(solution)/shard_map/ppermute | solution.py:64
  (52 other events, 243.6 us)

commit v5 on v4

--- a/solution.py
+++ b/solution.py
@@ -92,7 +92,7 @@
     for position, (stride, size) in enumerate(levels):
         if position > 0:
             parts = jnp.split(parts, size, axis=0)
-        parts = [parts[0]] + [partner(parts[k], k * stride, count) for k in range(1, size)]
+        parts = [parts[0]] + [partner(parts[k], k * stride, count) for k in range(size - 1, 0, -1)]
         if position == 0 and beside:
             parts[1], beside = lax.optimization_barrier((parts[1], beside))
         parts = total(parts).astype(BF16)
@@ -102,7 +102,7 @@
 def add_everywhere(parts, levels, count):
     for position, (stride, size) in enumerate(levels):
         if position == 0:
-            parts = [across(parts[k], k * stride, count) for k in range(size)]
+            parts = [across(parts[k], k * stride, count) for k in range(size - 1, -1, -1)]
         else:
             rows, columns = parts.shape
             split = parts.reshape(stride, size, rows // (stride * size), columns)
@@ -226,7 +226,8 @@
     rows_in, refs = refs[:parts], refs[parts:]
     held_taps, refs = refs[:taps], refs[taps:]
     in_proj, conv_weight, conv_bias, x_proj, x_out, act_out, *proj_outs = refs
-    x_part = jnp.dot(joined(rows_in), in_proj[...], preferred_element_type=F32)
+    weights = in_proj[...] if len(in_proj.shape) == 2 else in_proj[0]
+    x_part = jnp.dot(joined(rows_in), weights, preferred_element_type=F32)
     x_out[...] = x_part
     mixed = x_part * conv_weight[taps : taps + 1, :]
     for j in range(taps):
@@ -471,7 +472,14 @@
             ]
             + [((group_rows, x_proj.shape[0]), BF16)] * parts,
             [VMEM] * (parts + taps + 4),
-            (*rows_in, *window, held(in_x), conv_weight, conv_bias, held(x_proj)),
+            (
+                *rows_in,
+                *window,
+                held(in_x if step == 0 else in_proj),
+                conv_weight,
+                conv_bias,
+                held(x_proj),
+            ),
         )
         window = [*window[1:], x_part]
         proj = add_everywhere(proj, levels, count)

time: 133 us -> 128 us (0.962)
  waiting for transfers between devices: 53.5 us -> 48 us
    ppermute x29, waiting for transfers between devices: 39.6 us -> 35.1 us  [partner(): lax.ppermute(array, 'expert', [(i, i ^ distance) for i in range(count)])]
    unnamed x57 -> x55, local copies, waits for them, and re-layouts: 3.03 us -> 3.03 us
  transfers between devices with their start and end apart: 48 -> 48, of which waited for: 38 -> 40; matrix products, arithmetic and copies ran while one was open for 1% -> 1% of each run, Pallas kernels for 4% -> 4%
where the time goes in v5:
time: 128 us
  starting transfers between devices  52.6 us (41%)
  waiting for transfers between devices  48 us (38%)
  Pallas kernels  22.3 us (17%)
  local copies, waits for them, and re-layouts  3.61 us (3%)
    ppermute x29, starting transfers between devices, partner(): lax.ppermute(array, 'expert', [(i, i ^ distance) for i in range(count)])  41 us
    ppermute x29, waiting for transfers between devices, partner(): lax.ppermute(array, 'expert', [(i, i ^ distance) for i in range(count)])  35.1 us
    pallas_call x18, Pallas kernels, call(): pl.pallas_call(body, name=name, out_shape=[jax.ShapeDtypeStruct(s, d) for...  22.3 us
    ppermute x12, starting transfers between devices, across(): lax.ppermute(array, ('dp', 'expert'), pairs + [(b, a) for a, b in pairs])  10.4 us
    ppermute x12, waiting for transfers between devices, across(): lax.ppermute(array, ('dp', 'expert'), pairs + [(b, a) for a, b in pairs])  7.78 us
    ppermute x7, waiting for transfers between devices, other_core(): return lax.ppermute(array, 'dp', [(0, 1), (1, 0)])  5.15 us
    unnamed x55, local copies, waits for them, and re-layouts  3.03 us
  transfers between devices with their start and end apart: 48, of which 40 were waited for; matrix products, arithmetic and copies ran while one was open for 1% of the time, Pallas kernels for 4%

profile of v5, /device:TPU:0, one launch (start us, length us, event | category | flops | bytes accessed | tf_op | source)
XLA Modules:
  0.0 128.2 jit_solution(16338155677314738921)
XLA Ops:
  0.6 4.1 %collective-permute-start = (bf16[2,4,4096]{2,1,0:T(4,128)(2,1)}, bf16[2,4,4096]{2,1,0:T(4,128)(2,1)S(1)}, u32[]{:S(2)}, u32[]{:S(2)}) collective-permute-start(bf16[2,4,4096]{2,1,0:T(4,128)(2,1)} %own.1), channel_id=1, source_target_pairs={{0,4},{1,5},{2,6},{3,7},{4,0},{5,1},{6,2},{7,3},{8,12},{9,13},{10,... | collective-permute-start | bytes 196616 | tf_op jit(solution)/shard_map/ppermute | solution.py:64
  4.7 2.2 %fetch.1 = (bf16[4096,512]{1,0:T(8,128)(2,1)S(1)}, bf16[2,4,4096]{2,1,0:T(4,128)(2,1)S(1)}, f32[1,4096]{1,0:T(1,128)S(1)}) custom-call(bf16[2,4096,512]{2,1,0:T(8,128)(2,1)} %refs_4_.6, bf16[2,4,4096]{2,1,0:T(4,128)(2,1)} %own.1, f32[1,4096]{1,0:T(1,128)} %bitcast.40), custom_call_target="tpu_custom_call" | custom-call | flops 10000000000 | tf_op jit(solution)/shard_map/fetch/pallas_call | solution.py:42
  7.0 2.0 %copy-done.11 = bf16[4096,512]{1,0:T(8,128)(2,1)} copy-done((bf16[4096,512]{1,0:T(8,128)(2,1)}, bf16[4096,512]{1,0:T(8,128)(2,1)S(1)}, u32[]{:S(2)}) %copy-start.11) | copy-done | bytes 4194328
  9.2 2.6 %collective-permute-start.3 = (bf16[8,4096]{1,0:T(8,128)(2,1)S(1)}, bf16[8,4096]{1,0:T(8,128)(2,1)S(1)}, u32[]{:S(2)}, u32[]{:S(2)}) collective-permute-start(bf16[8,4096]{1,0:T(8,128)(2,1)S(1)} %get-tuple-element.86.refs_0_), channel_id=1, source_target_pairs={{0,3},{1,2},{2,1},{3,0},{4,7},{5,6},{6,5},{7,4},{8,11},{9,10},{10,... | collective-permute-start | bytes 196616 | tf_op jit(solution)/shard_map/ppermute | solution.py:64
  18.5 2.0 %collective-permute-start.7 = (bf16[32,288]{1,0:T(8,128)(2,1)S(1)}, bf16[32,288]{1,0:T(8,128)(2,1)S(1)}, u32[]{:S(2)}, u32[]{:S(2)}) collective-permute-start(bf16[32,288]{1,0:T(8,128)(2,1)S(1)} %get-tuple-element.94), channel_id=1, source_target_pairs={{0,11},{1,10},{2,9},{3,8},{4,15},{5,14},{6,13},{7,12},{11,0},{10,1... | collective-permute-start | bytes 55304 | tf_op jit(solution)/shard_map/ppermute | solution.py:73
  33.6 2.0 %collective-permute-done.13 = bf16[8,4096]{1,0:T(8,128)(2,1)S(1)} collective-permute-done((bf16[8,4096]{1,0:T(8,128)(2,1)S(1)}, bf16[8,4096]{1,0:T(8,128)(2,1)S(1)}, u32[]{:S(2)}, u32[]{:S(2)}) %collective-permute-start.13) | collective-permute-done | bytes 65568 | tf_op jit(solution)/shard_map/ppermute | solution.py:64
  36.8 1.9 %collective-permute-start.16 = (bf16[8,4096]{1,0:T(8,128)(2,1)S(1)}, bf16[8,4096]{1,0:T(8,128)(2,1)S(1)}, u32[]{:S(2)}, u32[]{:S(2)}) collective-permute-start(bf16[8,4096]{1,0:T(8,128)(2,1)S(1)} %add_convert_fusion.5.near), channel_id=1, source_target_pairs={{0,4},{1,5},{2,6},{3,7},{4,0},{5,1},{6,2},{7,3},{8,12},{9,13},{10,... | collective-permute-start | bytes 196616 | tf_op jit(solution)/shard_map/ppermute | solution.py:64
  39.5 2.8 %collective-permute-done.16.far = bf16[8,4096]{1,0:T(8,128)(2,1)S(1)} collective-permute-done((bf16[8,4096]{1,0:T(8,128)(2,1)S(1)}, bf16[8,4096]{1,0:T(8,128)(2,1)S(1)}, u32[]{:S(2)}, u32[]{:S(2)}) %collective-permute-start.16) | collective-permute-done | bytes 65568 | tf_op jit(solution)/shard_map/ppermute | solution.py:64
  43.9 2.0 %collective-permute-start.20 = (bf16[8,4096]{1,0:T(8,128)(2,1)S(1)}, bf16[8,4096]{1,0:T(8,128)(2,1)S(1)}, u32[]{:S(2)}, u32[]{:S(2)}) collective-permute-start(bf16[8,4096]{1,0:T(8,128)(2,1)S(1)} %pad_maximum_fusion.refs_0_), channel_id=1, source_target_pairs={{0,3},{1,2},{2,1},{3,0},{4,7},{5,6},{6,5},{7,4},{8,11},{9,10},{10,... | collective-permute-start | bytes 196616 | tf_op jit(solution)/shard_map/ppermute | solution.py:64
  47.4 2.1 %collective-permute-done.20.refs_3_ = bf16[8,4096]{1,0:T(8,128)(2,1)S(1)} collective-permute-done((bf16[8,4096]{1,0:T(8,128)(2,1)S(1)}, bf16[8,4096]{1,0:T(8,128)(2,1)S(1)}, u32[]{:S(2)}, u32[]{:S(2)}) %collective-permute-start.20) | collective-permute-done | bytes 65568 | tf_op jit(solution)/shard_map/ppermute | solution.py:64
  50.6 4.9 %experts.2 = (bf16[8,4096]{1,0:T(8,128)(2,1)S(1)}, bf16[8,4096]{1,0:T(8,128)(2,1)S(1)}, bf16[8,4096]{1,0:T(8,128)(2,1)S(1)}, bf16[8,4096]{1,0:T(8,128)(2,1)S(1)}) custom-call(bf16[8,4096]{1,0:T(8,128)(2,1)S(1)} %pad_maximum_fusion.refs_0_, bf16[8,4096]{1,0:T(8,128)(2,1)S(1)} %collective-permute-done.18.refs_1_, ...), custom_call_target="tpu_custom_call" | custom-call | flops 10000000000 | tf_op jit(solution)/shard_map/experts/pallas_call | solution.py:42
  55.5 1.9 %collective-permute-start.21 = (bf16[8,4096]{1,0:T(8,128)(2,1)S(1)}, bf16[8,4096]{1,0:T(8,128)(2,1)S(1)}, u32[]{:S(2)}, u32[]{:S(2)}) collective-permute-start(bf16[8,4096]{1,0:T(8,128)(2,1)S(1)} %get-tuple-element.114), channel_id=1, source_target_pairs={{0,3},{1,2},{2,1},{3,0},{4,7},{5,6},{6,5},{7,4},{8,11},{9,10},{10,... | collective-permute-start | bytes 196616 | tf_op jit(solution)/shard_map/ppermute | solution.py:64
  59.0 2.0 %collective-permute-done.21 = bf16[8,4096]{1,0:T(8,128)(2,1)S(1)} collective-permute-done((bf16[8,4096]{1,0:T(8,128)(2,1)S(1)}, bf16[8,4096]{1,0:T(8,128)(2,1)S(1)}, u32[]{:S(2)}, u32[]{:S(2)}) %collective-permute-start.21) | collective-permute-done | bytes 65568 | tf_op jit(solution)/shard_map/ppermute | solution.py:64
  64.3 3.3 %collective-permute-done.24 = bf16[8,4096]{1,0:T(8,128)(2,1)S(1)} collective-permute-done((bf16[8,4096]{1,0:T(8,128)(2,1)S(1)}, bf16[8,4096]{1,0:T(8,128)(2,1)S(1)}, u32[]{:S(2)}, u32[]{:S(2)}) %collective-permute-start.24) | collective-permute-done | bytes 65568 | tf_op jit(solution)/shard_map/ppermute | solution.py:64
  69.5 2.0 %collective-permute-start.28 = (bf16[8,4096]{1,0:T(8,128)(2,1)S(1)}, bf16[8,4096]{1,0:T(8,128)(2,1)S(1)}, u32[]{:S(2)}, u32[]{:S(2)}) collective-permute-start(bf16[8,4096]{1,0:T(8,128)(2,1)S(1)} %get-tuple-element.120.refs_0_), channel_id=1, source_target_pairs={{0,3},{1,2},{2,1},{3,0},{4,7},{5,6},{6,5},{7,4},{8,11},{9,10},{10,... | collective-permute-start | bytes 196616 | tf_op jit(solution)/shard_map/ppermute | solution.py:64
  73.0 2.1 %collective-permute-done.28.refs_3_ = bf16[8,4096]{1,0:T(8,128)(2,1)S(1)} collective-permute-done((bf16[8,4096]{1,0:T(8,128)(2,1)S(1)}, bf16[8,4096]{1,0:T(8,128)(2,1)S(1)}, u32[]{:S(2)}, u32[]{:S(2)}) %collective-permute-start.28) | collective-permute-done | bytes 65568 | tf_op jit(solution)/shard_map/ppermute | solution.py:64
  92.4 2.4 %collective-permute-done.35 = bf16[8,4096]{1,0:T(8,128)(2,1)S(1)} collective-permute-done((bf16[8,4096]{1,0:T(8,128)(2,1)S(1)}, bf16[8,4096]{1,0:T(8,128)(2,1)S(1)}, u32[]{:S(2)}, u32[]{:S(2)}) %collective-permute-start.35) | collective-permute-done | bytes 65568 | tf_op jit(solution)/shard_map/ppermute | solution.py:64
  95.5 2.4 %collective-permute-start.38 = (bf16[8,4096]{1,0:T(8,128)(2,1)S(1)}, bf16[8,4096]{1,0:T(8,128)(2,1)S(1)}, u32[]{:S(2)}, u32[]{:S(2)}) collective-permute-start(bf16[8,4096]{1,0:T(8,128)(2,1)S(1)} %add_convert_fusion.2.near), channel_id=1, source_target_pairs={{0,4},{1,5},{2,6},{3,7},{4,0},{5,1},{6,2},{7,3},{8,12},{9,13},{10,... | collective-permute-start | bytes 196616 | tf_op jit(solution)/shard_map/ppermute | solution.py:64
  98.0 2.8 %collective-permute-done.38.far = bf16[8,4096]{1,0:T(8,128)(2,1)S(1)} collective-permute-done((bf16[8,4096]{1,0:T(8,128)(2,1)S(1)}, bf16[8,4096]{1,0:T(8,128)(2,1)S(1)}, u32[]{:S(2)}, u32[]{:S(2)}) %collective-permute-start.38) | collective-permute-done | bytes 65568 | tf_op jit(solution)/shard_map/ppermute | solution.py:64
  102.4 2.0 %collective-permute-start.42 = (bf16[8,4096]{1,0:T(8,128)(2,1)S(1)}, bf16[8,4096]{1,0:T(8,128)(2,1)S(1)}, u32[]{:S(2)}, u32[]{:S(2)}) collective-permute-start(bf16[8,4096]{1,0:T(8,128)(2,1)S(1)} %pad_maximum_fusion.1.refs_0_), channel_id=1, source_target_pairs={{0,3},{1,2},{2,1},{3,0},{4,7},{5,6},{6,5},{7,4},{8,11},{9,10},{10,... | collective-permute-start | bytes 196616 | tf_op jit(solution)/shard_map/ppermute | solution.py:64
  105.9 2.1 %collective-permute-done.42.refs_3_ = bf16[8,4096]{1,0:T(8,128)(2,1)S(1)} collective-permute-done((bf16[8,4096]{1,0:T(8,128)(2,1)S(1)}, bf16[8,4096]{1,0:T(8,128)(2,1)S(1)}, u32[]{:S(2)}, u32[]{:S(2)}) %collective-permute-start.42) | collective-permute-done | bytes 65568 | tf_op jit(solution)/shard_map/ppermute | solution.py:64
  109.4 4.8 %experts.3 = (bf16[8,4096]{1,0:T(8,128)(2,1)S(1)}, bf16[8,4096]{1,0:T(8,128)(2,1)S(1)}, bf16[8,4096]{1,0:T(8,128)(2,1)S(1)}, bf16[8,4096]{1,0:T(8,128)(2,1)S(1)}) custom-call(bf16[8,4096]{1,0:T(8,128)(2,1)S(1)} %pad_maximum_fusion.1.refs_0_, bf16[8,4096]{1,0:T(8,128)(2,1)S(1)} %collective-permute-done.40.refs_1_, ...), custom_call_target="tpu_custom_call" | custom-call | flops 10000000000 | tf_op jit(solution)/shard_map/experts/pallas_call | solution.py:42
  120.8 2.6 %collective-permute-start.46 = (bf16[8,4096]{1,0:T(8,128)(2,1)S(1)}, bf16[8,4096]{1,0:T(8,128)(2,1)S(1)}, u32[]{:S(2)}, u32[]{:S(2)}) collective-permute-start(bf16[8,4096]{1,0:T(8,128)(2,1)S(1)} %add_convert_fusion.1), channel_id=1, source_target_pairs={{0,4},{1,5},{2,6},{3,7},{4,0},{5,1},{6,2},{7,3},{8,12},{9,13},{10,... | collective-permute-start | bytes 196616 | tf_op jit(solution)/shard_map/ppermute | solution.py:64
  123.4 2.7 %collective-permute-done.46 = bf16[8,4096]{1,0:T(8,128)(2,1)S(1)} collective-permute-done((bf16[8,4096]{1,0:T(8,128)(2,1)S(1)}, bf16[8,4096]{1,0:T(8,128)(2,1)S(1)}, u32[]{:S(2)}, u32[]{:S(2)}) %collective-permute-start.46) | collective-permute-done | bytes 65568 | tf_op jit(solution)/shard_map/ppermute | solution.py:64
  (178 shorter events, 65.4 us)
Async XLA Ops:
  0.6 8.3 %collective-permute-start = (bf16[2,4,4096]{2,1,0:T(4,128)(2,1)}, bf16[2,4,4096]{2,1,0:T(4,128)(2,1)S(1)}, u32[]{:S(2)}, u32[]{:S(2)}) collective-permute-start(bf16[2,4,4096]{2,1,0:T(4,128)(2,1)} %own.1), channel_id=1, source_target_pairs={{0,4},{1,5},{2,6},{3,7},{4,0},{5,1},{6,2},{7,3},{8,12},{9,13},{10,... | collective-permute-start | bytes 196616 | tf_op jit(solution)/shard_map/ppermute | solution.py:64
  9.2 6.7 %collective-permute-start.3 = (bf16[8,4096]{1,0:T(8,128)(2,1)S(1)}, bf16[8,4096]{1,0:T(8,128)(2,1)S(1)}, u32[]{:S(2)}, u32[]{:S(2)}) collective-permute-start(bf16[8,4096]{1,0:T(8,128)(2,1)S(1)} %get-tuple-element.86.refs_0_), channel_id=1, source_target_pairs={{0,3},{1,2},{2,1},{3,0},{4,7},{5,6},{6,5},{7,4},{8,11},{9,10},{10,... | collective-permute-start | bytes 196616 | tf_op jit(solution)/shard_map/ppermute | solution.py:64
  11.8 4.3 %collective-permute-start.2 = (bf16[8,4096]{1,0:T(8,128)(2,1)S(1)}, bf16[8,4096]{1,0:T(8,128)(2,1)S(1)}, u32[]{:S(2)}, u32[]{:S(2)}) collective-permute-start(bf16[8,4096]{1,0:T(8,128)(2,1)S(1)} %get-tuple-element.86.refs_0_), channel_id=1, source_target_pairs={{0,2},{1,3},{2,0},{3,1},{4,6},{5,7},{6,4},{7,5},{8,10},{9,11},{10,... | collective-permute-start | bytes 196616 | tf_op jit(solution)/shard_map/ppermute | solution.py:64
  13.1 4.3 %collective-permute-start.1 = (bf16[8,4096]{1,0:T(8,128)(2,1)S(1)}, bf16[8,4096]{1,0:T(8,128)(2,1)S(1)}, u32[]{:S(2)}, u32[]{:S(2)}) collective-permute-start(bf16[8,4096]{1,0:T(8,128)(2,1)S(1)} %get-tuple-element.86.refs_0_), channel_id=1, source_target_pairs={{0,1},{1,0},{2,3},{3,2},{4,5},{5,4},{6,7},{7,6},{8,9},{9,8},{10,11... | collective-permute-start | bytes 196616 | tf_op jit(solution)/shard_map/ppermute | solution.py:64
  30.1 5.5 %collective-permute-start.13 = (bf16[8,4096]{1,0:T(8,128)(2,1)S(1)}, bf16[8,4096]{1,0:T(8,128)(2,1)S(1)}, u32[]{:S(2)}, u32[]{:S(2)}) collective-permute-start(bf16[8,4096]{1,0:T(8,128)(2,1)S(1)} %get-tuple-element.102), channel_id=1, source_target_pairs={{0,3},{1,2},{2,1},{3,0},{4,7},{5,6},{6,5},{7,4},{8,11},{9,10},{10,... | collective-permute-start | bytes 196616 | tf_op jit(solution)/shard_map/ppermute | solution.py:64
  32.0 4.3 %collective-permute-start.14 = (bf16[8,4096]{1,0:T(8,128)(2,1)S(1)}, bf16[8,4096]{1,0:T(8,128)(2,1)S(1)}, u32[]{:S(2)}, u32[]{:S(2)}) collective-permute-start(bf16[8,4096]{1,0:T(8,128)(2,1)S(1)} %get-tuple-element.104), channel_id=1, source_target_pairs={{0,2},{1,3},{2,0},{3,1},{4,6},{5,7},{6,4},{7,5},{8,10},{9,11},{10,... | collective-permute-start | bytes 196616 | tf_op jit(solution)/shard_map/ppermute | solution.py:64
  32.4 4.3 %collective-permute-start.15 = (bf16[8,4096]{1,0:T(8,128)(2,1)S(1)}, bf16[8,4096]{1,0:T(8,128)(2,1)S(1)}, u32[]{:S(2)}, u32[]{:S(2)}) collective-permute-start(bf16[8,4096]{1,0:T(8,128)(2,1)S(1)} %get-tuple-element.105), channel_id=1, source_target_pairs={{0,1},{1,0},{2,3},{3,2},{4,5},{5,4},{6,7},{7,6},{8,9},{9,8},{10,11... | collective-permute-start | bytes 196616 | tf_op jit(solution)/shard_map/ppermute | solution.py:64
  36.8 5.5 %collective-permute-start.16 = (bf16[8,4096]{1,0:T(8,128)(2,1)S(1)}, bf16[8,4096]{1,0:T(8,128)(2,1)S(1)}, u32[]{:S(2)}, u32[]{:S(2)}) collective-permute-start(bf16[8,4096]{1,0:T(8,128)(2,1)S(1)} %add_convert_fusion.5.near), channel_id=1, source_target_pairs={{0,4},{1,5},{2,6},{3,7},{4,0},{5,1},{6,2},{7,3},{8,12},{9,13},{10,... | collective-permute-start | bytes 196616 | tf_op jit(solution)/shard_map/ppermute | solution.py:64
  43.9 5.6 %collective-permute-start.20 = (bf16[8,4096]{1,0:T(8,128)(2,1)S(1)}, bf16[8,4096]{1,0:T(8,128)(2,1)S(1)}, u32[]{:S(2)}, u32[]{:S(2)}) collective-permute-start(bf16[8,4096]{1,0:T(8,128)(2,1)S(1)} %pad_maximum_fusion.refs_0_), channel_id=1, source_target_pairs={{0,3},{1,2},{2,1},{3,0},{4,7},{5,6},{6,5},{7,4},{8,11},{9,10},{10,... | collective-permute-start | bytes 196616 | tf_op jit(solution)/shard_map/ppermute | solution.py:64
  45.9 4.3 %collective-permute-start.19 = (bf16[8,4096]{1,0:T(8,128)(2,1)S(1)}, bf16[8,4096]{1,0:T(8,128)(2,1)S(1)}, u32[]{:S(2)}, u32[]{:S(2)}) collective-permute-start(bf16[8,4096]{1,0:T(8,128)(2,1)S(1)} %pad_maximum_fusion.refs_0_), channel_id=1, source_target_pairs={{0,2},{1,3},{2,0},{3,1},{4,6},{5,7},{6,4},{7,5},{8,10},{9,11},{10,... | collective-permute-start | bytes 196616 | tf_op jit(solution)/shard_map/ppermute | solution.py:64
  46.3 4.3 %collective-permute-start.18 = (bf16[8,4096]{1,0:T(8,128)(2,1)S(1)}, bf16[8,4096]{1,0:T(8,128)(2,1)S(1)}, u32[]{:S(2)}, u32[]{:S(2)}) collective-permute-start(bf16[8,4096]{1,0:T(8,128)(2,1)S(1)} %pad_maximum_fusion.refs_0_), channel_id=1, source_target_pairs={{0,1},{1,0},{2,3},{3,2},{4,5},{5,4},{6,7},{7,6},{8,9},{9,8},{10,11... | collective-permute-start | bytes 196616 | tf_op jit(solution)/shard_map/ppermute | solution.py:64
  55.5 5.5 %collective-permute-start.21 = (bf16[8,4096]{1,0:T(8,128)(2,1)S(1)}, bf16[8,4096]{1,0:T(8,128)(2,1)S(1)}, u32[]{:S(2)}, u32[]{:S(2)}) collective-permute-start(bf16[8,4096]{1,0:T(8,128)(2,1)S(1)} %get-tuple-element.114), channel_id=1, source_target_pairs={{0,3},{1,2},{2,1},{3,0},{4,7},{5,6},{6,5},{7,4},{8,11},{9,10},{10,... | collective-permute-start | bytes 196616 | tf_op jit(solution)/shard_map/ppermute | solution.py:64
  62.4 5.2 %collective-permute-start.24 = (bf16[8,4096]{1,0:T(8,128)(2,1)S(1)}, bf16[8,4096]{1,0:T(8,128)(2,1)S(1)}, u32[]{:S(2)}, u32[]{:S(2)}) collective-permute-start(bf16[8,4096]{1,0:T(8,128)(2,1)S(1)} %add_convert_fusion.4), channel_id=1, source_target_pairs={{0,4},{1,5},{2,6},{3,7},{4,0},{5,1},{6,2},{7,3},{8,12},{9,13},{10,... | collective-permute-start | bytes 196616 | tf_op jit(solution)/shard_map/ppermute | solution.py:64
  69.5 5.6 %collective-permute-start.28 = (bf16[8,4096]{1,0:T(8,128)(2,1)S(1)}, bf16[8,4096]{1,0:T(8,128)(2,1)S(1)}, u32[]{:S(2)}, u32[]{:S(2)}) collective-permute-start(bf16[8,4096]{1,0:T(8,128)(2,1)S(1)} %get-tuple-element.120.refs_0_), channel_id=1, source_target_pairs={{0,3},{1,2},{2,1},{3,0},{4,7},{5,6},{6,5},{7,4},{8,11},{9,10},{10,... | collective-permute-start | bytes 196616 | tf_op jit(solution)/shard_map/ppermute | solution.py:64
  71.4 4.3 %collective-permute-start.27 = (bf16[8,4096]{1,0:T(8,128)(2,1)S(1)}, bf16[8,4096]{1,0:T(8,128)(2,1)S(1)}, u32[]{:S(2)}, u32[]{:S(2)}) collective-permute-start(bf16[8,4096]{1,0:T(8,128)(2,1)S(1)} %get-tuple-element.120.refs_0_), channel_id=1, source_target_pairs={{0,2},{1,3},{2,0},{3,1},{4,6},{5,7},{6,4},{7,5},{8,10},{9,11},{10,... | collective-permute-start | bytes 196616 | tf_op jit(solution)/shard_map/ppermute | solution.py:64
  71.9 4.3 %collective-permute-start.26 = (bf16[8,4096]{1,0:T(8,128)(2,1)S(1)}, bf16[8,4096]{1,0:T(8,128)(2,1)S(1)}, u32[]{:S(2)}, u32[]{:S(2)}) collective-permute-start(bf16[8,4096]{1,0:T(8,128)(2,1)S(1)} %get-tuple-element.120.refs_0_), channel_id=1, source_target_pairs={{0,1},{1,0},{2,3},{3,2},{4,5},{5,4},{6,7},{7,6},{8,9},{9,8},{10,11... | collective-permute-start | bytes 196616 | tf_op jit(solution)/shard_map/ppermute | solution.py:64
  89.0 5.9 %collective-permute-start.35 = (bf16[8,4096]{1,0:T(8,128)(2,1)S(1)}, bf16[8,4096]{1,0:T(8,128)(2,1)S(1)}, u32[]{:S(2)}, u32[]{:S(2)}) collective-permute-start(bf16[8,4096]{1,0:T(8,128)(2,1)S(1)} %get-tuple-element.131), channel_id=1, source_target_pairs={{0,3},{1,2},{2,1},{3,0},{4,7},{5,6},{6,5},{7,4},{8,11},{9,10},{10,... | collective-permute-start | bytes 196616 | tf_op jit(solution)/shard_map/ppermute | solution.py:64
  90.7 4.3 %collective-permute-start.36 = (bf16[8,4096]{1,0:T(8,128)(2,1)S(1)}, bf16[8,4096]{1,0:T(8,128)(2,1)S(1)}, u32[]{:S(2)}, u32[]{:S(2)}) collective-permute-start(bf16[8,4096]{1,0:T(8,128)(2,1)S(1)} %get-tuple-element.132), channel_id=1, source_target_pairs={{0,2},{1,3},{2,0},{3,1},{4,6},{5,7},{6,4},{7,5},{8,10},{9,11},{10,... | collective-permute-start | bytes 196616 | tf_op jit(solution)/shard_map/ppermute | solution.py:64
  91.2 4.3 %collective-permute-start.37 = (bf16[8,4096]{1,0:T(8,128)(2,1)S(1)}, bf16[8,4096]{1,0:T(8,128)(2,1)S(1)}, u32[]{:S(2)}, u32[]{:S(2)}) collective-permute-start(bf16[8,4096]{1,0:T(8,128)(2,1)S(1)} %get-tuple-element.133), channel_id=1, source_target_pairs={{0,1},{1,0},{2,3},{3,2},{4,5},{5,4},{6,7},{7,6},{8,9},{9,8},{10,11... | collective-permute-start | bytes 196616 | tf_op jit(solution)/shard_map/ppermute | solution.py:64
  95.5 5.2 %collective-permute-start.38 = (bf16[8,4096]{1,0:T(8,128)(2,1)S(1)}, bf16[8,4096]{1,0:T(8,128)(2,1)S(1)}, u32[]{:S(2)}, u32[]{:S(2)}) collective-permute-start(bf16[8,4096]{1,0:T(8,128)(2,1)S(1)} %add_convert_fusion.2.near), channel_id=1, source_target_pairs={{0,4},{1,5},{2,6},{3,7},{4,0},{5,1},{6,2},{7,3},{8,12},{9,13},{10,... | collective-permute-start | bytes 196616 | tf_op jit(solution)/shard_map/ppermute | solution.py:64
  102.4 5.6 %collective-permute-start.42 = (bf16[8,4096]{1,0:T(8,128)(2,1)S(1)}, bf16[8,4096]{1,0:T(8,128)(2,1)S(1)}, u32[]{:S(2)}, u32[]{:S(2)}) collective-permute-start(bf16[8,4096]{1,0:T(8,128)(2,1)S(1)} %pad_maximum_fusion.1.refs_0_), channel_id=1, source_target_pairs={{0,3},{1,2},{2,1},{3,0},{4,7},{5,6},{6,5},{7,4},{8,11},{9,10},{10,... | collective-permute-start | bytes 196616 | tf_op jit(solution)/shard_map/ppermute | solution.py:64
  104.4 4.3 %collective-permute-start.41 = (bf16[8,4096]{1,0:T(8,128)(2,1)S(1)}, bf16[8,4096]{1,0:T(8,128)(2,1)S(1)}, u32[]{:S(2)}, u32[]{:S(2)}) collective-permute-start(bf16[8,4096]{1,0:T(8,128)(2,1)S(1)} %pad_maximum_fusion.1.refs_0_), channel_id=1, source_target_pairs={{0,2},{1,3},{2,0},{3,1},{4,6},{5,7},{6,4},{7,5},{8,10},{9,11},{10,... | collective-permute-start | bytes 196616 | tf_op jit(solution)/shard_map/ppermute | solution.py:64
  114.2 5.3 %collective-permute-start.43 = (bf16[8,4096]{1,0:T(8,128)(2,1)S(1)}, bf16[8,4096]{1,0:T(8,128)(2,1)S(1)}, u32[]{:S(2)}, u32[]{:S(2)}) collective-permute-start(bf16[8,4096]{1,0:T(8,128)(2,1)S(1)} %get-tuple-element.139), channel_id=1, source_target_pairs={{0,3},{1,2},{2,1},{3,0},{4,7},{5,6},{6,5},{7,4},{8,11},{9,10},{10,... | collective-permute-start | bytes 196616 | tf_op jit(solution)/shard_map/ppermute | solution.py:64
  120.8 5.2 %collective-permute-start.46 = (bf16[8,4096]{1,0:T(8,128)(2,1)S(1)}, bf16[8,4096]{1,0:T(8,128)(2,1)S(1)}, u32[]{:S(2)}, u32[]{:S(2)}) collective-permute-start(bf16[8,4096]{1,0:T(8,128)(2,1)S(1)} %add_convert_fusion.1), channel_id=1, source_target_pairs={{0,4},{1,5},{2,6},{3,7},{4,0},{5,1},{6,2},{7,3},{8,12},{9,13},{10,... | collective-permute-start | bytes 196616 | tf_op jit(solution)/shard_map/ppermute | solution.py:64
  (51 other events, 238.6 us)

commit v6 on v5

--- a/solution.py
+++ b/solution.py
@@ -416,10 +416,9 @@
         (own_input, peer_input, mamba_gain),
     )
     moe_gain = held(moe_gain.reshape(1, width))
-    normed, layer_input, prompt_ssm, prompt_conv, route_ids, route_weights = (
-        lax.optimization_barrier(
-            (normed, layer_input, prompt_ssm, prompt_conv, route_ids, route_weights)
-        )
+    in_x, prompt_ssm, prompt_conv = lax.optimization_barrier((in_x, prompt_ssm, prompt_conv))
+    normed, route_ids, route_weights = lax.optimization_barrier(
+        (normed, route_ids, route_weights)
     )
     rows_in = spread(normed, levels, count)
     high = lax.reduce_precision(route_weights, 8, 7)

time: 128 us -> 137 us (1.070)
  waiting for transfers between devices: 48 us -> 56.4 us
  local copies, waits for them, and re-layouts: 3.61 us -> 10.3 us
  starting transfers between devices: 52.6 us -> 46.5 us
    ppermute x29, waiting for transfers between devices: 35.1 us -> 45.7 us  [partner(): lax.ppermute(array, 'expert', [(i, i ^ distance) for i in range(count)])]
    unnamed x55, local copies, waits for them, and re-layouts: 3.03 us -> 9.74 us
    ppermute x29, starting transfers between devices: 41 us -> 35.6 us  [partner(): lax.ppermute(array, 'expert', [(i, i ^ distance) for i in range(count)])]
    ppermute x12, waiting for transfers between devices: 7.78 us -> 6.29 us  [across(): lax.ppermute(array, ('dp', 'expert'), pairs + [(b, a) for a, b in pairs])]
  transfers between devices with their start and end apart: 48 -> 48, of which waited for: 40 -> 39; matrix products, arithmetic and copies ran while one was open for 1% -> 1% of each run, Pallas kernels for 4% -> 2%
where the time goes in v6:
time: 137 us
  waiting for transfers between devices  56.4 us (41%)
  starting transfers between devices  46.5 us (34%)
  Pallas kernels  22.4 us (16%)
  local copies, waits for them, and re-layouts  10.3 us (8%)
    ppermute x29, waiting for transfers between devices, partner(): lax.ppermute(array, 'expert', [(i, i ^ distance) for i in range(count)])  45.7 us
    ppermute x29, starting transfers between devices, partner(): lax.ppermute(array, 'expert', [(i, i ^ distance) for i in range(count)])  35.6 us
    pallas_call x18, Pallas kernels, call(): pl.pallas_call(body, name=name, out_shape=[jax.ShapeDtypeStruct(s, d) for...  22.4 us
    ppermute x12, starting transfers between devices, across(): lax.ppermute(array, ('dp', 'expert'), pairs + [(b, a) for a, b in pairs])  9.95 us
    unnamed x55, local copies, waits for them, and re-layouts  9.74 us
    ppermute x12, waiting for transfers between devices, across(): lax.ppermute(array, ('dp', 'expert'), pairs + [(b, a) for a, b in pairs])  6.29 us
    ppermute x7, waiting for transfers between devices, other_core(): return lax.ppermute(array, 'dp', [(0, 1), (1, 0)])  4.37 us
  transfers between devices with their start and end apart: 48, of which 39 were waited for; matrix products, arithmetic and copies ran while one was open for 1% of the time, Pallas kernels for 2%

profile of v6, /device:TPU:0, one launch (start us, length us, event | category | flops | bytes accessed | tf_op | source)
XLA Modules:
  0.0 137.3 jit_solution(16921511957464956987)
XLA Ops:
  0.7 2.3 %fetch.1 = (bf16[4096,512]{1,0:T(8,128)(2,1)S(1)}, bf16[2,4,4096]{2,1,0:T(4,128)(2,1)S(1)}, f32[1,4096]{1,0:T(1,128)S(1)}) custom-call(bf16[2,4096,512]{2,1,0:T(8,128)(2,1)} %refs_4_.6, bf16[2,4,4096]{2,1,0:T(4,128)(2,1)} %own.1, f32[1,4096]{1,0:T(1,128)} %bitcast.38), custom_call_target="tpu_custom_call" | custom-call | flops 10000000000 | tf_op jit(solution)/shard_map/fetch/pallas_call | solution.py:42
  2.9 2.0 %copy-done.12 = bf16[4096,512]{1,0:T(8,128)(2,1)} copy-done((bf16[4096,512]{1,0:T(8,128)(2,1)}, bf16[4096,512]{1,0:T(8,128)(2,1)S(1)}, u32[]{:S(2)}) %copy-start.12) | copy-done | bytes 4194328
  5.5 3.7 %collective-permute-start = (bf16[2,4,4096]{2,1,0:T(4,128)(2,1)S(1)}, bf16[2,4,4096]{2,1,0:T(4,128)(2,1)S(1)}, u32[]{:S(2)}, u32[]{:S(2)}) collective-permute-start(bf16[2,4,4096]{2,1,0:T(4,128)(2,1)S(1)} %copy-done.18), channel_id=1, source_target_pairs={{0,4},{1,5},{2,6},{3,7},{4,0},{5,1},{6,2},{7,3},{8,12},{9,13},{10,... | collective-permute-start | bytes 196616 | tf_op jit(solution)/shard_map/ppermute | solution.py:64
  9.3 3.9 %collective-permute-done.peer = bf16[2,4,4096]{2,1,0:T(4,128)(2,1)S(1)} collective-permute-done((bf16[2,4,4096]{2,1,0:T(4,128)(2,1)S(1)}, bf16[2,4,4096]{2,1,0:T(4,128)(2,1)S(1)}, u32[]{:S(2)}, u32[]{:S(2)}) %collective-permute-start) | collective-permute-done | bytes 65568 | tf_op jit(solution)/shard_map/ppermute | solution.py:64
  20.8 2.2 %copy-done.13 = bf16[4096,512]{1,0:T(8,128)(2,1)S(1)} copy-done((bf16[4096,512]{1,0:T(8,128)(2,1)S(1)}, bf16[4096,512]{1,0:T(8,128)(2,1)}, u32[]{:S(2)}) %copy-start.13) | copy-done | bytes 4194328
  29.2 2.2 %collective-permute-start.12 = (bf16[32,290]{1,0:T(8,128)(2,1)S(1)}, bf16[32,290]{1,0:T(8,128)(2,1)S(1)}, u32[]{:S(2)}, u32[]{:S(2)}) collective-permute-start(bf16[32,290]{1,0:T(8,128)(2,1)S(1)} %pad_maximum_fusion.2), channel_id=1, source_target_pairs={{0,12},{1,13},{2,14},{3,15},{4,8},{5,9},{6,10},{7,11},{12,0},{13,1... | collective-permute-start | bytes 55688 | tf_op jit(solution)/shard_map/ppermute | solution.py:73
  31.4 3.4 %copy-done = bf16[2,4096,512]{2,1,0:T(8,128)(2,1)S(1)} copy-done((bf16[2,4096,512]{2,1,0:T(8,128)(2,1)S(1)}, bf16[2,4096,512]{2,1,0:T(8,128)(2,1)}, u32[]{:S(2)}) %copy-start) | copy-done | bytes 8388632
  38.5 2.9 %collective-permute-start.13 = (bf16[8,4096]{1,0:T(8,128)(2,1)S(1)}, bf16[8,4096]{1,0:T(8,128)(2,1)S(1)}, u32[]{:S(2)}, u32[]{:S(2)}) collective-permute-start(bf16[8,4096]{1,0:T(8,128)(2,1)S(1)} %get-tuple-element.104), channel_id=1, source_target_pairs={{0,3},{1,2},{2,1},{3,0},{4,7},{5,6},{6,5},{7,4},{8,11},{9,10},{10,... | collective-permute-start | bytes 196616 | tf_op jit(solution)/shard_map/ppermute | solution.py:64
  47.5 3.8 %collective-permute-done.16.far = bf16[8,4096]{1,0:T(8,128)(2,1)S(1)} collective-permute-done((bf16[8,4096]{1,0:T(8,128)(2,1)S(1)}, bf16[8,4096]{1,0:T(8,128)(2,1)S(1)}, u32[]{:S(2)}, u32[]{:S(2)}) %collective-permute-start.16) | collective-permute-done | bytes 65568 | tf_op jit(solution)/shard_map/ppermute | solution.py:64
  52.9 2.0 %collective-permute-start.20 = (bf16[8,4096]{1,0:T(8,128)(2,1)S(1)}, bf16[8,4096]{1,0:T(8,128)(2,1)S(1)}, u32[]{:S(2)}, u32[]{:S(2)}) collective-permute-start(bf16[8,4096]{1,0:T(8,128)(2,1)S(1)} %pad_maximum_fusion.refs_0_), channel_id=1, source_target_pairs={{0,3},{1,2},{2,1},{3,0},{4,7},{5,6},{6,5},{7,4},{8,11},{9,10},{10,... | collective-permute-start | bytes 196616 | tf_op jit(solution)/shard_map/ppermute | solution.py:64
  59.7 4.8 %experts.2 = (bf16[8,4096]{1,0:T(8,128)(2,1)S(1)}, bf16[8,4096]{1,0:T(8,128)(2,1)S(1)}, bf16[8,4096]{1,0:T(8,128)(2,1)S(1)}, bf16[8,4096]{1,0:T(8,128)(2,1)S(1)}) custom-call(bf16[8,4096]{1,0:T(8,128)(2,1)S(1)} %pad_maximum_fusion.refs_0_, bf16[8,4096]{1,0:T(8,128)(2,1)S(1)} %collective-permute-done.18.refs_1_, ...), custom_call_target="tpu_custom_call" | custom-call | flops 10000000000 | tf_op jit(solution)/shard_map/experts/pallas_call | solution.py:42
  64.5 2.2 %collective-permute-start.21 = (bf16[8,4096]{1,0:T(8,128)(2,1)S(1)}, bf16[8,4096]{1,0:T(8,128)(2,1)S(1)}, u32[]{:S(2)}, u32[]{:S(2)}) collective-permute-start(bf16[8,4096]{1,0:T(8,128)(2,1)S(1)} %get-tuple-element.116), channel_id=1, source_target_pairs={{0,3},{1,2},{2,1},{3,0},{4,7},{5,6},{6,5},{7,4},{8,11},{9,10},{10,... | collective-permute-start | bytes 196616 | tf_op jit(solution)/shard_map/ppermute | solution.py:64
  68.0 2.1 %collective-permute-done.21 = bf16[8,4096]{1,0:T(8,128)(2,1)S(1)} collective-permute-done((bf16[8,4096]{1,0:T(8,128)(2,1)S(1)}, bf16[8,4096]{1,0:T(8,128)(2,1)S(1)}, u32[]{:S(2)}, u32[]{:S(2)}) %collective-permute-start.21) | collective-permute-done | bytes 65568 | tf_op jit(solution)/shard_map/ppermute | solution.py:64
  72.2 4.5 %collective-permute-done.24 = bf16[8,4096]{1,0:T(8,128)(2,1)S(1)} collective-permute-done((bf16[8,4096]{1,0:T(8,128)(2,1)S(1)}, bf16[8,4096]{1,0:T(8,128)(2,1)S(1)}, u32[]{:S(2)}, u32[]{:S(2)}) %collective-permute-start.24) | collective-permute-done | bytes 65568 | tf_op jit(solution)/shard_map/ppermute | solution.py:64
  78.5 2.0 %collective-permute-start.28 = (bf16[8,4096]{1,0:T(8,128)(2,1)S(1)}, bf16[8,4096]{1,0:T(8,128)(2,1)S(1)}, u32[]{:S(2)}, u32[]{:S(2)}) collective-permute-start(bf16[8,4096]{1,0:T(8,128)(2,1)S(1)} %get-tuple-element.122.refs_0_), channel_id=1, source_target_pairs={{0,3},{1,2},{2,1},{3,0},{4,7},{5,6},{6,5},{7,4},{8,11},{9,10},{10,... | collective-permute-start | bytes 196616 | tf_op jit(solution)/shard_map/ppermute | solution.py:64
  93.7 2.4 %collective-permute-done.34.refs_1_ = bf16[32,288]{1,0:T(8,128)(2,1)S(1)} collective-permute-done((bf16[32,288]{1,0:T(8,128)(2,1)S(1)}, bf16[32,288]{1,0:T(8,128)(2,1)S(1)}, u32[]{:S(2)}, u32[]{:S(2)}) %collective-permute-start.34) | collective-permute-done | bytes 18464 | tf_op jit(solution)/shard_map/ppermute | solution.py:73
  101.3 2.3 %collective-permute-done.35 = bf16[8,4096]{1,0:T(8,128)(2,1)S(1)} collective-permute-done((bf16[8,4096]{1,0:T(8,128)(2,1)S(1)}, bf16[8,4096]{1,0:T(8,128)(2,1)S(1)}, u32[]{:S(2)}, u32[]{:S(2)}) %collective-permute-start.35) | collective-permute-done | bytes 65568 | tf_op jit(solution)/shard_map/ppermute | solution.py:64
  105.5 4.4 %collective-permute-done.38.far = bf16[8,4096]{1,0:T(8,128)(2,1)S(1)} collective-permute-done((bf16[8,4096]{1,0:T(8,128)(2,1)S(1)}, bf16[8,4096]{1,0:T(8,128)(2,1)S(1)}, u32[]{:S(2)}, u32[]{:S(2)}) %collective-permute-start.38) | collective-permute-done | bytes 65568 | tf_op jit(solution)/shard_map/ppermute | solution.py:64
  111.4 2.1 %collective-permute-start.42 = (bf16[8,4096]{1,0:T(8,128)(2,1)S(1)}, bf16[8,4096]{1,0:T(8,128)(2,1)S(1)}, u32[]{:S(2)}, u32[]{:S(2)}) collective-permute-start(bf16[8,4096]{1,0:T(8,128)(2,1)S(1)} %pad_maximum_fusion.1.refs_0_), channel_id=1, source_target_pairs={{0,3},{1,2},{2,1},{3,0},{4,7},{5,6},{6,5},{7,4},{8,11},{9,10},{10,... | collective-permute-start | bytes 196616 | tf_op jit(solution)/shard_map/ppermute | solution.py:64
  115.0 2.1 %collective-permute-done.42.refs_3_ = bf16[8,4096]{1,0:T(8,128)(2,1)S(1)} collective-permute-done((bf16[8,4096]{1,0:T(8,128)(2,1)S(1)}, bf16[8,4096]{1,0:T(8,128)(2,1)S(1)}, u32[]{:S(2)}, u32[]{:S(2)}) %collective-permute-start.42) | collective-permute-done | bytes 65568 | tf_op jit(solution)/shard_map/ppermute | solution.py:64
  118.2 4.8 %experts.3 = (bf16[8,4096]{1,0:T(8,128)(2,1)S(1)}, bf16[8,4096]{1,0:T(8,128)(2,1)S(1)}, bf16[8,4096]{1,0:T(8,128)(2,1)S(1)}, bf16[8,4096]{1,0:T(8,128)(2,1)S(1)}) custom-call(bf16[8,4096]{1,0:T(8,128)(2,1)S(1)} %pad_maximum_fusion.1.refs_0_, bf16[8,4096]{1,0:T(8,128)(2,1)S(1)} %collective-permute-done.40.refs_1_, ...), custom_call_target="tpu_custom_call" | custom-call | flops 10000000000 | tf_op jit(solution)/shard_map/experts/pallas_call | solution.py:42
  123.1 1.9 %collective-permute-start.43 = (bf16[8,4096]{1,0:T(8,128)(2,1)S(1)}, bf16[8,4096]{1,0:T(8,128)(2,1)S(1)}, u32[]{:S(2)}, u32[]{:S(2)}) collective-permute-start(bf16[8,4096]{1,0:T(8,128)(2,1)S(1)} %get-tuple-element.141), channel_id=1, source_target_pairs={{0,3},{1,2},{2,1},{3,0},{4,7},{5,6},{6,5},{7,4},{8,11},{9,10},{10,... | collective-permute-start | bytes 196616 | tf_op jit(solution)/shard_map/ppermute | solution.py:64
  126.6 2.0 %collective-permute-done.43 = bf16[8,4096]{1,0:T(8,128)(2,1)S(1)} collective-permute-done((bf16[8,4096]{1,0:T(8,128)(2,1)S(1)}, bf16[8,4096]{1,0:T(8,128)(2,1)S(1)}, u32[]{:S(2)}, u32[]{:S(2)}) %collective-permute-start.43) | collective-permute-done | bytes 65568 | tf_op jit(solution)/shard_map/ppermute | solution.py:64
  130.9 4.2 %collective-permute-done.46 = bf16[8,4096]{1,0:T(8,128)(2,1)S(1)} collective-permute-done((bf16[8,4096]{1,0:T(8,128)(2,1)S(1)}, bf16[8,4096]{1,0:T(8,128)(2,1)S(1)}, u32[]{:S(2)}, u32[]{:S(2)}) %collective-permute-start.46) | collective-permute-done | bytes 65568 | tf_op jit(solution)/shard_map/ppermute | solution.py:64
  (177 shorter events, 66.0 us)
Async XLA Ops:
  5.0 4.4 %collective-permute-start.6 = (f32[2,3,512]{2,1,0:T(4,128)S(1)}, f32[2,3,512]{2,1,0:T(4,128)S(1)}, u32[]{:S(2)}, u32[]{:S(2)}) collective-permute-start(f32[2,3,512]{2,1,0:T(4,128)S(1)} %copy.30), channel_id=1, source_target_pairs={{0,8},{8,0},{1,9},{9,1},{2,10},{10,2},{3,11},{11,3},{4,12},{12,4},... | collective-permute-start | bytes 36872 | tf_op jit(solution)/shard_map/ppermute | solution.py:68
  5.5 7.8 %collective-permute-start = (bf16[2,4,4096]{2,1,0:T(4,128)(2,1)S(1)}, bf16[2,4,4096]{2,1,0:T(4,128)(2,1)S(1)}, u32[]{:S(2)}, u32[]{:S(2)}) collective-permute-start(bf16[2,4,4096]{2,1,0:T(4,128)(2,1)S(1)} %copy-done.18), channel_id=1, source_target_pairs={{0,4},{1,5},{2,6},{3,7},{4,0},{5,1},{6,2},{7,3},{8,12},{9,13},{10,... | collective-permute-start | bytes 196616 | tf_op jit(solution)/shard_map/ppermute | solution.py:64
  9.1 8.1 %collective-permute-start.5 = (f32[2,16,512]{2,1,0:T(8,128)S(1)}, f32[2,16,512]{2,1,0:T(8,128)S(1)}, u32[]{:S(2)}, u32[]{:S(2)}) collective-permute-start(f32[2,16,512]{2,1,0:T(8,128)S(1)} %copy-done.14), channel_id=1, source_target_pairs={{0,8},{8,0},{1,9},{9,1},{2,10},{10,2},{3,11},{11,3},{4,12},{12,4},... | collective-permute-start | bytes 196616 | tf_op jit(solution)/shard_map/ppermute | solution.py:68
  13.4 5.5 %collective-permute-start.3 = (bf16[8,4096]{1,0:T(8,128)(2,1)S(1)}, bf16[8,4096]{1,0:T(8,128)(2,1)S(1)}, u32[]{:S(2)}, u32[]{:S(2)}) collective-permute-start(bf16[8,4096]{1,0:T(8,128)(2,1)S(1)} %get-tuple-element.88.refs_0_), channel_id=1, source_target_pairs={{0,3},{1,2},{2,1},{3,0},{4,7},{5,6},{6,5},{7,4},{8,11},{9,10},{10,... | collective-permute-start | bytes 196616 | tf_op jit(solution)/shard_map/ppermute | solution.py:64
  15.2 4.5 %collective-permute-start.2 = (bf16[8,4096]{1,0:T(8,128)(2,1)S(1)}, bf16[8,4096]{1,0:T(8,128)(2,1)S(1)}, u32[]{:S(2)}, u32[]{:S(2)}) collective-permute-start(bf16[8,4096]{1,0:T(8,128)(2,1)S(1)} %get-tuple-element.88.refs_0_), channel_id=1, source_target_pairs={{0,2},{1,3},{2,0},{3,1},{4,6},{5,7},{6,4},{7,5},{8,10},{9,11},{10,... | collective-permute-start | bytes 196616 | tf_op jit(solution)/shard_map/ppermute | solution.py:64
  16.5 4.3 %collective-permute-start.1 = (bf16[8,4096]{1,0:T(8,128)(2,1)S(1)}, bf16[8,4096]{1,0:T(8,128)(2,1)S(1)}, u32[]{:S(2)}, u32[]{:S(2)}) collective-permute-start(bf16[8,4096]{1,0:T(8,128)(2,1)S(1)} %get-tuple-element.88.refs_0_), channel_id=1, source_target_pairs={{0,1},{1,0},{2,3},{3,2},{4,5},{5,4},{6,7},{7,6},{8,9},{9,8},{10,11... | collective-permute-start | bytes 196616 | tf_op jit(solution)/shard_map/ppermute | solution.py:64
  29.2 6.5 %collective-permute-start.12 = (bf16[32,290]{1,0:T(8,128)(2,1)S(1)}, bf16[32,290]{1,0:T(8,128)(2,1)S(1)}, u32[]{:S(2)}, u32[]{:S(2)}) collective-permute-start(bf16[32,290]{1,0:T(8,128)(2,1)S(1)} %pad_maximum_fusion.2), channel_id=1, source_target_pairs={{0,12},{1,13},{2,14},{3,15},{4,8},{5,9},{6,10},{7,11},{12,0},{13,1... | collective-permute-start | bytes 55688 | tf_op jit(solution)/shard_map/ppermute | solution.py:73
  31.3 4.3 %collective-permute-start.11 = (bf16[32,290]{1,0:T(8,128)(2,1)S(1)}, bf16[32,290]{1,0:T(8,128)(2,1)S(1)}, u32[]{:S(2)}, u32[]{:S(2)}) collective-permute-start(bf16[32,290]{1,0:T(8,128)(2,1)S(1)} %pad_maximum_fusion.2), channel_id=1, source_target_pairs={{0,8},{1,9},{2,10},{3,11},{4,12},{5,13},{6,14},{7,15},{8,0},{9,1},... | collective-permute-start | bytes 55688 | tf_op jit(solution)/shard_map/ppermute | solution.py:73
  38.5 5.4 %collective-permute-start.13 = (bf16[8,4096]{1,0:T(8,128)(2,1)S(1)}, bf16[8,4096]{1,0:T(8,128)(2,1)S(1)}, u32[]{:S(2)}, u32[]{:S(2)}) collective-permute-start(bf16[8,4096]{1,0:T(8,128)(2,1)S(1)} %get-tuple-element.104), channel_id=1, source_target_pairs={{0,3},{1,2},{2,1},{3,0},{4,7},{5,6},{6,5},{7,4},{8,11},{9,10},{10,... | collective-permute-start | bytes 196616 | tf_op jit(solution)/shard_map/ppermute | solution.py:64
  41.4 4.3 %collective-permute-start.14 = (bf16[8,4096]{1,0:T(8,128)(2,1)S(1)}, bf16[8,4096]{1,0:T(8,128)(2,1)S(1)}, u32[]{:S(2)}, u32[]{:S(2)}) collective-permute-start(bf16[8,4096]{1,0:T(8,128)(2,1)S(1)} %get-tuple-element.106), channel_id=1, source_target_pairs={{0,2},{1,3},{2,0},{3,1},{4,6},{5,7},{6,4},{7,5},{8,10},{9,11},{10,... | collective-permute-start | bytes 196616 | tf_op jit(solution)/shard_map/ppermute | solution.py:64
  45.7 5.5 %collective-permute-start.16 = (bf16[8,4096]{1,0:T(8,128)(2,1)S(1)}, bf16[8,4096]{1,0:T(8,128)(2,1)S(1)}, u32[]{:S(2)}, u32[]{:S(2)}) collective-permute-start(bf16[8,4096]{1,0:T(8,128)(2,1)S(1)} %add_convert_fusion.5.near), channel_id=1, source_target_pairs={{0,4},{1,5},{2,6},{3,7},{4,0},{5,1},{6,2},{7,3},{8,12},{9,13},{10,... | collective-permute-start | bytes 196616 | tf_op jit(solution)/shard_map/ppermute | solution.py:64
  52.9 5.4 %collective-permute-start.20 = (bf16[8,4096]{1,0:T(8,128)(2,1)S(1)}, bf16[8,4096]{1,0:T(8,128)(2,1)S(1)}, u32[]{:S(2)}, u32[]{:S(2)}) collective-permute-start(bf16[8,4096]{1,0:T(8,128)(2,1)S(1)} %pad_maximum_fusion.refs_0_), channel_id=1, source_target_pairs={{0,3},{1,2},{2,1},{3,0},{4,7},{5,6},{6,5},{7,4},{8,11},{9,10},{10,... | collective-permute-start | bytes 196616 | tf_op jit(solution)/shard_map/ppermute | solution.py:64
  64.5 5.6 %collective-permute-start.21 = (bf16[8,4096]{1,0:T(8,128)(2,1)S(1)}, bf16[8,4096]{1,0:T(8,128)(2,1)S(1)}, u32[]{:S(2)}, u32[]{:S(2)}) collective-permute-start(bf16[8,4096]{1,0:T(8,128)(2,1)S(1)} %get-tuple-element.116), channel_id=1, source_target_pairs={{0,3},{1,2},{2,1},{3,0},{4,7},{5,6},{6,5},{7,4},{8,11},{9,10},{10,... | collective-permute-start | bytes 196616 | tf_op jit(solution)/shard_map/ppermute | solution.py:64
  67.1 4.3 %collective-permute-start.23 = (bf16[8,4096]{1,0:T(8,128)(2,1)S(1)}, bf16[8,4096]{1,0:T(8,128)(2,1)S(1)}, u32[]{:S(2)}, u32[]{:S(2)}) collective-permute-start(bf16[8,4096]{1,0:T(8,128)(2,1)S(1)} %get-tuple-element.118), channel_id=1, source_target_pairs={{0,1},{1,0},{2,3},{3,2},{4,5},{5,4},{6,7},{7,6},{8,9},{9,8},{10,11... | collective-permute-start | bytes 196616 | tf_op jit(solution)/shard_map/ppermute | solution.py:64
  71.4 5.2 %collective-permute-start.24 = (bf16[8,4096]{1,0:T(8,128)(2,1)S(1)}, bf16[8,4096]{1,0:T(8,128)(2,1)S(1)}, u32[]{:S(2)}, u32[]{:S(2)}) collective-permute-start(bf16[8,4096]{1,0:T(8,128)(2,1)S(1)} %add_convert_fusion.4), channel_id=1, source_target_pairs={{0,4},{1,5},{2,6},{3,7},{4,0},{5,1},{6,2},{7,3},{8,12},{9,13},{10,... | collective-permute-start | bytes 196616 | tf_op jit(solution)/shard_map/ppermute | solution.py:64
  78.5 5.4 %collective-permute-start.28 = (bf16[8,4096]{1,0:T(8,128)(2,1)S(1)}, bf16[8,4096]{1,0:T(8,128)(2,1)S(1)}, u32[]{:S(2)}, u32[]{:S(2)}) collective-permute-start(bf16[8,4096]{1,0:T(8,128)(2,1)S(1)} %get-tuple-element.122.refs_0_), channel_id=1, source_target_pairs={{0,3},{1,2},{2,1},{3,0},{4,7},{5,6},{6,5},{7,4},{8,11},{9,10},{10,... | collective-permute-start | bytes 196616 | tf_op jit(solution)/shard_map/ppermute | solution.py:64
  86.2 4.3 %collective-permute-start.29 = (bf16[32,288]{1,0:T(8,128)(2,1)S(1)}, bf16[32,288]{1,0:T(8,128)(2,1)S(1)}, u32[]{:S(2)}, u32[]{:S(2)}) collective-permute-start(bf16[32,288]{1,0:T(8,128)(2,1)S(1)} %get-tuple-element.124), channel_id=1, source_target_pairs={{0,11},{1,10},{2,9},{3,8},{4,15},{5,14},{6,13},{7,12},{11,0},{10,1... | collective-permute-start | bytes 55304 | tf_op jit(solution)/shard_map/ppermute | solution.py:73
  97.8 5.8 %collective-permute-start.35 = (bf16[8,4096]{1,0:T(8,128)(2,1)S(1)}, bf16[8,4096]{1,0:T(8,128)(2,1)S(1)}, u32[]{:S(2)}, u32[]{:S(2)}) collective-permute-start(bf16[8,4096]{1,0:T(8,128)(2,1)S(1)} %get-tuple-element.133), channel_id=1, source_target_pairs={{0,3},{1,2},{2,1},{3,0},{4,7},{5,6},{6,5},{7,4},{8,11},{9,10},{10,... | collective-permute-start | bytes 196616 | tf_op jit(solution)/shard_map/ppermute | solution.py:64
  99.7 4.3 %collective-permute-start.36 = (bf16[8,4096]{1,0:T(8,128)(2,1)S(1)}, bf16[8,4096]{1,0:T(8,128)(2,1)S(1)}, u32[]{:S(2)}, u32[]{:S(2)}) collective-permute-start(bf16[8,4096]{1,0:T(8,128)(2,1)S(1)} %get-tuple-element.134), channel_id=1, source_target_pairs={{0,2},{1,3},{2,0},{3,1},{4,6},{5,7},{6,4},{7,5},{8,10},{9,11},{10,... | collective-permute-start | bytes 196616 | tf_op jit(solution)/shard_map/ppermute | solution.py:64
  104.6 5.2 %collective-permute-start.38 = (bf16[8,4096]{1,0:T(8,128)(2,1)S(1)}, bf16[8,4096]{1,0:T(8,128)(2,1)S(1)}, u32[]{:S(2)}, u32[]{:S(2)}) collective-permute-start(bf16[8,4096]{1,0:T(8,128)(2,1)S(1)} %add_convert_fusion.2.near), channel_id=1, source_target_pairs={{0,4},{1,5},{2,6},{3,7},{4,0},{5,1},{6,2},{7,3},{8,12},{9,13},{10,... | collective-permute-start | bytes 196616 | tf_op jit(solution)/shard_map/ppermute | solution.py:64
  111.4 5.6 %collective-permute-start.42 = (bf16[8,4096]{1,0:T(8,128)(2,1)S(1)}, bf16[8,4096]{1,0:T(8,128)(2,1)S(1)}, u32[]{:S(2)}, u32[]{:S(2)}) collective-permute-start(bf16[8,4096]{1,0:T(8,128)(2,1)S(1)} %pad_maximum_fusion.1.refs_0_), channel_id=1, source_target_pairs={{0,3},{1,2},{2,1},{3,0},{4,7},{5,6},{6,5},{7,4},{8,11},{9,10},{10,... | collective-permute-start | bytes 196616 | tf_op jit(solution)/shard_map/ppermute | solution.py:64
  123.1 5.5 %collective-permute-start.43 = (bf16[8,4096]{1,0:T(8,128)(2,1)S(1)}, bf16[8,4096]{1,0:T(8,128)(2,1)S(1)}, u32[]{:S(2)}, u32[]{:S(2)}) collective-permute-start(bf16[8,4096]{1,0:T(8,128)(2,1)S(1)} %get-tuple-element.141), channel_id=1, source_target_pairs={{0,3},{1,2},{2,1},{3,0},{4,7},{5,6},{6,5},{7,4},{8,11},{9,10},{10,... | collective-permute-start | bytes 196616 | tf_op jit(solution)/shard_map/ppermute | solution.py:64
  125.0 4.3 %collective-permute-start.44 = (bf16[8,4096]{1,0:T(8,128)(2,1)S(1)}, bf16[8,4096]{1,0:T(8,128)(2,1)S(1)}, u32[]{:S(2)}, u32[]{:S(2)}) collective-permute-start(bf16[8,4096]{1,0:T(8,128)(2,1)S(1)} %get-tuple-element.142), channel_id=1, source_target_pairs={{0,2},{1,3},{2,0},{3,1},{4,6},{5,7},{6,4},{7,5},{8,10},{9,11},{10,... | collective-permute-start | bytes 196616 | tf_op jit(solution)/shard_map/ppermute | solution.py:64
  129.9 5.2 %collective-permute-start.46 = (bf16[8,4096]{1,0:T(8,128)(2,1)S(1)}, bf16[8,4096]{1,0:T(8,128)(2,1)S(1)}, u32[]{:S(2)}, u32[]{:S(2)}) collective-permute-start(bf16[8,4096]{1,0:T(8,128)(2,1)S(1)} %add_convert_fusion.1), channel_id=1, source_target_pairs={{0,4},{1,5},{2,6},{3,7},{4,0},{5,1},{6,2},{7,3},{8,12},{9,13},{10,... | collective-permute-start | bytes 196616 | tf_op jit(solution)/shard_map/ppermute | solution.py:64
  (51 other events, 252.3 us)
